TPU v7x, 256 devices: a whole 4x4x8 slice. The times are simulated.
256 devices in a mesh: rep: 8 (over y, core), shard: 32 (over z, x).
Axes of the slice: x: 4, y: 4, z: 8, core: 2. Of those that a mesh axis runs over, the one named last changes fastest.
Arguments:
- gu_slow: float32 [2, 256, 29568], P(None, 'shard'), may hold values from -6 to 6
- gu_fast: bfloat16 [8, 2, 256, 29568], P('rep', None, 'shard'), may hold values from -6 to 6
- gu_error: bfloat16 [8, 2, 256, 29568], P('rep', None, 'shard'), may hold values from -6 to 6
- gu_moment: float32 [2, 256, 29568], P(None, 'shard'), may hold values from -6 to 6
- gu_basis: bfloat16 [29568, 128], P('shard'), may hold values from -0.03125 to 0.03125
- dn_slow: float32 [256, 8192], P('shard'), may hold values from -6 to 6
- dn_fast: bfloat16 [8, 256, 8192], P('rep', 'shard'), may hold values from -6 to 6
- dn_error: bfloat16 [8, 256, 8192], P('rep', 'shard'), may hold values from -6 to 6
- dn_moment: float32 [256, 8192], P('shard'), may hold values from -6 to 6
- dn_basis: bfloat16 [8192, 64], P('shard'), may hold values from -0.0625 to 0.0625
Outputs:
- gu_slow_next: float32 [2, 256, 29568], P(None, 'shard')
- gu_error_next: bfloat16 [8, 2, 256, 29568], P('rep', None, 'shard')
- gu_moment_next: float32 [2, 256, 29568], P(None, 'shard')
- gu_basis_next: bfloat16 [29568, 128], P('shard')
- dn_slow_next: float32 [256, 8192], P('shard')
- dn_error_next: bfloat16 [8, 256, 8192], P('rep', 'shard')
- dn_moment_next: float32 [256, 8192], P('shard')
- dn_basis_next: bfloat16 [8192, 64], P('shard')
All inputs are finite; a program needn't handle non-finite values.
Results may differ from a plain program's by a relative error of at most 0.014.
Values may be sent and summed in bfloat16 or wider, within the bound.
No kernel may reach another device: no remote copies, remote signals or barrier semaphores. Data moves between devices by JAX's collectives and lax.ppermute only.
A program may use at most 128 MiB of HBM per device.

v0:
```python
import jax
import jax.numpy as jnp
from jax import lax
from jax.sharding import PartitionSpec as P


def orthonormal(p_mean, gram_matrix):
    lower = jnp.linalg.cholesky(gram_matrix)
    return lax.linalg.triangular_solve(lower, p_mean, left_side=False, lower=True, transpose_a=True)


def shared_basis(p_rows, replica_count):
    p_mean = lax.psum(p_rows, "rep") / replica_count
    gram_local = jnp.einsum("brk,brl->bkl", p_mean, p_mean, precision=lax.Precision.HIGHEST)
    gram_matrix = lax.psum(gram_local, "shard")
    own_basis = orthonormal(p_mean, gram_matrix).astype(jnp.bfloat16)
    every_basis = lax.all_gather(own_basis, "shard", axis=1, tiled=True)
    return (own_basis, every_basis)


def outer_group(slow, fast, error, moment, basis):
    matrices, local_rows, columns_total = slow.shape
    replica_count = lax.axis_size("rep")
    rank_size = basis.shape[1] // matrices
    combined = slow - fast[0].astype(jnp.float32) + error[0].astype(jnp.float32)
    lowered = combined.astype(jnp.bfloat16)
    local_factor = basis.reshape(basis.shape[0], matrices, rank_size)
    column_block = lax.all_to_all(lowered, "shard", split_axis=2, concat_axis=1, tiled=True)
    p_rows = jnp.transpose(
        lax.psum_scatter(
            jnp.einsum(
                "brn,nbk->rbk", column_block, local_factor, preferred_element_type=jnp.float32
            ),
            "shard",
            scatter_dimension=0,
            tiled=True,
        ),
        (1, 0, 2),
    )
    own_basis, every_basis = shared_basis(p_rows, replica_count)
    q_term = jnp.einsum(
        "brn,brk->nbk", column_block, every_basis, preferred_element_type=jnp.float32
    )
    q_low = (lax.psum(q_term, "rep") / replica_count).astype(jnp.bfloat16)
    recon_block = jnp.einsum(
        "brk,nbk->brn", every_basis, q_low, preferred_element_type=jnp.float32
    ).astype(jnp.bfloat16)
    recon = lax.all_to_all(recon_block, "shard", split_axis=1, concat_axis=2, tiled=True).astype(
        jnp.float32
    )
    error_next = (combined - recon).astype(jnp.bfloat16)
    moment_next = 0.9 * moment + recon
    slow_next = slow - 0.7 * (recon + 0.9 * moment_next)
    return (
        slow_next,
        error_next[None],
        moment_next,
        q_low.reshape(q_low.shape[0], matrices * rank_size),
    )


def on_device(
    gu_slow, gu_fast, gu_error, gu_moment, gu_basis, dn_slow, dn_fast, dn_error, dn_moment, dn_basis
):
    gate_slow, gate_error, gate_moment, gate_basis = outer_group(
        gu_slow, gu_fast, gu_error, gu_moment, gu_basis
    )
    down_slow, down_error, down_moment, down_basis = outer_group(
        dn_slow[None], dn_fast[:, None], dn_error[:, None], dn_moment[None], dn_basis
    )
    return (
        gate_slow,
        gate_error,
        gate_moment,
        gate_basis,
        down_slow[0],
        down_error[:, 0],
        down_moment[0],
        down_basis,
    )


def solution(mesh):
    return jax.shard_map(
        on_device,
        mesh=mesh,
        in_specs=(
            P(None, "shard", None),
            P("rep", None, "shard", None),
            P("rep", None, "shard", None),
            P(None, "shard", None),
            P("shard", None),
            P("shard", None),
            P("rep", "shard", None),
            P("rep", "shard", None),
            P("shard", None),
            P("shard", None),
        ),
        out_specs=(
            P(None, "shard", None),
            P("rep", None, "shard", None),
            P(None, "shard", None),
            P("shard", None),
            P("shard", None),
            P("rep", "shard", None),
            P("shard", None),
            P("shard", None),
        ),
        check_vma=False,
    )
```

profile of v0, /device:TPU:1, one launch (start us, length us, event | category | flops | bytes accessed | tf_op | source)
XLA Modules:
  0.0 787.2 jit_solution(18097229195772656909)
XLA Ops:
  7.2 7.9 %copy.124 = f32[1,8,8192]{1,0,2:T(1,128)} copy(bf16[1,8,8192]{2,1,0:T(8,128)(2,1)} %param.17) | data formatting | bytes 393216 | tf_op jit(solution)/shard_map/convert_element_type | solution.py:25
  15.1 2.7 copy.122
  17.8 6.1 copy.123
  23.9 8.4 %fusion.32 = bf16[8192,1,8]{2,1,0:T(2,128)(2,1)} fusion(f32[1,8,8192]{1,0,2:T(1,128)} %copy.124, f32[1,8,8192]{1,0,2:T(1,128)} %bitcast.123, f32[1,8,8192]{1,0,2:T(1,128)} %copy.123), kind=kLoop, calls=%fused_computation.68 | loop fusion | flops 196608 | bytes 917504
  32.8 45.2 %reduce.15 = bf16[8192,8]{1,0:T(8,128)(2,1)S(1)} reduce(bf16[8192,1,8]{2,1,0:T(2,128)(2,1)} %fusion.32, bf16[]{:T(256)} %broadcast.116), dimensions={1}, to_apply=%fusion.32.reduce_sub_computation | reduce | bytes 262146
  78.0 2.8 reshape.167
  80.9 11.9 %all-to-all-start.2 = ((bf16[32,2,1024]{2,1,0:T(2,128)(2,1)}), bf16[32,2,1024]{2,1,0:T(2,128)(2,1)S(1)}, u32[]{:S(2)}, u32[]{:S(2)}) async-start(bf16[32,2,1024]{2,1,0:T(2,128)(2,1)} %reshape.167), calls=%async_computation.2 | async-start | bytes 262144 | tf_op jit(solution)/shard_map/all_to_all | solution.py:28
  94.8 22.9 %copy.109 = bf16[2,8,29568]{1,0,2:T(2,128)(2,1)} copy(bf16[2,8,29568]{2,1,0:T(8,128)(2,1)S(1)} %fusion.4) | data formatting | bytes 1892352 | tf_op jit(solution)/shard_map/convert_element_type | solution.py:26
  117.7 19.0 %reshape.165 = bf16[32,2,7392]{2,1,0:T(2,128)(2,1)} reshape(bf16[29568,2,8]{2,1,0:T(2,128)(2,1)} %bitcast.121) | data formatting | bytes 1892352
  136.8 9.3 %all-to-all-start = ((bf16[32,2,7392]{2,1,0:T(2,128)(2,1)}), bf16[32,2,7392]{2,1,0:T(2,128)(2,1)S(1)}, u32[]{:S(2)}, u32[]{:S(2)}) async-start(bf16[32,2,7392]{2,1,0:T(2,128)(2,1)} %reshape.165), calls=%async_computation | async-start | bytes 1900544 | tf_op jit(solution)/shard_map/all_to_all | solution.py:28
  147.8 8.7 %reshape.168 = bf16[8192,1,8]{2,1,0:T(2,128)(2,1)} reshape(bf16[32,2,1024]{2,1,0:T(2,128)(2,1)S(1)} %all-to-all-done.2) | data formatting | bytes 262144
  156.5 7.8 copy.125
  165.2 4.7 all-to-all-done
  169.9 15.8 %reshape.166 = bf16[29568,2,8]{2,1,0:T(2,128)(2,1)} reshape(bf16[32,2,7392]{2,1,0:T(2,128)(2,1)S(1)} %all-to-all-done) | data formatting | bytes 1892352
  185.7 32.1 %copy.110 = bf16[2,8,32,924]{3,1,2,0:T(8,128)(2,1)S(1)} copy(bf16[2,8,32,924]{1,0,3,2:T(2,128)(2,1)} %bitcast.122) | data formatting | bytes 1892352 | tf_op jit(solution)/shard_map/all_to_all | solution.py:28
  219.2 140.7 %all-reduce.9.cloned.1.call-done = (f32[256,2,64]{2,1,0:T(2,128)}, f32[256,1,64]{2,1,0:T(1,128)}) async-done(((f32[256,2,64]{2,1,0:T(2,128)}, f32[256,1,64]{2,1,0:T(1,128)}), (f32[256,2,64]{2,1,0:T(2,128)}, f32[256,1,64]{2,1,0:T(1,128)})) %all-reduce.9.cloned.1.call-update) | async-done | bytes 196624
  361.3 25.3 %all-reduce.4 = (f32[2,8,64]{2,1,0:T(8,128)S(1)}, f32[1,8,64]{2,1,0:T(8,128)S(1)}) all-reduce(f32[2,8,64]{2,1,0:T(8,128)S(1)} %bitcast.137, f32[1,8,64]{2,1,0:T(8,128)S(1)} %bitcast.138), channel_id=1, replica_groups=mesh['rep'=8,'shard'=32] {'rep'}, use_global_device_ids=true, to_apply=%region_1.0 | all-reduce | flops 1536 | bytes 12288 | tf_op jit(solution)/shard_map/psum | solution.py:13
  387.1 112.8 %all-reduce.2 = (f32[2,64,64]{1,2,0:T(8,128)S(1)}, f32[1,64,64]{1,2,0:T(8,128)S(1)}) all-reduce(f32[2,64,64]{1,2,0:T(8,128)S(1)} %fusion.17, f32[1,64,64]{1,2,0:T(8,128)S(1)} %convolution_bitcast_fusion.3), channel_id=1, replica_groups=mesh['rep'=8,'shard'=32] {'shard'}, use_global_device_ids=true, to_apply=%region_2.0 | all-reduce | flops 12288 | bytes 98304 | tf_op jit(solution)/shard_map/psum | solution.py:15
  500.1 11.7 %custom-call.14 = f32[2,64,64]{2,1,0:T(8,128)S(1)} custom-call(f32[2,64,64]{2,1,0:T(8,128)S(1)} %fusion.11), custom_call_target="Cholesky" | custom-call | tf_op jit(solution)/shard_map/jit(cholesky)/cholesky | solution.py:8
  512.0 9.8 %custom-call.15 = f32[2,1,64,64]{2,3,1,0:T(8,128)S(1)} custom-call(f32[2,1,64,64]{3,2,1,0:T(8,128)S(1)} %select_bitcast_fusion), custom_call_target="InvertDiagBlocksLowerTriangular" | custom-call | tf_op jit(solution)/shard_map/triangular_solve | solution.py:9
  522.0 33.7 %all_gather.6 = bf16[2,256,64]{2,1,0:T(8,128)(2,1)S(1)} all-gather(bf16[2,8,64]{2,1,0:T(8,128)(2,1)S(1)} %convolution_convert_fusion.2), channel_id=1, replica_groups=mesh['rep'=8,'shard'=32] {'shard'}, dimensions={1}, use_global_device_ids=true | all-gather | bytes 67584 | tf_op jit(solution)/shard_map/all_gather | solution.py:17
  557.0 5.8 custom-call.16
  564.1 4.9 custom-call.17
  569.2 36.2 %all-gather = bf16[256,64]{1,0:T(8,128)(2,1)S(1)} all-gather(bf16[8,64]{1,0:T(8,128)(2,1)S(1)} %convolution_convert_fusion.3), channel_id=2, replica_groups=mesh['rep'=8,'shard'=32] {'shard'}, dimensions={0}, use_global_device_ids=true | all-gather | bytes 33792 | tf_op jit(solution)/shard_map/all_gather | solution.py:17
  606.3 114.5 %all-reduce.11.cloned.1.call-done = (f32[924,2,64]{0,2,1:T(8,128)}, f32[256,1,64]{0,2,1:T(8,128)}) async-done(((f32[924,2,64]{0,2,1:T(8,128)}, f32[256,1,64]{0,2,1:T(8,128)}), (f32[924,2,64]{0,2,1:T(8,128)}, f32[256,1,64]{0,2,1:T(8,128)})) %all-reduce.11.cloned.1.call-update) | async-done | bytes 538640 | tf_op jit(solution)/shard_map/psum | solution.py:44
  725.2 9.5 %all-to-all-start.3 = ((bf16[32,2,1024]{2,1,0:T(2,128)(2,1)}), bf16[32,2,1024]{2,1,0:T(2,128)(2,1)S(1)}, u32[]{:S(2)}, u32[]{:S(2)}) async-start(bf16[32,2,1024]{2,1,0:T(2,128)(2,1)} %reshape.169), calls=%async_computation.3 | async-start | bytes 262144 | tf_op jit(solution)/shard_map/all_to_all | solution.py:48
  738.4 5.8 all-to-all-done.3
  744.2 4.2 all-to-all-start.1
  748.5 2.3 copy.131
  750.8 9.8 %subtract_convert_fusion = bf16[1,8,8192]{1,0,2:T(2,128)(2,1)} fusion(f32[1,8,8192]{1,0,2:T(1,128)} %bitcast.125, f32[1,8,8192]{1,0,2:T(1,128)} %copy.124, f32[1,8,8192]{1,0,2:T(1,128)} %bitcast.124, f32[1,8,8192]{1,0,2:T(1,128)} %copy.123), kind=kLoop, calls=%fused_computation | loop fusion | flops 262144 | bytes 1179648 | tf_op jit(solution)/shard_map/convert_element_type | solution.py:51
  760.6 8.6 %copy.134 = bf16[1,8,8192]{2,1,0:T(8,128)(2,1)} copy(bf16[1,8,8192]{1,0,2:T(2,128)(2,1)} %subtract_convert_fusion) | data formatting | bytes 262144
  774.9 5.5 multiply_subtract_fusion
  (68 shorter events, 25.5 us)
Async XLA Ops:
  7.2 157.2 %copy-start = (bf16[256,64]{0,1:T(8,128)(2,1)S(1)}, bf16[256,64]{0,1:T(8,128)(2,1)}, u32[]{:S(2)}) copy-start(bf16[256,64]{0,1:T(8,128)(2,1)} %param.19) | copy-start | bytes 98308
  7.2 7.9 %copy-start.3 = (f32[8,8192]{1,0:T(8,128)S(1)}, f32[8,8192]{1,0:T(8,128)}, u32[]{:S(2)}) copy-start(f32[8,8192]{1,0:T(8,128)} %param.15) | copy-start | bytes 786436
  15.1 2.7 copy-start.6
  78.0 14.7 %copy-start.2 = (bf16[1,2,8,29568]{3,2,1,0:T(8,128)(2,1)S(1)}, bf16[1,2,8,29568]{3,2,1,0:T(8,128)(2,1)}, u32[]{:S(2)}) copy-start(bf16[1,2,8,29568]{3,2,1,0:T(8,128)(2,1)} %param.12) | copy-start | bytes 2838532
  80.9 55.9 %all-to-all-start.2 = ((bf16[32,2,1024]{2,1,0:T(2,128)(2,1)}), bf16[32,2,1024]{2,1,0:T(2,128)(2,1)S(1)}, u32[]{:S(2)}, u32[]{:S(2)}) async-start(bf16[32,2,1024]{2,1,0:T(2,128)(2,1)} %reshape.167), calls=%async_computation.2 | async-start | bytes 262144 | tf_op jit(solution)/shard_map/all_to_all | solution.py:28
  117.7 28.6 %copy-start.5 = (bf16[924,128]{1,0:T(8,128)(2,1)S(1)}, bf16[924,128]{1,0:T(8,128)(2,1)}, u32[]{:S(2)}) copy-start(bf16[924,128]{1,0:T(8,128)(2,1)} %param.14) | copy-start | bytes 709636
  136.8 9.8 %copy-start.8 = (u32[256]{0:T(256)S(1)}, u32[256]{0:T(256)}, u32[]{:S(2)}) copy-start(u32[256]{0:T(256)} %constant.109) | copy-start | bytes 3076
  136.8 33.2 %all-to-all-start = ((bf16[32,2,7392]{2,1,0:T(2,128)(2,1)}), bf16[32,2,7392]{2,1,0:T(2,128)(2,1)S(1)}, u32[]{:S(2)}, u32[]{:S(2)}) async-start(bf16[32,2,7392]{2,1,0:T(2,128)(2,1)} %reshape.165), calls=%async_computation | async-start | bytes 1900544 | tf_op jit(solution)/shard_map/all_to_all | solution.py:28
  146.1 213.8 %all-reduce.9.cloned.1.call-start = ((), (), s32[]{:S(2)}) async-start(), calls=%async_computation.4 | async-start | bytes 786432
  219.1 501.6 %all-reduce.11.cloned.1.call-start = ((), (), s32[]{:S(2)}) async-start(), calls=%async_computation.5 | async-start | bytes 1179648 | tf_op jit(solution)/shard_map/psum | solution.py:44
  722.7 14.8 %copy-start.7 = (bf16[256,64]{0,1:T(8,128)(2,1)}, bf16[256,64]{0,1:T(8,128)(2,1)S(1)}, u32[]{:S(2)}) copy-start(bf16[256,64]{0,1:T(8,128)(2,1)S(1)} %fusion.13) | copy-start | bytes 98308
  725.2 19.0 %all-to-all-start.3 = ((bf16[32,2,1024]{2,1,0:T(2,128)(2,1)}), bf16[32,2,1024]{2,1,0:T(2,128)(2,1)S(1)}, u32[]{:S(2)}, u32[]{:S(2)}) async-start(bf16[32,2,1024]{2,1,0:T(2,128)(2,1)} %reshape.169), calls=%async_computation.3 | async-start | bytes 262144 | tf_op jit(solution)/shard_map/all_to_all | solution.py:48
  744.2 26.8 %all-to-all-start.1 = ((bf16[2,256,924]{2,0,1:T(2,128)(2,1)}), bf16[2,256,924]{2,0,1:T(2,128)(2,1)S(1)}, u32[]{:S(2)}, u32[]{:S(2)}) async-start(bf16[2,256,924]{2,0,1:T(2,128)(2,1)} %copy.119), calls=%async_computation.1 | async-start | bytes 2097152 | tf_op jit(solution)/shard_map/all_to_all | solution.py:48
  760.6 8.6 %copy-start.4 = (f32[8,8192]{1,0:T(8,128)S(1)}, f32[8,8192]{1,0:T(8,128)}, u32[]{:S(2)}) copy-start(f32[8,8192]{1,0:T(8,128)} %param.18) | copy-start | bytes 786436
  774.9 5.5 copy-start.1
Sparse Core Ops, SparseCore 0:
  219.3 140.6 all-reduce.8
  606.4 114.3 all-reduce.10
where the time goes:
time: 796 us; the launch traced here: 787 us
  waiting for transfers between devices  267 us (34%)
  blocking collectives  208 us (26%)
  local copies, waits for them, and re-layouts  148 us (19%)
  other arithmetic  109 us (14%)
  starting transfers between devices  35.2 us (4%)
  between operations  15 us (2%)
    unnamed x3, waiting for transfers between devices  141 us
    psum x1, waiting for transfers between devices, outer_group(): q_low = (lax.psum(q_term, 'rep') / replica_count).astype(jnp.bfloat16)  114 us
    psum x1, blocking collectives, shared_basis(): gram_matrix = lax.psum(gram_local, 'shard')  113 us
    all_gather x2, blocking collectives, shared_basis(): every_basis = lax.all_gather(own_basis, 'shard', axis=1, tiled=True)  69.9 us
    unnamed x33, local copies, waits for them, and re-layouts  62 us
    unnamed x3, other arithmetic  55.1 us
    all_to_all x2, local copies, waits for them, and re-layouts, outer_group(): lax.all_to_all(lowered, 'shard', split_axis=2, concat_axis=1, tiled=True)  39.9 us
    psum x1, blocking collectives, shared_basis(): p_mean = lax.psum(p_rows, 'rep') / replica_count  25.3 us
  transfers between devices with their start and end apart: 6, of which 5 were waited for; matrix products, arithmetic and copies ran while one was open for 11% of the time, Pallas kernels for 0%

commit v1 on v0

v1 whole, which is shorter than its diff:
```python
import functools

import jax
import jax.numpy as jnp
from jax import lax
from jax.experimental import pallas as pl
from jax.experimental.pallas import tpu as pltpu
from jax.sharding import Mesh
from jax.sharding import PartitionSpec as P

FF = 29568
D = 8192
SHARDS = 32
REPS = 8
GU_COLS = FF // SHARDS
DN_COLS = D // SHARDS
GU_SUB = 116
DN_SUB = DN_COLS // REPS
LANES = 128
FF_PAD = FF + LANES
D_PAD = D + LANES
RANK = 64
F32 = jnp.float32
BF16 = jnp.bfloat16
SHARD = ("z", "x")
VMEM = pl.BlockSpec(memory_space=pltpu.VMEM)
SMEM = pl.BlockSpec(memory_space=pltpu.SMEM)
ANY = pl.BlockSpec(memory_space=pl.ANY)
GROUPS = 4


def params(mib):
    return pltpu.CompilerParams(vmem_limit_bytes=mib * 2**20)


def up_to(value, unit):
    return -(-value // unit) * unit


def piece_bounds():
    per = SHARDS // GROUPS
    gu, dn = [0], [0]
    for g in range(GROUPS):
        gu.append(min(FF, up_to(GU_COLS * per * (g + 1) + 32, LANES)))
        dn.append(min(D, DN_COLS * per * (g + 1) + LANES))
    gu[-1], dn[-1] = FF, D
    return gu, dn


def lower_kernel(pos, gs, gf, ge, ds, df, de, own, oth, gsv, gfv, gev, dsv, dfv, dev, sems):
    y, core = pos[0], pos[1]
    gu_at, dn_at = piece_bounds()
    copies = []
    for g in range(GROUPS):
        a, n = gu_at[g], gu_at[g + 1] - gu_at[g]
        c, m = dn_at[g], dn_at[g + 1] - dn_at[g]
        row = []
        for i, (src, dst) in enumerate(((gs, gsv), (gf, gfv), (ge, gev))):
            at = (slice(None), slice(None), pl.ds(a, n))
            row.append(pltpu.make_async_copy(src.at[at], dst.at[at], sems.at[g, i]))
        for i, (src, dst) in enumerate(((ds, dsv), (df, dfv), (de, dev))):
            at = (slice(None), pl.ds(c, m))
            row.append(pltpu.make_async_copy(src.at[at], dst.at[at], sems.at[g, 3 + i]))
        for copy in row:
            copy.start()
        copies.append(row)
    for ref in (gsv, gfv, gev):
        ref[:, :, FF:] = jnp.zeros((2, 8, LANES), ref.dtype)
    for ref in (dsv, dfv, dev):
        ref[:, D:] = jnp.zeros((8, LANES), ref.dtype)
    first = core == 0
    per = SHARDS // GROUPS
    for shard in range(SHARDS):
        if shard % per == 0:
            for copy in copies[shard // per]:
                copy.wait()
        start = GU_COLS * shard
        base = start // LANES * LANES
        end = up_to(start + GU_SUB * 7 + LANES, LANES)
        at = (slice(None), slice(None), slice(base, end))
        gu = gsv[at] - gfv[at].astype(F32) + gev[at].astype(F32)
        dn_start = DN_COLS * shard
        at = (slice(None), slice(dn_start, dn_start + DN_COLS + LANES))
        dn = dsv[at] - dfv[at].astype(F32) + dev[at].astype(F32)
        for yy in range(4):
            slot = lax.rem(yy - y + 4, 4)
            parts = []
            for c in range(2):
                r = 2 * yy + c
                o = start - base + GU_SUB * r
                parts.append(
                    jnp.concatenate(
                        [
                            gu[0, :, o : o + LANES],
                            gu[1, :, o : o + LANES],
                            dn[:, DN_SUB * r : DN_SUB * r + LANES],
                        ],
                        axis=0,
                    )
                )
            own[slot, shard] = jnp.where(first, parts[0], parts[1]).astype(BF16)
            oth[slot, shard] = jnp.where(first, parts[1], parts[0]).astype(BF16)


def lower(pos, gs, gf, ge, ds, df, de):
    shape = jax.ShapeDtypeStruct((4, SHARDS, 24, LANES), BF16)
    return pl.pallas_call(
        lower_kernel,
        out_shape=(shape, shape),
        in_specs=[SMEM] + [ANY] * 6,
        out_specs=(VMEM, VMEM),
        scratch_shapes=[
            pltpu.VMEM((2, 8, FF_PAD), F32),
            pltpu.VMEM((2, 8, FF_PAD), BF16),
            pltpu.VMEM((2, 8, FF_PAD), BF16),
            pltpu.VMEM((8, D_PAD), F32),
            pltpu.VMEM((8, D_PAD), BF16),
            pltpu.VMEM((8, D_PAD), BF16),
            pltpu.SemaphoreType.DMA((GROUPS, 6)),
        ],
        compiler_params=params(32),
    )(pos, gs, gf, ge, ds, df, de)


def split_hi_lo(value):
    hi = value.astype(BF16).astype(F32)
    return jnp.concatenate([hi, value - hi], axis=-1).astype(BF16)


def p_part_kernel(lx, bz, out):
    acc_gu = jnp.zeros((96, LANES), F32)
    acc_dn = jnp.zeros((96, LANES), F32)
    for z in range(8):
        lhs = lx[:, z].astype(F32).reshape(96, LANES).astype(BF16)
        acc_gu = acc_gu + jnp.dot(lhs, bz[z, 0:128, :], preferred_element_type=F32)
        acc_dn = acc_dn + jnp.dot(lhs[:, 0:32], bz[z, 128:160, :], preferred_element_type=F32)
    acc_gu = acc_gu.reshape(4, 24, LANES)
    acc_dn = acc_dn.reshape(4, 24, LANES)
    part = jnp.concatenate(
        [acc_gu[:, 0:8, 0:RANK], acc_gu[:, 8:16, RANK:LANES], acc_dn[:, 16:24, 0:RANK]], axis=1
    )
    block = split_hi_lo(part)
    for rep in range(REPS):
        out[4 * rep : 4 * rep + 4] = block


def p_part(lx, bz):
    return pl.pallas_call(
        p_part_kernel,
        out_shape=jax.ShapeDtypeStruct((32, 24, LANES), BF16),
        in_specs=[VMEM, VMEM],
        out_specs=VMEM,
        compiler_params=params(16),
    )(lx, bz)


def p_sum_kernel(ps, lbar, out):
    total = jnp.sum(ps[...].astype(F32), axis=0)
    rows = split_hi_lo(total[:, 0:RANK] + total[:, RANK:LANES])
    out[:, 0:24, :] = lbar[...]
    out[:, 24:48, :] = jnp.broadcast_to(rows[None], (SHARDS, 24, LANES))


def p_sum(ps, lbar):
    return pl.pallas_call(
        p_sum_kernel,
        out_shape=jax.ShapeDtypeStruct((SHARDS, 48, LANES), BF16),
        in_specs=[VMEM, VMEM],
        out_specs=VMEM,
        compiler_params=params(16),
    )(ps, lbar)


def inverse_factors(grams):
    eye = (
        lax.broadcasted_iota(jnp.int32, (RANK, RANK), 0)
        == lax.broadcasted_iota(jnp.int32, (RANK, RANK), 1)
    ).astype(F32)
    blocks = []
    for gram in grams:
        work = jnp.concatenate([gram, eye], axis=1)
        blocks.append([work[8 * b : 8 * b + 8] for b in range(8)])
    sub = lax.broadcasted_iota(jnp.int32, (8, LANES), 0)
    rows = [[] for _ in grams]
    for k in range(RANK):
        b0, s = k // 8, k % 8
        for m, work in enumerate(blocks):
            row = jnp.broadcast_to(work[b0][s : s + 1], (8, LANES))
            cols = [jnp.broadcast_to(work[b][:, k : k + 1], (8, LANES)) for b in range(b0, 8)]
            pivot = jnp.broadcast_to(cols[0][s : s + 1], (8, LANES))
            rows[m].append((row * lax.rsqrt(pivot))[0:1])
            scaled = row / pivot
            for b in range(b0, 8):
                factor = cols[b - b0]
                if b == b0:
                    if s == 7:
                        continue
                    factor = jnp.where(sub > s, factor, 0.0)
                work[b] = work[b] - factor * scaled
    return [jnp.concatenate(r, axis=0)[:, RANK:LANES] for r in rows]


def exact_dot(a, b, dims):
    return lax.dot_general(
        a, b, (dims, ((), ())), precision=lax.Precision.HIGHEST, preferred_element_type=F32
    )


def factor_kernel(recv, a_out, q_out):
    block = recv[...].astype(F32)
    columns = [
        block[:, 8 * m : 8 * m + 8, :].reshape(256, LANES).astype(BF16) for m in range(3)
    ]
    left = block[:, 24:48, :]
    left = left[:, :, 0:RANK] + left[:, :, RANK:LANES]
    lefts = [left[:, 8 * m : 8 * m + 8, :].reshape(256, RANK) for m in range(3)]
    grams = [exact_dot(p, p, ((0,), (0,))) for p in lefts]
    inverses = inverse_factors(grams)
    qs, recons = [], []
    for p, inverse, column in zip(lefts, inverses, columns):
        h = exact_dot(p, inverse, ((1,), (1,))).astype(BF16)
        q = lax.dot_general(column, h, (((0,), (0,)), ((), ())), preferred_element_type=F32)
        q = (q * (1.0 / REPS)).astype(BF16)
        qs.append(q)
        recon = lax.dot_general(h, q, (((1,), (1,)), ((), ())), preferred_element_type=F32)
        recons.append(recon.reshape(SHARDS, 8, LANES))
    a_out[...] = jnp.concatenate(recons, axis=1).astype(BF16)
    q_out[0:128, :] = jnp.concatenate([qs[0].astype(F32), qs[1].astype(F32)], axis=1).astype(BF16)
    dn = qs[2].astype(F32)[0:DN_SUB]
    q_out[128:160, :] = jnp.concatenate([dn, jnp.zeros_like(dn)], axis=1).astype(BF16)


def factor(recv):
    return pl.pallas_call(
        factor_kernel,
        out_shape=(
            jax.ShapeDtypeStruct((SHARDS, 24, LANES), BF16),
            jax.ShapeDtypeStruct((160, LANES), BF16),
        ),
        in_specs=[VMEM],
        out_specs=(VMEM, VMEM),
        compiler_params=params(32),
    )(recv)


STEPS = 8
GU_TILE = 29 * LANES
DN_TILE = D // STEPS
PAYLOAD = SHARDS * 24 + 160


def finish_kernel(
    pos, b0, b1, b2, b3, b4, b5, b6, b7, gs, gf, ge, gm, ds, df, de, dm,
    gs_o, ge_o, gm_o, ds_o, de_o, dm_o, gb_o, db_o, stage, gu_full, dn_full, q_full, sems,
):
    step = pl.program_id(0)

    @pl.when(step == 0)
    def _():
        y, core = pos[0], pos[1]
        copies = []
        for i, ref in enumerate((b0, b1, b2, b3, b4, b5, b6, b7)):
            whose = lax.rem(y - i % 4 + 4, 4)
            side = core if i < 4 else 1 - core
            copies.append(
                pltpu.make_async_copy(ref, stage.at[2 * whose + side], sems.at[i])
            )
            copies[-1].start()
        for copy in copies:
            copy.wait()
        for shard in range(SHARDS):
            for r in range(REPS):
                block = stage[r, 24 * shard : 24 * shard + 24, :].astype(F32)
                at = GU_COLS * shard + GU_SUB * r
                gu_full[0, :, at : at + LANES] = block[0:8]
                gu_full[1, :, at : at + LANES] = block[8:16]
                at = DN_COLS * shard + DN_SUB * r
                dn_full[:, at : at + LANES] = block[16:24]
        for r in range(REPS):
            q_full[GU_SUB * r : GU_SUB * r + 128, :] = stage[r, 768:896, :].astype(F32)
        gb_o[...] = q_full[0:GU_COLS, :].astype(BF16)
        for r in range(REPS):
            db_o[DN_SUB * r : DN_SUB * r + DN_SUB, :] = stage[r, 896:928, :][:, 0:RANK]

    def outer(slow, fast, error, moment, recon):
        combined = slow - fast.astype(F32) + error.astype(F32)
        moment_next = 0.9 * moment + recon
        return (
            slow - 0.7 * (recon + 0.9 * moment_next),
            (combined - recon).astype(BF16),
            moment_next,
        )

    recon = gu_full[:, :, pl.ds(pl.multiple_of(step * GU_TILE, LANES), GU_TILE)]
    gs_o[...], e, gm_o[...] = outer(gs[...], gf[0], ge[0], gm[...], recon)
    ge_o[...] = e[None]
    recon = dn_full[:, pl.ds(pl.multiple_of(step * DN_TILE, LANES), DN_TILE)]
    ds_o[...], e, dm_o[...] = outer(ds[...], df[0], de[0], dm[...], recon)
    de_o[...] = e[None]


def finish(pos, blocks, gs, gf, ge, gm, ds, df, de, dm):
    gu = pl.BlockSpec((2, 8, GU_TILE), lambda i: (0, 0, i))
    gu1 = pl.BlockSpec((1, 2, 8, GU_TILE), lambda i: (0, 0, 0, i))
    dn = pl.BlockSpec((8, DN_TILE), lambda i: (0, i))
    dn1 = pl.BlockSpec((1, 8, DN_TILE), lambda i: (0, 0, i))

    def like(a):
        return jax.ShapeDtypeStruct(a.shape, a.dtype)

    return pl.pallas_call(
        finish_kernel,
        grid=(STEPS,),
        out_shape=(
            like(gs), like(ge), like(gm), like(ds), like(de), like(dm),
            jax.ShapeDtypeStruct((GU_COLS, LANES), BF16),
            jax.ShapeDtypeStruct((DN_COLS, RANK), BF16),
        ),
        in_specs=[SMEM] + [ANY] * 8 + [gu, gu1, gu1, gu, dn, dn1, dn1, dn],
        out_specs=(
            gu, gu1, gu, dn, dn1, dn,
            pl.BlockSpec((GU_COLS, LANES), lambda i: (0, 0)),
            pl.BlockSpec((DN_COLS, RANK), lambda i: (0, 0)),
        ),
        scratch_shapes=[
            pltpu.VMEM((REPS, PAYLOAD, LANES), BF16),
            pltpu.VMEM((2, 8, GU_TILE * STEPS), F32),
            pltpu.VMEM((8, D_PAD), F32),
            pltpu.VMEM((960, LANES), F32),
            pltpu.SemaphoreType.DMA((8,)),
        ],
        compiler_params=params(40),
    )(pos, *blocks, gs, gf, ge, gm, ds, df, de, dm)


def shift(value, axis, size, by):
    return lax.ppermute(value, axis, [(i, (i + by) % size) for i in range(size)])


def swap(value):
    return lax.ppermute(value, "core", [(0, 1), (1, 0)])


def exchange(value, axis):
    return lax.all_to_all(value, axis, 0, 0, tiled=False)


def on_device(
    gu_slow, gu_fast, gu_error, gu_moment, gu_basis, dn_slow, dn_fast, dn_error, dn_moment, dn_basis
):
    y, core = lax.axis_index("y"), lax.axis_index("core")
    rep = 2 * y + core
    pos = jnp.stack([y, core]).astype(jnp.int32)
    own, oth = lower(pos, gu_slow, gu_fast[0], gu_error[0], dn_slow, dn_fast[0], dn_error[0])
    came = swap(oth)
    pair = own.astype(F32) + came.astype(F32)
    sends = {by: pair[by].astype(BF16) for by in (2, 1, 3)}
    comes = {by: shift(sends[by], "y", 4, by) for by in (2, 1, 3)}

    gu_b = jnp.pad(gu_basis, ((0, 4), (0, 0)))
    gu_b = jnp.pad(lax.dynamic_slice(gu_b, (GU_SUB * rep, 0), (GU_SUB, LANES)), ((0, 12), (0, 0)))
    dn_b = lax.dynamic_slice(dn_basis, (DN_SUB * rep, 0), (DN_SUB, RANK))
    b_own = jnp.concatenate([gu_b, jnp.pad(dn_b, ((0, 0), (0, RANK)))], axis=0)
    b_z = exchange(jnp.broadcast_to(b_own[None], (8, 160, LANES)), "z")

    total = pair[0] + comes[1].astype(F32) + comes[2].astype(F32) + comes[3].astype(F32)
    lbar = total.astype(BF16)
    l_x = exchange(jnp.swapaxes(lbar.reshape(8, 4, 24, LANES), 0, 1), "x")
    parts = exchange(p_part(l_x, b_z), ("y", "core", "x"))
    recv = exchange(p_sum(parts, lbar), SHARD)
    a_blocks, q_block = factor(recv)
    a_rows = exchange(a_blocks, SHARD)
    payload = jnp.concatenate([a_rows.reshape(SHARDS * 24, LANES), q_block], axis=0)
    mine = {0: payload}
    for by in (2, 1, 3):
        mine[by] = shift(payload, "y", 4, by)
    blocks = [mine[by] for by in range(4)]
    blocks = blocks + [swap(b) for b in blocks]
    gs, ge, gm, ds, de, dm, gb, db = finish(
        pos, blocks, gu_slow, gu_fast, gu_error, gu_moment, dn_slow, dn_fast, dn_error, dn_moment
    )
    return gs, ge, gm, gb, ds, de, dm, db


def solution(mesh):
    fine = Mesh(mesh.devices.reshape(4, 2, 8, 4), ("y", "core", "z", "x"))
    rep = ("y", "core")
    weights, shared = P(None, SHARD, None), P(SHARD, None)
    replica = P(rep, None, SHARD, None)
    dn_replica = P(rep, SHARD, None)
    return jax.shard_map(
        on_device,
        mesh=fine,
        in_specs=(
            weights, replica, replica, weights, shared,
            shared, dn_replica, dn_replica, shared, shared,
        ),
        out_specs=(
            weights, replica, weights, shared,
            shared, dn_replica, shared, shared,
        ),
        check_vma=False,
    )
```

time: 796 us -> 153 us (0.19); the launches traced: 787 us -> 153 us
  waiting for transfers between devices: 267 us -> 9.59 us
  blocking collectives: 208 us -> 59.7 us
  local copies, waits for them, and re-layouts: 148 us -> 8.47 us
  other arithmetic: 109 us -> 1.55 us
  Pallas kernels: 0 us -> 42.4 us
  between operations: 15 us -> 0.85 us
    unnamed x3 -> x0, waiting for transfers between devices: 141 us -> none
    psum x2 -> x0, blocking collectives: 138 us -> none  [the longest x1 113 us: shared_basis(): gram_matrix = lax.psum(gram_local, 'shard')]
    psum x1 -> x0, waiting for transfers between devices: 114 us -> none  [outer_group(): q_low = (lax.psum(q_term, 'rep') / replica_count).astype(jnp.bfloat16)]
    all_gather x2 -> x0, blocking collectives: 69.9 us -> none  [shared_basis(): every_basis = lax.all_gather(own_basis, 'shard', axis=1, tiled=True)]
    all_to_all x0 -> x4, blocking collectives: none -> 59.7 us  [exchange(): return lax.all_to_all(value, axis, 0, 0, tiled=False)]
    unnamed x3 -> x0, other arithmetic: 55.1 us -> none
    unnamed x33 -> x34, local copies, waits for them, and re-layouts: 62 us -> 7.5 us
    convert_element_type x9 -> x1, local copies, waits for them, and re-layouts: 45.3 us -> 0.06 us  [on_device(): sends = {by: pair[by].astype(BF16) for by in (2, 1, 3)}]
  transfers between devices with their start and end apart: 6 -> 12, of which waited for: 5 -> 3; matrix products, arithmetic and copies ran while one was open for 11% -> 2% of each run, Pallas kernels for 0% -> 0%
where the time goes in v1:
time: 153 us
  blocking collectives  59.7 us (39%)
  Pallas kernels  42.4 us (28%)
  starting transfers between devices  30 us (20%)
  waiting for transfers between devices  9.59 us (6%)
  local copies, waits for them, and re-layouts  8.47 us (6%)
  other arithmetic  1.55 us (1%)
    all_to_all x4, blocking collectives, exchange(): return lax.all_to_all(value, axis, 0, 0, tiled=False)  59.7 us
    pallas_call x1, Pallas kernels, lower(): pl.pallas_call(lower_kernel, out_shape=(shape, shape), in_specs=[SMEM] +...  20.3 us
    ppermute x5, starting transfers between devices, swap(): return lax.ppermute(value, 'core', [(0, 1), (1, 0)])  16.9 us
    pallas_call x1, Pallas kernels, finish(): pl.pallas_call(finish_kernel, grid=(STEPS,), out_shape=(like(gs), like(ge...  11 us
    pallas_call x1, Pallas kernels, factor(): pl.pallas_call(factor_kernel, out_shape=(jax.ShapeDtypeStruct((SHARDS, 24...  10.5 us
    ppermute x6, waiting for transfers between devices, shift(): lax.ppermute(value, axis, [(i, (i + by) % size) for i in range(size)])  8.47 us
    unnamed x34, local copies, waits for them, and re-layouts  7.5 us
    ppermute x6, starting transfers between devices, shift(): lax.ppermute(value, axis, [(i, (i + by) % size) for i in range(size)])  6.66 us
  transfers between devices with their start and end apart: 12, of which 3 were waited for; matrix products, arithmetic and copies ran while one was open for 2% of the time, Pallas kernels for 0%

profile of v1, /device:TPU:1, one launch (start us, length us, event | category | flops | bytes accessed | tf_op | source)
XLA Modules:
  0.0 152.5 jit_solution(17276580444814064843)
XLA Ops:
  0.7 1.5 copy-done.1
  2.3 1.2 copy-done.3
  3.4 1.2 copy-done.5
  4.6 0.9 copy-done.8
  5.6 0.9 copy-done.10
  6.5 0.9 copy-done.12
  7.4 20.3 %shard_map.161 = (bf16[4,32,24,128]{3,2,1,0:T(8,128)(2,1)S(1)}, bf16[4,32,24,128]{3,2,1,0:T(8,128)(2,1)S(1)}) custom-call(s32[2]{0:T(128)S(1)} %pad_add_fusion.pos, f32[2,8,29568]{2,1,0:T(8,128)S(1)} %copy-done.1, bf16[2,8,29568]{2,1,0:T(8,128)(2,1)S(1)} %bitcast.27, bf16[2,8,29568]{2,1,0:T(8,128)(2,1)S(1)} %bitcast.28, f32[8,8192]{1,0:T(8,128)S(1)} %copy-done.8, ...), custom_call_target="tpu_custom_call" | custom-call | tf_op jit(solution)/shard_map/pallas_call | solution.py:107
  27.7 3.3 %collective-permute-start = (bf16[4,32,24,128]{3,2,1,0:T(8,128)(2,1)S(1)}, bf16[4,32,24,128]{3,2,1,0:T(8,128)(2,1)}, u32[]{:S(2)}, u32[]{:S(2)}) collective-permute-start(bf16[4,32,24,128]{3,2,1,0:T(8,128)(2,1)S(1)} %get-tuple-element.21), channel_id=1, source_target_pairs={{0,32},{32,0},{1,33},{33,1},{2,34},{34,2},{3,35},{35,3},{4,36},{36... | collective-permute-start | bytes 2359304 | tf_op jit(solution)/shard_map/ppermute | solution.py:341
  31.3 0.8 broadcast_in_dim.2
  32.0 6.5 %all-to-all-start.1 = ((bf16[8,160,128]{2,1,0:T(8,128)(2,1)}), bf16[8,160,128]{2,1,0:T(8,128)(2,1)S(1)}, u32[]{:S(2)}, u32[]{:S(2)}) async-start(bf16[8,160,128]{2,1,0:T(8,128)(2,1)} %broadcast_in_dim.2), calls=%async_computation.1 | async-start | bytes 655360 | tf_op jit(solution)/shard_map/all_to_all | solution.py:345
  38.5 1.3 fusion.7
  39.9 1.4 collective-permute-start.1
  41.3 1.5 %collective-permute-start.3 = (bf16[32,24,128]{2,1,0:T(8,128)(2,1)S(1)}, bf16[32,24,128]{2,1,0:T(8,128)(2,1)S(1)}, u32[]{:S(2)}, u32[]{:S(2)}) collective-permute-start(bf16[32,24,128]{2,1,0:T(8,128)(2,1)S(1)} %get-tuple-element.43), channel_id=1, source_target_pairs={{0,192},{64,0},{128,64},{192,128},{1,193},{65,1},{129,65},{193,129... | collective-permute-start | bytes 589832 | tf_op jit(solution)/shard_map/ppermute | solution.py:337
  42.8 1.6 %collective-permute-start.2 = (bf16[32,24,128]{2,1,0:T(8,128)(2,1)S(1)}, bf16[32,24,128]{2,1,0:T(8,128)(2,1)S(1)}, u32[]{:S(2)}, u32[]{:S(2)}) collective-permute-start(bf16[32,24,128]{2,1,0:T(8,128)(2,1)S(1)} %get-tuple-element.44), channel_id=1, source_target_pairs={{0,128},{64,192},{128,0},{192,64},{1,129},{65,193},{129,1},{193,65... | collective-permute-start | bytes 589832 | tf_op jit(solution)/shard_map/ppermute | solution.py:337
  44.4 3.1 %collective-permute-done.1 = bf16[32,24,128]{2,1,0:T(8,128)(2,1)S(1)} collective-permute-done((bf16[32,24,128]{2,1,0:T(8,128)(2,1)S(1)}, bf16[32,24,128]{2,1,0:T(8,128)(2,1)S(1)}, u32[]{:S(2)}, u32[]{:S(2)}) %collective-permute-start.1) | collective-permute-done | bytes 196640 | tf_op jit(solution)/shard_map/ppermute | solution.py:337
  47.5 5.3 %collective-permute-done.2 = bf16[32,24,128]{2,1,0:T(8,128)(2,1)S(1)} collective-permute-done((bf16[32,24,128]{2,1,0:T(8,128)(2,1)S(1)}, bf16[32,24,128]{2,1,0:T(8,128)(2,1)S(1)}, u32[]{:S(2)}, u32[]{:S(2)}) %collective-permute-start.2) | collective-permute-done | bytes 196640 | tf_op jit(solution)/shard_map/ppermute | solution.py:337
  53.0 9.1 %all_to_all.25.lx = bf16[4,8,24,128]{3,2,1,0:T(8,128)(2,1)S(1)} all-to-all(bf16[4,8,24,128]{3,2,1,0:T(8,128)(2,1)S(1)} %bitcast.32), channel_id=1, replica_groups=mesh['y'=4,'core'=2,'z'=8,'x'=4] {'x'}, dimensions={0} | all-to-all | bytes 393216 | tf_op jit(solution)/shard_map/all_to_all | solution.py:345
  62.1 0.4 shard_map.162
  62.6 14.8 %all_to_all.26.ps = bf16[32,24,128]{2,1,0:T(8,128)(2,1)S(1)} all-to-all(bf16[32,24,128]{2,1,0:T(8,128)(2,1)S(1)} %shard_map.162), channel_id=1, replica_groups=mesh['y'=4,'core'=2,'z'=8,'x'=4] {'y','core','x'}, dimensions={0} | all-to-all | bytes 393216 | tf_op jit(solution)/shard_map/all_to_all | solution.py:345
  77.4 0.2 shard_map.163
  77.6 21.2 %all_to_all.27.recv = bf16[32,48,128]{2,1,0:T(8,128)(2,1)S(1)} all-to-all(bf16[32,48,128]{2,1,0:T(8,128)(2,1)S(1)} %shard_map.163), channel_id=1, replica_groups=mesh['y'=4,'core'=2,'z'=8,'x'=4] {'z','x'}, dimensions={0} | all-to-all | bytes 786432 | tf_op jit(solution)/shard_map/all_to_all | solution.py:345
  98.8 10.5 %shard_map.164 = (bf16[32,24,128]{2,1,0:T(8,128)(2,1)S(1)}, bf16[160,128]{1,0:T(8,128)(2,1)S(1)}) custom-call(bf16[32,48,128]{2,1,0:T(8,128)(2,1)S(1)} %all_to_all.27.recv), custom_call_target="tpu_custom_call" | custom-call | tf_op jit(solution)/shard_map/pallas_call | solution.py:234
  109.3 14.6 %all_to_all.28 = bf16[32,24,128]{2,1,0:T(8,128)(2,1)S(1)} all-to-all(bf16[32,24,128]{2,1,0:T(8,128)(2,1)S(1)} %get-tuple-element.22), channel_id=1, replica_groups=mesh['y'=4,'core'=2,'z'=8,'x'=4] {'z','x'}, dimensions={0} | all-to-all | bytes 393216 | tf_op jit(solution)/shard_map/all_to_all | solution.py:345
  123.9 1.0 collective-permute-start.6
  124.9 1.2 collective-permute-start.5
  126.1 3.7 %collective-permute-start.7 = (bf16[928,128]{1,0:T(8,128)(2,1)S(1)}, bf16[928,128]{1,0:T(8,128)(2,1)S(1)}, u32[]{:S(2)}, u32[]{:S(2)}) collective-permute-start(bf16[928,128]{1,0:T(8,128)(2,1)S(1)} %pad_maximum_fusion.b0), channel_id=1, source_target_pairs={{0,32},{32,0},{1,33},{33,1},{2,34},{34,2},{3,35},{35,3},{4,36},{36... | collective-permute-start | bytes 712712 | tf_op jit(solution)/shard_map/ppermute | solution.py:341
  129.8 4.9 %collective-permute-start.10 = (bf16[928,128]{1,0:T(8,128)(2,1)S(1)}, bf16[928,128]{1,0:T(8,128)(2,1)S(1)}, u32[]{:S(2)}, u32[]{:S(2)}) collective-permute-start(bf16[928,128]{1,0:T(8,128)(2,1)S(1)} %collective-permute-done.6.b3), channel_id=1, source_target_pairs={{0,32},{32,0},{1,33},{33,1},{2,34},{34,2},{3,35},{35,3},{4,36},{36... | collective-permute-start | bytes 712712 | tf_op jit(solution)/shard_map/ppermute | solution.py:341
  134.7 2.5 %collective-permute-start.9 = (bf16[928,128]{1,0:T(8,128)(2,1)S(1)}, bf16[928,128]{1,0:T(8,128)(2,1)S(1)}, u32[]{:S(2)}, u32[]{:S(2)}) collective-permute-start(bf16[928,128]{1,0:T(8,128)(2,1)S(1)} %collective-permute-done.5.b2), channel_id=1, source_target_pairs={{0,32},{32,0},{1,33},{33,1},{2,34},{34,2},{3,35},{35,3},{4,36},{36... | collective-permute-start | bytes 712712 | tf_op jit(solution)/shard_map/ppermute | solution.py:341
  137.2 2.4 %collective-permute-start.8 = (bf16[928,128]{1,0:T(8,128)(2,1)S(1)}, bf16[928,128]{1,0:T(8,128)(2,1)S(1)}, u32[]{:S(2)}, u32[]{:S(2)}) collective-permute-start(bf16[928,128]{1,0:T(8,128)(2,1)S(1)} %collective-permute-done.4.b1), channel_id=1, source_target_pairs={{0,32},{32,0},{1,33},{33,1},{2,34},{34,2},{3,35},{35,3},{4,36},{36... | collective-permute-start | bytes 712712 | tf_op jit(solution)/shard_map/ppermute | solution.py:341
  139.7 1.1 collective-permute-done.8.b5
  140.9 11.0 %shard_map.165 = (f32[2,8,29568]{2,1,0:T(8,128)}, bf16[1,2,8,29568]{3,2,1,0:T(8,128)(2,1)}, f32[2,8,29568]{2,1,0:T(8,128)}, f32[8,8192]{1,0:T(8,128)}, bf16[1,8,...) custom-call(s32[2]{0:T(128)S(1)} %pad_add_fusion.pos, ...), custom_call_target="tpu_custom_call" | custom-call | tf_op jit(solution)/shard_map/pallas_call | solution.py:311
  151.8 0.7 copy.20
  (45 shorter events, 0.6 us)
Async XLA Ops:
  0.6 30.4 %copy-start = (bf16[256,64]{0,1:T(8,128)(2,1)S(1)}, bf16[256,64]{0,1:T(8,128)(2,1)}, u32[]{:S(2)}) copy-start(bf16[256,64]{0,1:T(8,128)(2,1)} %param.19) | copy-start | bytes 98308
  0.7 1.5 copy-start.1
  2.2 1.2 copy-start.3
  3.4 1.2 copy-start.5
  4.6 0.9 copy-start.8
  5.6 0.9 copy-start.10
  6.5 0.9 copy-start.12
  7.4 23.8 %copy-start.15 = (bf16[924,128]{1,0:T(8,128)(2,1)S(1)}, bf16[924,128]{1,0:T(8,128)(2,1)}, u32[]{:S(2)}) copy-start(bf16[924,128]{1,0:T(8,128)(2,1)} %param.14) | copy-start | bytes 709636
  27.7 10.8 %collective-permute-start = (bf16[4,32,24,128]{3,2,1,0:T(8,128)(2,1)S(1)}, bf16[4,32,24,128]{3,2,1,0:T(8,128)(2,1)}, u32[]{:S(2)}, u32[]{:S(2)}) collective-permute-start(bf16[4,32,24,128]{3,2,1,0:T(8,128)(2,1)S(1)} %get-tuple-element.21), channel_id=1, source_target_pairs={{0,32},{32,0},{1,33},{33,1},{2,34},{34,2},{3,35},{35,3},{4,36},{36... | collective-permute-start | bytes 2359304 | tf_op jit(solution)/shard_map/ppermute | solution.py:341
  32.0 21.0 %all-to-all-start.1 = ((bf16[8,160,128]{2,1,0:T(8,128)(2,1)}), bf16[8,160,128]{2,1,0:T(8,128)(2,1)S(1)}, u32[]{:S(2)}, u32[]{:S(2)}) async-start(bf16[8,160,128]{2,1,0:T(8,128)(2,1)} %broadcast_in_dim.2), calls=%async_computation.1 | async-start | bytes 655360 | tf_op jit(solution)/shard_map/all_to_all | solution.py:345
  39.8 101.0 %copy-start.9 = (f32[8,8192]{1,0:T(8,128)S(1)}, f32[8,8192]{1,0:T(8,128)}, u32[]{:S(2)}) copy-start(f32[8,8192]{1,0:T(8,128)} %ds.3) | copy-start | bytes 786436
  39.8 101.0 %copy-start.13 = (bf16[1,8,8192]{2,1,0:T(8,128)(2,1)S(1)}, bf16[1,8,8192]{2,1,0:T(8,128)(2,1)}, u32[]{:S(2)}) copy-start(bf16[1,8,8192]{2,1,0:T(8,128)(2,1)} %de.1) | copy-start | bytes 393220
  39.9 101.0 %copy-start.14 = (f32[8,8192]{1,0:T(8,128)S(1)}, f32[8,8192]{1,0:T(8,128)}, u32[]{:S(2)}) copy-start(f32[8,8192]{1,0:T(8,128)} %dm.1) | copy-start | bytes 786436
  39.9 7.6 %collective-permute-start.1 = (bf16[32,24,128]{2,1,0:T(8,128)(2,1)S(1)}, bf16[32,24,128]{2,1,0:T(8,128)(2,1)S(1)}, u32[]{:S(2)}, u32[]{:S(2)}) collective-permute-start(bf16[32,24,128]{2,1,0:T(8,128)(2,1)S(1)} %get-tuple-element.42), channel_id=1, source_target_pairs={{0,64},{64,128},{128,192},{192,0},{1,65},{65,129},{129,193},{193,1... | collective-permute-start | bytes 589832 | tf_op jit(solution)/shard_map/ppermute | solution.py:337
  41.3 6.2 %collective-permute-start.3 = (bf16[32,24,128]{2,1,0:T(8,128)(2,1)S(1)}, bf16[32,24,128]{2,1,0:T(8,128)(2,1)S(1)}, u32[]{:S(2)}, u32[]{:S(2)}) collective-permute-start(bf16[32,24,128]{2,1,0:T(8,128)(2,1)S(1)} %get-tuple-element.43), channel_id=1, source_target_pairs={{0,192},{64,0},{128,64},{192,128},{1,193},{65,1},{129,65},{193,129... | collective-permute-start | bytes 589832 | tf_op jit(solution)/shard_map/ppermute | solution.py:337
  42.8 10.0 %collective-permute-start.2 = (bf16[32,24,128]{2,1,0:T(8,128)(2,1)S(1)}, bf16[32,24,128]{2,1,0:T(8,128)(2,1)S(1)}, u32[]{:S(2)}, u32[]{:S(2)}) collective-permute-start(bf16[32,24,128]{2,1,0:T(8,128)(2,1)S(1)} %get-tuple-element.44), channel_id=1, source_target_pairs={{0,128},{64,192},{128,0},{192,64},{1,129},{65,193},{129,1},{193,65... | collective-permute-start | bytes 589832 | tf_op jit(solution)/shard_map/ppermute | solution.py:337
  52.9 88.0 %copy-start.7 = (f32[2,8,29568]{2,1,0:T(8,128)S(1)}, f32[2,8,29568]{2,1,0:T(8,128)}, u32[]{:S(2)}) copy-start(f32[2,8,29568]{2,1,0:T(8,128)} %gm.1) | copy-start | bytes 5677060
  62.1 78.7 %copy-start.6 = (bf16[1,2,8,29568]{3,2,1,0:T(8,128)(2,1)S(1)}, bf16[1,2,8,29568]{3,2,1,0:T(8,128)(2,1)}, u32[]{:S(2)}) copy-start(bf16[1,2,8,29568]{3,2,1,0:T(8,128)(2,1)} %ge.1) | copy-start | bytes 2838532
  62.6 78.3 %copy-start.2 = (f32[2,8,29568]{2,1,0:T(8,128)S(1)}, f32[2,8,29568]{2,1,0:T(8,128)}, u32[]{:S(2)}) copy-start(f32[2,8,29568]{2,1,0:T(8,128)} %gs.3) | copy-start | bytes 5677060
  62.6 78.3 %copy-start.4 = (bf16[1,2,8,29568]{3,2,1,0:T(8,128)(2,1)S(1)}, bf16[1,2,8,29568]{3,2,1,0:T(8,128)(2,1)}, u32[]{:S(2)}) copy-start(bf16[1,2,8,29568]{3,2,1,0:T(8,128)(2,1)} %gf.1) | copy-start | bytes 2838532
  62.6 78.3 %copy-start.11 = (bf16[1,8,8192]{2,1,0:T(8,128)(2,1)S(1)}, bf16[1,8,8192]{2,1,0:T(8,128)(2,1)}, u32[]{:S(2)}) copy-start(bf16[1,8,8192]{2,1,0:T(8,128)(2,1)} %df.1) | copy-start | bytes 393220
  123.9 5.9 %collective-permute-start.6 = (bf16[928,128]{1,0:T(8,128)(2,1)S(1)}, bf16[928,128]{1,0:T(8,128)(2,1)S(1)}, u32[]{:S(2)}, u32[]{:S(2)}) collective-permute-start(bf16[928,128]{1,0:T(8,128)(2,1)S(1)} %pad_maximum_fusion.b0), channel_id=1, source_target_pairs={{0,192},{64,0},{128,64},{192,128},{1,193},{65,1},{129,65},{193,129... | collective-permute-start | bytes 712712 | tf_op jit(solution)/shard_map/ppermute | solution.py:337
  124.9 9.9 %collective-permute-start.5 = (bf16[928,128]{1,0:T(8,128)(2,1)S(1)}, bf16[928,128]{1,0:T(8,128)(2,1)S(1)}, u32[]{:S(2)}, u32[]{:S(2)}) collective-permute-start(bf16[928,128]{1,0:T(8,128)(2,1)S(1)} %pad_maximum_fusion.b0), channel_id=1, source_target_pairs={{0,128},{64,192},{128,0},{192,64},{1,129},{65,193},{129,1},{193,65... | collective-permute-start | bytes 712712 | tf_op jit(solution)/shard_map/ppermute | solution.py:337
  126.1 11.1 %collective-permute-start.4 = (bf16[928,128]{1,0:T(8,128)(2,1)S(1)}, bf16[928,128]{1,0:T(8,128)(2,1)S(1)}, u32[]{:S(2)}, u32[]{:S(2)}) collective-permute-start(bf16[928,128]{1,0:T(8,128)(2,1)S(1)} %pad_maximum_fusion.b0), channel_id=1, source_target_pairs={{0,64},{64,128},{128,192},{192,0},{1,65},{65,129},{129,193},{193,1... | collective-permute-start | bytes 712712 | tf_op jit(solution)/shard_map/ppermute | solution.py:337
  126.1 13.5 %collective-permute-start.7 = (bf16[928,128]{1,0:T(8,128)(2,1)S(1)}, bf16[928,128]{1,0:T(8,128)(2,1)S(1)}, u32[]{:S(2)}, u32[]{:S(2)}) collective-permute-start(bf16[928,128]{1,0:T(8,128)(2,1)S(1)} %pad_maximum_fusion.b0), channel_id=1, source_target_pairs={{0,32},{32,0},{1,33},{33,1},{2,34},{34,2},{3,35},{35,3},{4,36},{36... | collective-permute-start | bytes 712712 | tf_op jit(solution)/shard_map/ppermute | solution.py:341
  129.8 9.8 %collective-permute-start.10 = (bf16[928,128]{1,0:T(8,128)(2,1)S(1)}, bf16[928,128]{1,0:T(8,128)(2,1)S(1)}, u32[]{:S(2)}, u32[]{:S(2)}) collective-permute-start(bf16[928,128]{1,0:T(8,128)(2,1)S(1)} %collective-permute-done.6.b3), channel_id=1, source_target_pairs={{0,32},{32,0},{1,33},{33,1},{2,34},{34,2},{3,35},{35,3},{4,36},{36... | collective-permute-start | bytes 712712 | tf_op jit(solution)/shard_map/ppermute | solution.py:341
  134.7 4.9 %collective-permute-start.9 = (bf16[928,128]{1,0:T(8,128)(2,1)S(1)}, bf16[928,128]{1,0:T(8,128)(2,1)S(1)}, u32[]{:S(2)}, u32[]{:S(2)}) collective-permute-start(bf16[928,128]{1,0:T(8,128)(2,1)S(1)} %collective-permute-done.5.b2), channel_id=1, source_target_pairs={{0,32},{32,0},{1,33},{33,1},{2,34},{34,2},{3,35},{35,3},{4,36},{36... | collective-permute-start | bytes 712712 | tf_op jit(solution)/shard_map/ppermute | solution.py:341
  137.2 3.6 %collective-permute-start.8 = (bf16[928,128]{1,0:T(8,128)(2,1)S(1)}, bf16[928,128]{1,0:T(8,128)(2,1)S(1)}, u32[]{:S(2)}, u32[]{:S(2)}) collective-permute-start(bf16[928,128]{1,0:T(8,128)(2,1)S(1)} %collective-permute-done.4.b1), channel_id=1, source_target_pairs={{0,32},{32,0},{1,33},{33,1},{2,34},{34,2},{3,35},{35,3},{4,36},{36... | collective-permute-start | bytes 712712 | tf_op jit(solution)/shard_map/ppermute | solution.py:341

commit v2 on v1

v2 whole, which is shorter than its diff:
```python
import functools

import jax
import jax.numpy as jnp
from jax import lax
from jax.experimental import pallas as pl
from jax.experimental.pallas import tpu as pltpu
from jax.sharding import Mesh
from jax.sharding import PartitionSpec as P

FF = 29568
D = 8192
SHARDS = 32
REPS = 8
GU_COLS = FF // SHARDS
DN_COLS = D // SHARDS
LANES = 128
TILES = FF // LANES
RANK = 64
F32 = jnp.float32
BF16 = jnp.bfloat16
SHARD = ("z", "x")
VMEM = pl.BlockSpec(memory_space=pltpu.VMEM)
SMEM = pl.BlockSpec(memory_space=pltpu.SMEM)
ANY = pl.BlockSpec(memory_space=pl.ANY)
GROUPS = 4
PER = SHARDS // GROUPS


def params(mib):
    return pltpu.CompilerParams(vmem_limit_bytes=mib * 2**20)


def first_tile(shard):
    return TILES * shard // SHARDS


def offset(shard):
    return GU_COLS * shard - LANES * first_tile(shard)


def has_ninth(shard):
    return offset(shard) > 8 * LANES - GU_COLS


def lane_ids():
    return lax.broadcasted_iota(jnp.int32, (8, LANES), 1)


def group_bounds():
    bounds = [0]
    for g in range(GROUPS):
        bounds.append(min(TILES, first_tile(PER * (g + 1)) + 1) * LANES)
    return bounds


GU_ROWS = SHARDS * 16
DN_TILES = D // REPS // LANES
BLOCK = GU_ROWS + DN_TILES * 8


def lower_kernel(pos, gs, gf, ge, ds, df, de, own, oth, gsv, gfv, gev, dsv, dfv, dev, sems):
    y, core = pos[0], pos[1]
    bounds = group_bounds()
    copies = []
    for g in range(GROUPS):
        a, n = bounds[g], bounds[g + 1] - bounds[g]
        c, m = DN_COLS * PER * g, DN_COLS * PER
        row = []
        for i, (src, dst) in enumerate(((gs, gsv), (gf, gfv), (ge, gev))):
            at = (slice(None), slice(None), pl.ds(a, n))
            row.append(pltpu.make_async_copy(src.at[at], dst.at[at], sems.at[g, i]))
        for i, (src, dst) in enumerate(((ds, dsv), (df, dfv), (de, dev))):
            at = (slice(None), pl.ds(c, m))
            row.append(pltpu.make_async_copy(src.at[at], dst.at[at], sems.at[g, 3 + i]))
        for copy in row:
            copy.start()
        copies.append(row)
    first = core == 0
    lane = lane_ids()
    slots = [lax.rem(yy - y + 4, 4) for yy in range(4)]

    def gu_tile(tile):
        at = (slice(None), slice(None), pl.ds(tile * LANES, LANES))
        return gsv[at] - gfv[at].astype(F32) + gev[at].astype(F32)

    for shard in range(SHARDS):
        if shard % PER == 0:
            for copy in copies[shard // PER]:
                copy.wait()
        tiles = [gu_tile(first_tile(shard) + j) for j in range(8)]
        if has_ninth(shard):
            tiles[0] = jnp.where(lane[None] < 24, gu_tile(first_tile(shard) + 8), tiles[0])
        for yy in range(4):
            one, two = (tiles[2 * yy + c].reshape(16, LANES) for c in range(2))
            at = slice(16 * shard, 16 * shard + 16)
            own[slots[yy], at] = jnp.where(first, one, two).astype(BF16)
            oth[slots[yy], at] = jnp.where(first, two, one).astype(BF16)
    for half in range(DN_TILES // 2):
        parts = [[None, None] for _ in range(REPS)]
        for k in range(2):
            wide = pl.ds(4 * DN_COLS * (2 * half + k), 4 * DN_COLS)
            dn = dsv[:, wide] - dfv[:, wide].astype(F32) + dev[:, wide].astype(F32)
            for r in range(REPS):
                tile = None
                for a in range(4):
                    at = DN_COLS * a + LANES * (r // 4)
                    piece = dn[:, at : at + LANES]
                    if a != r % 4:
                        piece = pltpu.roll(piece, 32 * (a - r % 4) % LANES, 1)
                    tile = piece if a == 0 else jnp.where(lane < 32 * a, tile, piece)
                parts[r][k] = tile
        for yy in range(4):
            one, two = (jnp.concatenate(parts[2 * yy + c], axis=0) for c in range(2))
            at = slice(GU_ROWS + 16 * half, GU_ROWS + 16 * half + 16)
            own[slots[yy], at] = jnp.where(first, one, two).astype(BF16)
            oth[slots[yy], at] = jnp.where(first, two, one).astype(BF16)


def lower(pos, gs, gf, ge, ds, df, de):
    shape = jax.ShapeDtypeStruct((4, BLOCK, LANES), BF16)
    return pl.pallas_call(
        lower_kernel,
        out_shape=(shape, shape),
        in_specs=[SMEM] + [ANY] * 6,
        out_specs=(VMEM, VMEM),
        scratch_shapes=[
            pltpu.VMEM((2, 8, FF), F32),
            pltpu.VMEM((2, 8, FF), BF16),
            pltpu.VMEM((2, 8, FF), BF16),
            pltpu.VMEM((8, D), F32),
            pltpu.VMEM((8, D), BF16),
            pltpu.VMEM((8, D), BF16),
            pltpu.SemaphoreType.DMA((GROUPS, 6)),
        ],
        compiler_params=params(56),
    )(pos, gs, gf, ge, ds, df, de)


B_ROWS = LANES + 16


def basis_kernel(pos, gu, dn_t, out, rows, dn_rows):
    rep, shard = 2 * pos[0] + pos[1], pos[2]
    start = LANES - offset(shard)
    rows[0:LANES, :] = jnp.zeros((LANES, LANES), F32)
    rows[LANES : LANES + GU_COLS, :] = gu[...].astype(F32)
    rows[LANES + GU_COLS :, :] = jnp.zeros((rows.shape[0] - LANES - GU_COLS, LANES), F32)
    tile = rows[pl.ds(start + LANES * rep, LANES), :]
    ninth = rows[pl.ds(start + LANES * 8, LANES), :]
    tile = tile + jnp.where(rep == 0, ninth, 0.0)
    dn_rows[...] = dn_t[...].astype(F32).T
    dn = dn_rows[pl.ds(pl.multiple_of(32 * rep, 32), 32), :]
    dn = jnp.concatenate([dn[0:16], dn[16:32]], axis=1)
    block = jnp.concatenate([tile, dn], axis=0).astype(BF16)
    for s in range(SHARDS):
        out[s] = block


def basis_tiles(pos, gu, dn_t):
    return pl.pallas_call(
        basis_kernel,
        out_shape=jax.ShapeDtypeStruct((SHARDS, B_ROWS, LANES), BF16),
        in_specs=[SMEM, VMEM, VMEM],
        out_specs=VMEM,
        scratch_shapes=[pltpu.VMEM((1280, LANES), F32), pltpu.VMEM((DN_COLS, RANK), F32)],
        compiler_params=params(16),
    )(pos, gu, dn_t)


def y_sum_kernel(own, came, one, two, three, out):
    for at in range(0, BLOCK, 64):
        rows = slice(at, at + 64)
        total = own[0, rows].astype(F32) + came[0, rows].astype(F32)
        for ref in (one, two, three):
            total = total + ref[rows].astype(F32)
        out[rows] = total.astype(BF16)


def y_sum(own, came, comes):
    return pl.pallas_call(
        y_sum_kernel,
        out_shape=jax.ShapeDtypeStruct((BLOCK, LANES), BF16),
        in_specs=[VMEM] * 5,
        out_specs=VMEM,
        compiler_params=params(16),
    )(own, came, comes[1], comes[2], comes[3])


def split_hi_lo(value):
    hi = value.astype(BF16).astype(F32)
    return jnp.concatenate([hi, value - hi], axis=-1).astype(BF16)


def p_part_kernel(lbar, basis, out):
    gu = jnp.zeros((16, LANES), F32)
    for s in range(0, SHARDS, 2):
        left = jnp.concatenate(
            [lbar[16 * s : 16 * s + 16, :], lbar[16 * s + 16 : 16 * s + 32, :]], axis=1
        )
        right = basis[s : s + 2, 0:LANES, :].reshape(2 * LANES, LANES)
        gu = gu + jnp.dot(left, right, preferred_element_type=F32)
    tiles = lbar[GU_ROWS:BLOCK, :].astype(F32)
    dn = jnp.zeros((8, RANK), F32)
    for q in range(DN_TILES):
        right = basis[4 * q : 4 * q + 4, LANES:B_ROWS, :].astype(F32)
        right = jnp.concatenate([right[:, :, 0:RANK], right[:, :, RANK:LANES]], axis=1)
        dn = dn + jnp.dot(
            tiles[8 * q : 8 * q + 8].astype(BF16),
            right.reshape(LANES, RANK).astype(BF16),
            preferred_element_type=F32,
        )
    part = jnp.concatenate([gu[0:8, 0:RANK], gu[8:16, RANK:LANES], dn], axis=0)
    block = split_hi_lo(part)
    for rep in range(REPS):
        out[rep] = block


def p_part(lbar, basis):
    return pl.pallas_call(
        p_part_kernel,
        out_shape=jax.ShapeDtypeStruct((REPS, 24, LANES), BF16),
        in_specs=[VMEM, VMEM],
        out_specs=VMEM,
        compiler_params=params(16),
    )(lbar, basis)


def p_sum_kernel(ps, lbar, out):
    total = jnp.sum(ps[...].astype(F32), axis=0)
    rows = split_hi_lo(total[:, 0:RANK] + total[:, RANK:LANES]).astype(F32)
    tiles = lbar[GU_ROWS:BLOCK, :].astype(F32)
    for s in range(SHARDS):
        gu = lbar[16 * s : 16 * s + 16, :].astype(F32)
        dn = tiles[8 * (s // 4) : 8 * (s // 4) + 8]
        out[s] = jnp.concatenate([gu, dn, rows], axis=0).astype(BF16)


def p_sum(ps, lbar):
    return pl.pallas_call(
        p_sum_kernel,
        out_shape=jax.ShapeDtypeStruct((SHARDS, 48, LANES), BF16),
        in_specs=[VMEM, VMEM],
        out_specs=VMEM,
        compiler_params=params(16),
    )(ps, lbar)


def inverse_factors(grams):
    eye = (
        lax.broadcasted_iota(jnp.int32, (RANK, RANK), 0)
        == lax.broadcasted_iota(jnp.int32, (RANK, RANK), 1)
    ).astype(F32)
    sub = lax.broadcasted_iota(jnp.int32, (8, LANES), 0)

    def spread_lane(x, k):
        return jnp.broadcast_to(x[:, k : k + 1], (8, LANES))

    def spread_row(x, k):
        return jnp.broadcast_to(x[k : k + 1], (8, LANES))

    works = []
    for gram in grams:
        work = jnp.concatenate([gram, eye], axis=1)
        works.append([work[8 * b : 8 * b + 8] for b in range(8)])
    outs = [[] for _ in grams]
    for now in range(8):
        pivots = [jnp.ones((8, LANES), F32) for _ in grams]
        ratios, rows = [[] for _ in grams], [[] for _ in grams]
        spread = [[spread_lane(work[now], 8 * now + j) for j in range(8)] for work in works]
        for j in range(8):
            for m, work in enumerate(works):
                cols = spread[m]
                pivot = spread_row(cols[j], j)
                inverse = 1.0 / pivot
                pivots[m] = jnp.where(sub == j, pivot, pivots[m])
                rows[m].append(spread_row(work[now], j) * inverse)
                ratios[m].append([spread_row(cols[i], j) * inverse for i in range(j + 1, 8)])
                if j < 7:
                    below = jnp.where(sub > j, cols[j], 0.0)
                    for i in range(j + 1, 8):
                        cols[i] = cols[i] - below * ratios[m][j][i - j - 1]
                    work[now] = work[now] - below * rows[m][j]
        for m, work in enumerate(works):
            for b in range(now + 1, 8):
                cols = [spread_lane(work[b], 8 * now + j) for j in range(8)]
                for j in range(8):
                    for i in range(j + 1, 8):
                        cols[i] = cols[i] - cols[j] * ratios[m][j][i - j - 1]
                    work[b] = work[b] - cols[j] * rows[m][j]
            outs[m].append(work[now] * lax.rsqrt(pivots[m]))
    return [jnp.concatenate(out, axis=0)[:, RANK:LANES] for out in outs]


def exact_dot(a, b, dims):
    return lax.dot_general(
        a, b, (dims, ((), ())), precision=lax.Precision.HIGHEST, preferred_element_type=F32
    )


def factor_kernel(pos, recv, a_out, q_out, q_rows):
    block = recv[...].astype(F32)
    columns = [
        block[:, 8 * m : 8 * m + 8, :].reshape(256, LANES).astype(BF16) for m in range(3)
    ]
    left = block[:, 24:48, :]
    left = left[:, :, 0:RANK] + left[:, :, RANK:LANES]
    lefts = [left[:, 8 * m : 8 * m + 8, :].reshape(256, RANK) for m in range(3)]
    grams = [exact_dot(p, p, ((0,), (0,))) for p in lefts]
    inverses = inverse_factors(grams)
    hs = [exact_dot(p, v, ((1,), (1,))).astype(BF16) for p, v in zip(lefts, inverses)]
    recons, qs = [], []
    for h, column in zip(hs, columns):
        q = lax.dot_general(column, h, (((0,), (0,)), ((), ())), preferred_element_type=F32)
        q = (q * (1.0 / REPS)).astype(BF16)
        qs.append(q.astype(F32))
        recon = lax.dot_general(h, q, (((1,), (1,)), ((), ())), preferred_element_type=F32)
        recons.append(recon.reshape(SHARDS, 8, LANES))
    a_out[...] = jnp.concatenate(recons, axis=1).astype(BF16)
    q_rows[...] = qs[2]
    dn = q_rows[pl.ds(pl.multiple_of(32 * lax.rem(pos[2], 4), 32), 32), :]
    dn = jnp.concatenate([dn, jnp.zeros_like(dn)], axis=1)
    gu = jnp.concatenate(qs[:2], axis=1)
    q_out[...] = jnp.concatenate([gu, dn], axis=0).astype(BF16)


def factor(pos, recv):
    return pl.pallas_call(
        factor_kernel,
        out_shape=(
            jax.ShapeDtypeStruct((SHARDS, 24, LANES), BF16),
            jax.ShapeDtypeStruct((Q_ROWS, LANES), BF16),
        ),
        in_specs=[SMEM, VMEM],
        out_specs=(VMEM, VMEM),
        scratch_shapes=[pltpu.VMEM((LANES, RANK), F32)],
        compiler_params=params(32),
    )(pos, recv)


Q_ROWS = LANES + 32
PAYLOAD = BLOCK + Q_ROWS


def pack_kernel(rows, q, out):
    for s in range(SHARDS):
        out[16 * s : 16 * s + 16, :] = rows[s].astype(F32)[0:16].astype(BF16)
    for half in range(DN_TILES // 2):
        two = [rows[8 * half + 4 * k].astype(F32)[16:24] for k in range(2)]
        at = GU_ROWS + 16 * half
        out[at : at + 16, :] = jnp.concatenate(two, axis=0).astype(BF16)
    out[BLOCK:PAYLOAD, :] = q[...]


def pack(rows, q):
    return pl.pallas_call(
        pack_kernel,
        out_shape=jax.ShapeDtypeStruct((PAYLOAD, LANES), BF16),
        in_specs=[VMEM, VMEM],
        out_specs=VMEM,
        compiler_params=params(16),
    )(rows, q)


def finish_kernel(
    pos, b0, b1, b2, b3, b4, b5, b6, b7, gs, gf, ge, gm, ds, df, de, dm,
    gs_o, ge_o, gm_o, ds_o, de_o, dm_o, gb_o, db_o,
    gs_v, ge_v, gm_v, ds_v, de_v, dm_v, stage, q_full, q_dn,
    gs_i, gf_i, ge_i, gm_i, ds_i, df_i, de_i, dm_i, sems, sems_in,
):
    arrivals = []

    def bring(pairs, at):
        row = []
        for i, (src, dst) in enumerate(pairs):
            row.append(
                pltpu.make_async_copy(src.at[at], dst.at[at], sems_in.at[len(arrivals), i])
            )
            row[-1].start()
        arrivals.append(row)

    bounds = [first_tile(PER * g) * LANES for g in range(GROUPS + 1)]
    for g in range(GROUPS):
        bring(
            ((gs, gs_i), (gf, gf_i), (ge, ge_i), (gm, gm_i)),
            (slice(None), slice(None), pl.ds(bounds[g], bounds[g + 1] - bounds[g])),
        )
    bring(((ds, ds_i), (df, df_i), (de, de_i), (dm, dm_i)), (slice(None), slice(None)))
    y, core, mine = pos[0], pos[1], pos[2]
    for i, block in enumerate((b0, b1, b2, b3, b4, b5, b6, b7)):
        rep = 2 * lax.rem(y - i % 4 + 4, 4) + (core if i < 4 else 1 - core)
        stage[rep] = block[...]

    def outer(slow, fast, error, moment, recon):
        combined = slow - fast.astype(F32) + error.astype(F32)
        moment_next = 0.9 * moment + recon
        return (
            slow - 0.7 * (recon + 0.9 * moment_next),
            (combined - recon).astype(BF16),
            moment_next,
        )

    copies = []

    def send(pairs, at):
        for src, dst in pairs:
            copies.append(pltpu.make_async_copy(src.at[at], dst.at[at], sems.at[len(copies)]))
            copies[-1].start()

    lane = lane_ids()

    def gu_recon(rep, shard):
        return stage[rep, 16 * shard : 16 * shard + 16, :].astype(F32).reshape(2, 8, LANES)

    for g in range(GROUPS):
        for copy in arrivals[g]:
            copy.wait()
        for shard in range(PER * g, PER * (g + 1)):
            for j in range(first_tile(shard + 1) - first_tile(shard)):
                recon = gu_recon(j, shard)
                if j == 0 and offset(shard) > 0:
                    other = gu_recon(0 if has_ninth(shard - 1) else 7, shard - 1)
                    recon = jnp.where(lane[None] < offset(shard), other, recon)
                at = (slice(None), slice(None), pl.ds((first_tile(shard) + j) * LANES, LANES))
                gs_v[at], ge_v[at], gm_v[at] = outer(
                    gs_i[at], gf_i[at], ge_i[at], gm_i[at], recon
                )
        send(
            ((gs_v, gs_o), (ge_v, ge_o), (gm_v, gm_o)),
            (slice(None), slice(None), pl.ds(bounds[g], bounds[g + 1] - bounds[g])),
        )
    for copy in arrivals[GROUPS]:
        copy.wait()
    tiles = [stage[r, GU_ROWS:BLOCK, :].astype(F32) for r in range(REPS)]
    for shard in range(SHARDS):
        q, a = shard // 4, shard % 4
        for half in range(2):
            recon = None
            for k in range(4):
                piece = tiles[4 * half + k][8 * q : 8 * q + 8]
                if k != a:
                    piece = pltpu.roll(piece, 32 * (k - a) % LANES, 1)
                recon = piece if k == 0 else jnp.where(lane < 32 * k, recon, piece)
            at = (slice(None), pl.ds(DN_COLS * shard + LANES * half, LANES))
            ds_v[at], de_v[at], dm_v[at] = outer(ds_i[at], df_i[at], de_i[at], dm_i[at], recon)
    send(((ds_v, ds_o), (de_v, de_o), (dm_v, dm_o)), (slice(None), slice(None)))

    for r in range(REPS):
        block = stage[r, BLOCK:PAYLOAD, :].astype(F32)
        q_full[LANES * r : LANES * r + LANES, :] = block[0:LANES]
        if r == 0:
            q_full[8 * LANES : 9 * LANES, :] = block[0:LANES]
        q_dn[32 * r : 32 * r + 32, :] = block[LANES:Q_ROWS, 0:RANK]
    gb_o[...] = q_full[pl.ds(offset(mine), GU_COLS), :].astype(BF16)
    db_o[...] = q_dn[...].T.astype(BF16)
    for copy in copies:
        copy.wait()


def finish(pos, blocks, gs, gf, ge, gm, ds, df, de, dm):
    def like(a):
        return jax.ShapeDtypeStruct(a.shape, a.dtype)

    gu, dn = (2, 8, FF), (8, D)
    return pl.pallas_call(
        finish_kernel,
        out_shape=(
            like(gs), like(ge), like(gm), like(ds), like(de), like(dm),
            jax.ShapeDtypeStruct((GU_COLS, LANES), BF16),
            jax.ShapeDtypeStruct((RANK, DN_COLS), BF16),
        ),
        in_specs=[SMEM] + [VMEM] * 8 + [ANY] * 8,
        out_specs=(ANY,) * 6 + (VMEM, VMEM),
        scratch_shapes=[
            pltpu.VMEM(gu, F32),
            pltpu.VMEM(gu, BF16),
            pltpu.VMEM(gu, F32),
            pltpu.VMEM(dn, F32),
            pltpu.VMEM(dn, BF16),
            pltpu.VMEM(dn, F32),
            pltpu.VMEM((REPS, PAYLOAD, LANES), BF16),
            pltpu.VMEM((9 * LANES, LANES), F32),
            pltpu.VMEM((DN_COLS, RANK), F32),
            pltpu.VMEM(gu, F32),
            pltpu.VMEM(gu, BF16),
            pltpu.VMEM(gu, BF16),
            pltpu.VMEM(gu, F32),
            pltpu.VMEM(dn, F32),
            pltpu.VMEM(dn, BF16),
            pltpu.VMEM(dn, BF16),
            pltpu.VMEM(dn, F32),
            pltpu.SemaphoreType.DMA((3 * (GROUPS + 1),)),
            pltpu.SemaphoreType.DMA((GROUPS + 1, 4)),
        ],
        compiler_params=params(56),
    )(pos, *blocks, gs, gf, ge, gm, ds, df, de, dm)


def shift(value, axis, size, by):
    return lax.ppermute(value, axis, [(i, (i + by) % size) for i in range(size)])


def swap(value):
    return lax.ppermute(value, "core", [(0, 1), (1, 0)])


def exchange(value, axis):
    return lax.all_to_all(value, axis, 0, 0, tiled=False)


def on_device(
    gu_slow, gu_fast, gu_error, gu_moment, gu_basis, dn_slow, dn_fast, dn_error, dn_moment, dn_basis
):
    pos = jnp.stack([lax.axis_index("y"), lax.axis_index("core"), lax.axis_index(SHARD)])
    pos = pos.astype(jnp.int32)
    gu_fast, gu_error = gu_fast[0], gu_error[0]
    dn_fast, dn_error = dn_fast[0], dn_error[0]
    basis = exchange(basis_tiles(pos, gu_basis, dn_basis.T), SHARD)
    own, oth = lower(pos, gu_slow, gu_fast, gu_error, dn_slow, dn_fast, dn_error)
    came = swap(oth)
    pair = own.astype(F32) + came.astype(F32)
    sends = {by: pair[by].astype(BF16) for by in (2, 1, 3)}
    comes = {by: shift(sends[by], "y", 4, by) for by in (2, 1, 3)}
    lbar = y_sum(own, came, comes)
    parts = exchange(p_part(lbar, basis), ("y", "core"))
    recv = exchange(p_sum(parts, lbar), SHARD)
    a_blocks, q_block = factor(pos, recv)
    payload = pack(exchange(a_blocks, SHARD), q_block)
    mine = {0: payload}
    for by in (2, 1, 3):
        mine[by] = shift(payload, "y", 4, by)
    blocks = [mine[by] for by in range(4)]
    blocks = blocks + [swap(b) for b in blocks]
    gs, ge, gm, ds, de, dm, gb, db = finish(
        pos, blocks, gu_slow, gu_fast, gu_error, gu_moment, dn_slow, dn_fast, dn_error, dn_moment
    )
    return gs, ge[None], gm, gb, ds, de[None], dm, db.T


def solution(mesh):
    fine = Mesh(mesh.devices.reshape(4, 2, 8, 4), ("y", "core", "z", "x"))
    rep = ("y", "core")
    weights, shared = P(None, SHARD, None), P(SHARD, None)
    replica = P(rep, None, SHARD, None)
    dn_replica = P(rep, SHARD, None)
    return jax.shard_map(
        on_device,
        mesh=fine,
        in_specs=(
            weights, replica, replica, weights, shared,
            shared, dn_replica, dn_replica, shared, shared,
        ),
        out_specs=(
            weights, replica, weights, shared,
            shared, dn_replica, shared, shared,
        ),
        check_vma=False,
    )
```

time: 153 us -> 120 us (0.78)
  Pallas kernels: 42.4 us -> 19.4 us
  blocking collectives: 59.7 us -> 45.8 us
  waiting for transfers between devices: 9.59 us -> 19 us
  local copies, waits for them, and re-layouts: 8.47 us -> 2.43 us
    pallas_call x1, Pallas kernels: 20.3 us -> 4.3 us  [lower(): pl.pallas_call(lower_kernel, out_shape=(shape, shape), in_specs=[SMEM] +...]
    all_to_all x4 -> x3, blocking collectives: 59.7 us -> 45.8 us  [exchange(): return lax.all_to_all(value, axis, 0, 0, tiled=False)]
    all_to_all x1, waiting for transfers between devices: 0.01 us -> 6.75 us  [exchange(): return lax.all_to_all(value, axis, 0, 0, tiled=False)]
    pallas_call x1, Pallas kernels: 10.5 us -> 5.02 us  [factor(): pl.pallas_call(factor_kernel, out_shape=(jax.ShapeDtypeStruct((SHARDS, 24...]
    all_to_all x1, starting transfers between devices: 6.45 us -> 11.9 us  [exchange(): return lax.all_to_all(value, axis, 0, 0, tiled=False)]
    unnamed x34 -> x26, local copies, waits for them, and re-layouts: 7.5 us -> 2.4 us
    ppermute x5, starting transfers between devices: 16.9 us -> 12.5 us  [swap(): return lax.ppermute(value, 'core', [(0, 1), (1, 0)])]
    ppermute x5, waiting for transfers between devices: 1.13 us -> 2.87 us  [swap(): return lax.ppermute(value, 'core', [(0, 1), (1, 0)])]
  transfers between devices with their start and end apart: 12 -> 12, of which waited for: 3 -> 6; matrix products, arithmetic and copies ran while one was open for 2% -> 1% of each run, Pallas kernels for 0% -> 4%
where the time goes in v2:
time: 120 us; the launch traced here: 119 us
  blocking collectives  45.8 us (38%)
  starting transfers between devices  30.4 us (25%)
  Pallas kernels  19.4 us (16%)
  waiting for transfers between devices  19 us (16%)
  local copies, waits for them, and re-layouts  2.43 us (2%)
  other arithmetic  1.37 us (1%)
    all_to_all x3, blocking collectives, exchange(): return lax.all_to_all(value, axis, 0, 0, tiled=False)  45.8 us
    ppermute x5, starting transfers between devices, swap(): return lax.ppermute(value, 'core', [(0, 1), (1, 0)])  12.5 us
    all_to_all x1, starting transfers between devices, exchange(): return lax.all_to_all(value, axis, 0, 0, tiled=False)  11.9 us
    ppermute x6, waiting for transfers between devices, shift(): lax.ppermute(value, axis, [(i, (i + by) % size) for i in range(size)])  9.4 us
    pallas_call x1, Pallas kernels, finish(): pl.pallas_call(finish_kernel, out_shape=(like(gs), like(ge), like(gm), li...  7.53 us
    all_to_all x1, waiting for transfers between devices, exchange(): return lax.all_to_all(value, axis, 0, 0, tiled=False)  6.75 us
    ppermute x6, starting transfers between devices, shift(): lax.ppermute(value, axis, [(i, (i + by) % size) for i in range(size)])  6 us
    pallas_call x1, Pallas kernels, factor(): pl.pallas_call(factor_kernel, out_shape=(jax.ShapeDtypeStruct((SHARDS, 24...  5.02 us
  transfers between devices with their start and end apart: 12, of which 6 were waited for; matrix products, arithmetic and copies ran while one was open for 1% of the time, Pallas kernels for 4%

profile of v2, /device:TPU:1, one launch (start us, length us, event | category | flops | bytes accessed | tf_op | source)
XLA Modules:
  0.0 119.3 jit_solution(12217031393483707934)
XLA Ops:
  0.6 0.1 pad_add_fusion.pos
  0.7 0.9 copy-done.2
  1.7 0.8 copy-done.3
  2.4 1.8 %shard_map.163 = bf16[32,144,128]{2,1,0:T(8,128)(2,1)} custom-call(s32[3]{0:T(128)S(1)} %pad_add_fusion.pos, bf16[924,128]{1,0:T(8,128)(2,1)S(1)} %copy-done.2, bf16[64,256]{1,0:T(8,128)(2,1)S(1)} %bitcast.17), custom_call_target="tpu_custom_call" | custom-call | tf_op jit(solution)/shard_map/pallas_call | solution.py:161
  4.2 11.9 %all-to-all-start = ((bf16[32,144,128]{2,1,0:T(8,128)(2,1)}), bf16[32,144,128]{2,1,0:T(8,128)(2,1)S(1)}, u32[]{:S(2)}, u32[]{:S(2)}) async-start(bf16[32,144,128]{2,1,0:T(8,128)(2,1)} %shard_map.163), calls=%async_computation | async-start | bytes 2359296 | tf_op jit(solution)/shard_map/all_to_all | solution.py:508
  16.1 4.3 %shard_map.161 = (bf16[4,576,128]{2,1,0:T(8,128)(2,1)}, bf16[4,576,128]{2,1,0:T(8,128)(2,1)}) custom-call(s32[3]{0:T(128)} %copy-done.4, f32[2,8,29568]{2,1,0:T(8,128)} %gs.3, bf16[2,8,29568]{2,1,0:T(8,128)(2,1)} %bitcast.18, bf16[2,8,29568]{2,1,0:T(8,128)(2,1)} %bitcast.20, f32[8,8192]{1,0:T(8,128)} %ds.3, bf16[8,8192]{1,0:T(8,128)(2,1)} %bitcast.22, ...), custom_call_target="tpu_custom_call" | custom-call | tf_op jit(solution)/shard_map/pallas_call | solution.py:122
  20.4 1.0 collective-permute-start
  21.4 1.8 %collective-permute-done.came = bf16[4,576,128]{2,1,0:T(8,128)(2,1)S(1)} collective-permute-done((bf16[4,576,128]{2,1,0:T(8,128)(2,1)}, bf16[4,576,128]{2,1,0:T(8,128)(2,1)S(1)}, u32[]{:S(2)}, u32[]{:S(2)}) %collective-permute-start) | collective-permute-done | bytes 589856 | tf_op jit(solution)/shard_map/ppermute | solution.py:504
  23.2 1.3 %add_convert_fusion = bf16[4,576,128]{2,1,0:T(8,128)(2,1)S(1)} fusion(bf16[4,576,128]{2,1,0:T(8,128)(2,1)S(1)} %collective-permute-done.came, bf16[4,576,128]{2,1,0:T(8,128)(2,1)} %get-tuple-element.20.own), kind=kLoop, calls=%fused_computation | loop fusion | flops 1179648 | bytes 1769472 | tf_op jit(solution)/shard_map/convert.2
  24.6 2.8 %collective-permute-start.3 = (bf16[576,128]{1,0:T(8,128)(2,1)S(1)}, bf16[576,128]{1,0:T(8,128)(2,1)S(1)}, u32[]{:S(2)}, u32[]{:S(2)}) collective-permute-start(bf16[576,128]{1,0:T(8,128)(2,1)S(1)} %get-tuple-element.32), channel_id=1, source_target_pairs={{0,192},{64,0},{128,64},{192,128},{1,193},{65,1},{129,65},{193,129... | collective-permute-start | bytes 442376 | tf_op jit(solution)/shard_map/ppermute | solution.py:500
  27.4 0.3 collective-permute-start.2
  27.7 0.7 collective-permute-start.1
  28.4 4.9 %collective-permute-done.3.three = bf16[576,128]{1,0:T(8,128)(2,1)S(1)} collective-permute-done((bf16[576,128]{1,0:T(8,128)(2,1)S(1)}, bf16[576,128]{1,0:T(8,128)(2,1)S(1)}, u32[]{:S(2)}, u32[]{:S(2)}) %collective-permute-start.3) | collective-permute-done | bytes 147488 | tf_op jit(solution)/shard_map/ppermute | solution.py:500
  33.3 0.4 collective-permute-done.2.two
  33.7 4.1 %collective-permute-done.1.one = bf16[576,128]{1,0:T(8,128)(2,1)S(1)} collective-permute-done((bf16[576,128]{1,0:T(8,128)(2,1)S(1)}, bf16[576,128]{1,0:T(8,128)(2,1)S(1)}, u32[]{:S(2)}, u32[]{:S(2)}) %collective-permute-start.1) | collective-permute-done | bytes 147488 | tf_op jit(solution)/shard_map/ppermute | solution.py:500
  37.8 0.1 shard_map.162.lbar
  37.9 6.7 %all-to-all-done.basis = bf16[32,144,128]{2,1,0:T(8,128)(2,1)S(1)} async-done(((bf16[32,144,128]{2,1,0:T(8,128)(2,1)}), bf16[32,144,128]{2,1,0:T(8,128)(2,1)S(1)}, u32[]{:S(2)}, u32[]{:S(2)}) %all-to-all-start) | async-done | bytes 1179680 | tf_op jit(solution)/shard_map/all_to_all | solution.py:508
  44.7 0.5 shard_map.164
  45.1 12.2 %all_to_all.20.ps = bf16[8,24,128]{2,1,0:T(8,128)(2,1)S(1)} all-to-all(bf16[8,24,128]{2,1,0:T(8,128)(2,1)S(1)} %shard_map.164), channel_id=1, replica_groups=mesh['y'=4,'core'=2,'z'=8,'x'=4] {'y','core'}, dimensions={0} | all-to-all | bytes 98304 | tf_op jit(solution)/shard_map/all_to_all | solution.py:508
  57.3 0.2 shard_map.165
  57.5 19.1 %all_to_all.21.recv = bf16[32,48,128]{2,1,0:T(8,128)(2,1)S(1)} all-to-all(bf16[32,48,128]{2,1,0:T(8,128)(2,1)S(1)} %shard_map.165), channel_id=1, replica_groups=mesh['y'=4,'core'=2,'z'=8,'x'=4] {'z','x'}, dimensions={0} | all-to-all | bytes 786432 | tf_op jit(solution)/shard_map/all_to_all | solution.py:508
  76.6 5.0 %shard_map.166 = (bf16[32,24,128]{2,1,0:T(8,128)(2,1)S(1)}, bf16[160,128]{1,0:T(8,128)(2,1)S(1)}) custom-call(s32[3]{0:T(128)S(1)} %copy-done.5, bf16[32,48,128]{2,1,0:T(8,128)(2,1)S(1)} %all_to_all.21.recv), custom_call_target="tpu_custom_call" | custom-call | tf_op jit(solution)/shard_map/pallas_call | solution.py:328
  81.6 14.6 %all_to_all.22.rows = bf16[32,24,128]{2,1,0:T(8,128)(2,1)S(1)} all-to-all(bf16[32,24,128]{2,1,0:T(8,128)(2,1)S(1)} %get-tuple-element.22), channel_id=1, replica_groups=mesh['y'=4,'core'=2,'z'=8,'x'=4] {'z','x'}, dimensions={0} | all-to-all | bytes 393216 | tf_op jit(solution)/shard_map/all_to_all | solution.py:508
  96.2 1.0 collective-permute-start.6
  97.2 1.2 collective-permute-start.5
  98.4 3.7 %collective-permute-start.7 = (bf16[736,128]{1,0:T(8,128)(2,1)S(1)}, bf16[736,128]{1,0:T(8,128)(2,1)S(1)}, u32[]{:S(2)}, u32[]{:S(2)}) collective-permute-start(bf16[736,128]{1,0:T(8,128)(2,1)S(1)} %shard_map.167.b0), channel_id=1, source_target_pairs={{0,32},{32,0},{1,33},{33,1},{2,34},{34,2},{3,35},{35,3},{4,36},{36... | collective-permute-start | bytes 565256 | tf_op jit(solution)/shard_map/ppermute | solution.py:504
  102.1 3.4 %collective-permute-start.10 = (bf16[736,128]{1,0:T(8,128)(2,1)S(1)}, bf16[736,128]{1,0:T(8,128)(2,1)S(1)}, u32[]{:S(2)}, u32[]{:S(2)}) collective-permute-start(bf16[736,128]{1,0:T(8,128)(2,1)S(1)} %collective-permute-done.6.b3), channel_id=1, source_target_pairs={{0,32},{32,0},{1,33},{33,1},{2,34},{34,2},{3,35},{35,3},{4,36},{36... | collective-permute-start | bytes 565256 | tf_op jit(solution)/shard_map/ppermute | solution.py:504
  105.5 2.5 %collective-permute-start.9 = (bf16[736,128]{1,0:T(8,128)(2,1)S(1)}, bf16[736,128]{1,0:T(8,128)(2,1)S(1)}, u32[]{:S(2)}, u32[]{:S(2)}) collective-permute-start(bf16[736,128]{1,0:T(8,128)(2,1)S(1)} %collective-permute-done.5.b2), channel_id=1, source_target_pairs={{0,32},{32,0},{1,33},{33,1},{2,34},{34,2},{3,35},{35,3},{4,36},{36... | collective-permute-start | bytes 565256 | tf_op jit(solution)/shard_map/ppermute | solution.py:504
  108.0 1.9 %collective-permute-start.8 = (bf16[736,128]{1,0:T(8,128)(2,1)S(1)}, bf16[736,128]{1,0:T(8,128)(2,1)S(1)}, u32[]{:S(2)}, u32[]{:S(2)}) collective-permute-start(bf16[736,128]{1,0:T(8,128)(2,1)S(1)} %collective-permute-done.4.b1), channel_id=1, source_target_pairs={{0,32},{32,0},{1,33},{33,1},{2,34},{34,2},{3,35},{35,3},{4,36},{36... | collective-permute-start | bytes 565256 | tf_op jit(solution)/shard_map/ppermute | solution.py:504
  109.9 1.0 collective-permute-done.8.b5
  111.0 0.7 copy-done.12
  111.6 7.5 %shard_map.168 = (f32[2,8,29568]{2,1,0:T(8,128)}, bf16[2,8,29568]{2,1,0:T(8,128)(2,1)}, f32[2,8,29568]{2,1,0:T(8,128)}, f32[8,8192]{1,0:T(8,128)}, bf16[8,8192]{...) custom-call(s32[3]{0:T(128)} %copy-done.4, bf16[736,128]{1,0:T(8,128)(2,1)} %copy-done.1, ...), custom_call_target="tpu_custom_call" | custom-call | tf_op jit(solution)/shard_map/pallas_call | solution.py:465
  (32 shorter events, 0.1 us)
Async XLA Ops:
  0.7 3.5 %copy-start.4 = (s32[3]{0:T(128)}, s32[3]{0:T(128)S(1)}, u32[]{:S(2)}) copy-start(s32[3]{0:T(128)S(1)} %pad_add_fusion.pos) | copy-start | bytes 40
  0.7 0.9 copy-start.2
  1.7 0.8 copy-start.3
  4.2 40.5 %all-to-all-start = ((bf16[32,144,128]{2,1,0:T(8,128)(2,1)}), bf16[32,144,128]{2,1,0:T(8,128)(2,1)S(1)}, u32[]{:S(2)}, u32[]{:S(2)}) async-start(bf16[32,144,128]{2,1,0:T(8,128)(2,1)} %shard_map.163), calls=%async_computation | async-start | bytes 2359296 | tf_op jit(solution)/shard_map/all_to_all | solution.py:508
  20.4 2.9 %collective-permute-start = (bf16[4,576,128]{2,1,0:T(8,128)(2,1)}, bf16[4,576,128]{2,1,0:T(8,128)(2,1)S(1)}, u32[]{:S(2)}, u32[]{:S(2)}) collective-permute-start(bf16[4,576,128]{2,1,0:T(8,128)(2,1)} %get-tuple-element.21), channel_id=1, source_target_pairs={{0,32},{32,0},{1,33},{33,1},{2,34},{34,2},{3,35},{35,3},{4,36},{36... | collective-permute-start | bytes 1769480 | tf_op jit(solution)/shard_map/ppermute | solution.py:504
  23.2 14.6 %copy-start = (bf16[4,576,128]{2,1,0:T(8,128)(2,1)S(1)}, bf16[4,576,128]{2,1,0:T(8,128)(2,1)}, u32[]{:S(2)}) copy-start(bf16[4,576,128]{2,1,0:T(8,128)(2,1)} %get-tuple-element.20.own) | copy-start | bytes 1769476
  24.6 8.7 %collective-permute-start.3 = (bf16[576,128]{1,0:T(8,128)(2,1)S(1)}, bf16[576,128]{1,0:T(8,128)(2,1)S(1)}, u32[]{:S(2)}, u32[]{:S(2)}) collective-permute-start(bf16[576,128]{1,0:T(8,128)(2,1)S(1)} %get-tuple-element.32), channel_id=1, source_target_pairs={{0,192},{64,0},{128,64},{192,128},{1,193},{65,1},{129,65},{193,129... | collective-permute-start | bytes 442376 | tf_op jit(solution)/shard_map/ppermute | solution.py:500
  27.4 6.3 %collective-permute-start.2 = (bf16[576,128]{1,0:T(8,128)(2,1)S(1)}, bf16[576,128]{1,0:T(8,128)(2,1)S(1)}, u32[]{:S(2)}, u32[]{:S(2)}) collective-permute-start(bf16[576,128]{1,0:T(8,128)(2,1)S(1)} %get-tuple-element.33), channel_id=1, source_target_pairs={{0,128},{64,192},{128,0},{192,64},{1,129},{65,193},{129,1},{193,65... | collective-permute-start | bytes 442376 | tf_op jit(solution)/shard_map/ppermute | solution.py:500
  27.7 10.1 %collective-permute-start.1 = (bf16[576,128]{1,0:T(8,128)(2,1)S(1)}, bf16[576,128]{1,0:T(8,128)(2,1)S(1)}, u32[]{:S(2)}, u32[]{:S(2)}) collective-permute-start(bf16[576,128]{1,0:T(8,128)(2,1)S(1)} %get-tuple-element.34), channel_id=1, source_target_pairs={{0,64},{64,128},{128,192},{192,0},{1,65},{65,129},{129,193},{193,1... | collective-permute-start | bytes 442376 | tf_op jit(solution)/shard_map/ppermute | solution.py:500
  37.9 38.6 %copy-start.5 = (s32[3]{0:T(128)S(1)}, s32[3]{0:T(128)}, u32[]{:S(2)}) copy-start(s32[3]{0:T(128)} %copy-done.4) | copy-start | bytes 40
  96.2 14.7 %copy-start.1 = (bf16[736,128]{1,0:T(8,128)(2,1)}, bf16[736,128]{1,0:T(8,128)(2,1)S(1)}, u32[]{:S(2)}) copy-start(bf16[736,128]{1,0:T(8,128)(2,1)S(1)} %shard_map.167.b0) | copy-start | bytes 565252
  96.2 5.9 %collective-permute-start.6 = (bf16[736,128]{1,0:T(8,128)(2,1)S(1)}, bf16[736,128]{1,0:T(8,128)(2,1)S(1)}, u32[]{:S(2)}, u32[]{:S(2)}) collective-permute-start(bf16[736,128]{1,0:T(8,128)(2,1)S(1)} %shard_map.167.b0), channel_id=1, source_target_pairs={{0,192},{64,0},{128,64},{192,128},{1,193},{65,1},{129,65},{193,129... | collective-permute-start | bytes 565256 | tf_op jit(solution)/shard_map/ppermute | solution.py:500
  97.2 8.3 %collective-permute-start.5 = (bf16[736,128]{1,0:T(8,128)(2,1)S(1)}, bf16[736,128]{1,0:T(8,128)(2,1)S(1)}, u32[]{:S(2)}, u32[]{:S(2)}) collective-permute-start(bf16[736,128]{1,0:T(8,128)(2,1)S(1)} %shard_map.167.b0), channel_id=1, source_target_pairs={{0,128},{64,192},{128,0},{192,64},{1,129},{65,193},{129,1},{193,65... | collective-permute-start | bytes 565256 | tf_op jit(solution)/shard_map/ppermute | solution.py:500
  98.4 9.6 %collective-permute-start.4 = (bf16[736,128]{1,0:T(8,128)(2,1)S(1)}, bf16[736,128]{1,0:T(8,128)(2,1)S(1)}, u32[]{:S(2)}, u32[]{:S(2)}) collective-permute-start(bf16[736,128]{1,0:T(8,128)(2,1)S(1)} %shard_map.167.b0), channel_id=1, source_target_pairs={{0,64},{64,128},{128,192},{192,0},{1,65},{65,129},{129,193},{193,1... | collective-permute-start | bytes 565256 | tf_op jit(solution)/shard_map/ppermute | solution.py:500
  98.4 11.5 %collective-permute-start.7 = (bf16[736,128]{1,0:T(8,128)(2,1)S(1)}, bf16[736,128]{1,0:T(8,128)(2,1)S(1)}, u32[]{:S(2)}, u32[]{:S(2)}) collective-permute-start(bf16[736,128]{1,0:T(8,128)(2,1)S(1)} %shard_map.167.b0), channel_id=1, source_target_pairs={{0,32},{32,0},{1,33},{33,1},{2,34},{34,2},{3,35},{35,3},{4,36},{36... | collective-permute-start | bytes 565256 | tf_op jit(solution)/shard_map/ppermute | solution.py:504
  102.1 8.9 %copy-start.6 = (bf16[736,128]{1,0:T(8,128)(2,1)}, bf16[736,128]{1,0:T(8,128)(2,1)S(1)}, u32[]{:S(2)}) copy-start(bf16[736,128]{1,0:T(8,128)(2,1)S(1)} %collective-permute-done.6.b3) | copy-start | bytes 565252
  102.1 7.8 %collective-permute-start.10 = (bf16[736,128]{1,0:T(8,128)(2,1)S(1)}, bf16[736,128]{1,0:T(8,128)(2,1)S(1)}, u32[]{:S(2)}, u32[]{:S(2)}) collective-permute-start(bf16[736,128]{1,0:T(8,128)(2,1)S(1)} %collective-permute-done.6.b3), channel_id=1, source_target_pairs={{0,32},{32,0},{1,33},{33,1},{2,34},{34,2},{3,35},{35,3},{4,36},{36... | collective-permute-start | bytes 565256 | tf_op jit(solution)/shard_map/ppermute | solution.py:504
  105.5 5.5 %copy-start.7 = (bf16[736,128]{1,0:T(8,128)(2,1)}, bf16[736,128]{1,0:T(8,128)(2,1)S(1)}, u32[]{:S(2)}) copy-start(bf16[736,128]{1,0:T(8,128)(2,1)S(1)} %collective-permute-done.5.b2) | copy-start | bytes 565252
  105.5 4.4 %collective-permute-start.9 = (bf16[736,128]{1,0:T(8,128)(2,1)S(1)}, bf16[736,128]{1,0:T(8,128)(2,1)S(1)}, u32[]{:S(2)}, u32[]{:S(2)}) collective-permute-start(bf16[736,128]{1,0:T(8,128)(2,1)S(1)} %collective-permute-done.5.b2), channel_id=1, source_target_pairs={{0,32},{32,0},{1,33},{33,1},{2,34},{34,2},{3,35},{35,3},{4,36},{36... | collective-permute-start | bytes 565256 | tf_op jit(solution)/shard_map/ppermute | solution.py:504
  107.9 3.0 %copy-start.8 = (bf16[736,128]{1,0:T(8,128)(2,1)}, bf16[736,128]{1,0:T(8,128)(2,1)S(1)}, u32[]{:S(2)}) copy-start(bf16[736,128]{1,0:T(8,128)(2,1)S(1)} %collective-permute-done.4.b1) | copy-start | bytes 565252
  108.0 3.0 %collective-permute-start.8 = (bf16[736,128]{1,0:T(8,128)(2,1)S(1)}, bf16[736,128]{1,0:T(8,128)(2,1)S(1)}, u32[]{:S(2)}, u32[]{:S(2)}) collective-permute-start(bf16[736,128]{1,0:T(8,128)(2,1)S(1)} %collective-permute-done.4.b1), channel_id=1, source_target_pairs={{0,32},{32,0},{1,33},{33,1},{2,34},{34,2},{3,35},{35,3},{4,36},{36... | collective-permute-start | bytes 565256 | tf_op jit(solution)/shard_map/ppermute | solution.py:504
  109.9 1.1 copy-start.9
  109.9 1.1 copy-start.10
  109.9 1.1 copy-start.11
  111.0 0.7 copy-start.12

commit v3 on v2

--- a/solution.py
+++ b/solution.py
@@ -21,12 +21,15 @@
 BF16 = jnp.bfloat16
 SHARD = ("z", "x")
 VMEM = pl.BlockSpec(memory_space=pltpu.VMEM)
-SMEM = pl.BlockSpec(memory_space=pltpu.SMEM)
+HBM = pl.BlockSpec(memory_space=pltpu.HBM)
 ANY = pl.BlockSpec(memory_space=pl.ANY)
 GROUPS = 4
 PER = SHARDS // GROUPS
 
 
+LIGHT = pl.CostEstimate(flops=1, bytes_accessed=1, transcendentals=0)
+
+
 def params(mib):
     return pltpu.CompilerParams(vmem_limit_bytes=mib * 2**20)
 
@@ -41,6 +44,10 @@
 
 def has_ninth(shard):
     return offset(shard) > 8 * LANES - GU_COLS
+
+
+def places():
+    return lax.axis_index("y"), lax.axis_index("core"), lax.axis_index("z") * 4 + lax.axis_index("x")
 
 
 def lane_ids():
@@ -59,8 +66,8 @@
 BLOCK = GU_ROWS + DN_TILES * 8
 
 
-def lower_kernel(pos, gs, gf, ge, ds, df, de, own, oth, gsv, gfv, gev, dsv, dfv, dev, sems):
-    y, core = pos[0], pos[1]
+def lower_kernel(gs, gf, ge, ds, df, de, own, oth, gsv, gfv, gev, dsv, dfv, dev, sems):
+    y, core, _ = places()
     bounds = group_bounds()
     copies = []
     for g in range(GROUPS):
@@ -117,12 +124,12 @@
             oth[slots[yy], at] = jnp.where(first, two, one).astype(BF16)
 
 
-def lower(pos, gs, gf, ge, ds, df, de):
+def lower(gs, gf, ge, ds, df, de):
     shape = jax.ShapeDtypeStruct((4, BLOCK, LANES), BF16)
     return pl.pallas_call(
         lower_kernel,
         out_shape=(shape, shape),
-        in_specs=[SMEM] + [ANY] * 6,
+        in_specs=[HBM] * 6,
         out_specs=(VMEM, VMEM),
         scratch_shapes=[
             pltpu.VMEM((2, 8, FF), F32),
@@ -133,16 +140,26 @@
             pltpu.VMEM((8, D), BF16),
             pltpu.SemaphoreType.DMA((GROUPS, 6)),
         ],
-        compiler_params=params(56),
-    )(pos, gs, gf, ge, ds, df, de)
+        compiler_params=params(59),
+        cost_estimate=LIGHT,
+    )(gs, gf, ge, ds, df, de)
 
 
 B_ROWS = LANES + 16
 
 
-def basis_kernel(pos, gu, dn_t, out, rows, dn_rows):
-    rep, shard = 2 * pos[0] + pos[1], pos[2]
+def basis_kernel(gu_any, dn_any, out, rows, dn_rows, gu, dn_t, sems):
+    y, core, shard = places()
+    rep = 2 * y + core
     start = LANES - offset(shard)
+    copies = [
+        pltpu.make_async_copy(gu_any, gu, sems.at[0]),
+        pltpu.make_async_copy(dn_any, dn_t, sems.at[1]),
+    ]
+    for copy in copies:
+        copy.start()
+    for copy in copies:
+        copy.wait()
     rows[0:LANES, :] = jnp.zeros((LANES, LANES), F32)
     rows[LANES : LANES + GU_COLS, :] = gu[...].astype(F32)
     rows[LANES + GU_COLS :, :] = jnp.zeros((rows.shape[0] - LANES - GU_COLS, LANES), F32)
@@ -153,38 +170,96 @@
     dn = dn_rows[pl.ds(pl.multiple_of(32 * rep, 32), 32), :]
     dn = jnp.concatenate([dn[0:16], dn[16:32]], axis=1)
     block = jnp.concatenate([tile, dn], axis=0).astype(BF16)
-    for s in range(SHARDS):
-        out[s] = block
-
-
-def basis_tiles(pos, gu, dn_t):
+    for z in range(8):
+        out[z] = block
+
+
+def basis_tiles(gu, dn_t):
     return pl.pallas_call(
         basis_kernel,
-        out_shape=jax.ShapeDtypeStruct((SHARDS, B_ROWS, LANES), BF16),
-        in_specs=[SMEM, VMEM, VMEM],
+        out_shape=jax.ShapeDtypeStruct((8, B_ROWS, LANES), BF16),
+        in_specs=[HBM, HBM],
         out_specs=VMEM,
-        scratch_shapes=[pltpu.VMEM((1280, LANES), F32), pltpu.VMEM((DN_COLS, RANK), F32)],
+        scratch_shapes=[
+            pltpu.VMEM((1280, LANES), F32),
+            pltpu.VMEM((DN_COLS, RANK), F32),
+            pltpu.VMEM((GU_COLS, LANES), BF16),
+            pltpu.VMEM((RANK, DN_COLS), BF16),
+            pltpu.SemaphoreType.DMA((2,)),
+        ],
+        compiler_params=params(59),
+    )(gu, dn_t)
+
+
+def pair_kernel(own, came, zero, one, two, three, own_v, came_v, sems):
+    order = (2, 1, 3, 0)
+    copies = []
+    for k in order:
+        row = []
+        for i, (src, dst) in enumerate(((own, own_v), (came, came_v))):
+            row.append(pltpu.make_async_copy(src.at[k], dst.at[k], sems.at[k, i]))
+            row[-1].start()
+        copies.append(row)
+    outs = (zero, one, two, three)
+    for k, row in zip(order, copies):
+        for copy in row:
+            copy.wait()
+        for at in range(0, BLOCK, 64):
+            rows = slice(at, at + 64)
+            total = own_v[k, rows].astype(F32) + came_v[k, rows].astype(F32)
+            outs[k][rows] = total.astype(outs[k].dtype)
+
+
+def pair_sums(own, came):
+    block = (BLOCK, LANES)
+    return pl.pallas_call(
+        pair_kernel,
+        out_shape=(
+            jax.ShapeDtypeStruct(block, F32),
+            *[jax.ShapeDtypeStruct(block, BF16)] * 3,
+        ),
+        in_specs=[ANY] * 2,
+        out_specs=(VMEM,) * 4,
+        scratch_shapes=[
+            pltpu.VMEM((4, BLOCK, LANES), BF16),
+            pltpu.VMEM((4, BLOCK, LANES), BF16),
+            pltpu.SemaphoreType.DMA((4, 2)),
+        ],
         compiler_params=params(16),
-    )(pos, gu, dn_t)
-
-
-def y_sum_kernel(own, came, one, two, three, out):
+        cost_estimate=LIGHT,
+    )(own, came)
+
+
+X_ROWS = 8 * 16 + DN_TILES * 8
+
+
+def y_sum_kernel(zero, one, two, three, out, x0, x1, x2, x3):
     for at in range(0, BLOCK, 64):
         rows = slice(at, at + 64)
-        total = own[0, rows].astype(F32) + came[0, rows].astype(F32)
+        total = zero[rows]
         for ref in (one, two, three):
             total = total + ref[rows].astype(F32)
         out[rows] = total.astype(BF16)
-
-
-def y_sum(own, came, comes):
+    x = lax.axis_index("x")
+    for k, ref in enumerate((x0, x1, x2, x3)):
+        to_x = lax.rem(x + k, 4)
+        for z in range(8):
+            at = pl.multiple_of(16 * (4 * z + to_x), 16)
+            ref[16 * z : 16 * z + 16, :] = out[pl.ds(at, 16), :]
+        ref[8 * 16 :, :] = out[GU_ROWS:BLOCK, :]
+
+
+def y_sum(zero, comes):
     return pl.pallas_call(
         y_sum_kernel,
-        out_shape=jax.ShapeDtypeStruct((BLOCK, LANES), BF16),
-        in_specs=[VMEM] * 5,
-        out_specs=VMEM,
+        out_shape=(
+            jax.ShapeDtypeStruct((BLOCK, LANES), BF16),
+            *[jax.ShapeDtypeStruct((X_ROWS, LANES), BF16)] * 4,
+        ),
+        in_specs=[VMEM] * 4,
+        out_specs=(VMEM,) * 5,
         compiler_params=params(16),
-    )(own, came, comes[1], comes[2], comes[3])
+    )(zero, comes[1], comes[2], comes[3])
 
 
 def split_hi_lo(value):
@@ -192,43 +267,62 @@
     return jnp.concatenate([hi, value - hi], axis=-1).astype(BF16)
 
 
-def p_part_kernel(lbar, basis, out):
-    gu = jnp.zeros((16, LANES), F32)
-    for s in range(0, SHARDS, 2):
-        left = jnp.concatenate(
-            [lbar[16 * s : 16 * s + 16, :], lbar[16 * s + 16 : 16 * s + 32, :]], axis=1
+def p_part_kernel(l0, l1, l2, l3, basis, out, dn_rows):
+    x = lax.axis_index("x")
+    lefts = (l0, l1, l2, l3)
+    gu = jnp.zeros((64, LANES), F32)
+    for z in range(0, 8, 2):
+        left = [
+            jnp.concatenate([ref[16 * i : 16 * i + 16, :] for ref in lefts], axis=0)
+            for i in (z, z + 1)
+        ]
+        right = basis[z : z + 2, 0:LANES, :].reshape(2 * LANES, LANES)
+        gu = gu + jnp.dot(jnp.concatenate(left, axis=1), right, preferred_element_type=F32)
+    dn_rows[...] = jnp.zeros_like(dn_rows)
+    right = basis[:, LANES:B_ROWS, :].astype(F32)
+    right = jnp.concatenate([right[:, :, 0:RANK], right[:, :, RANK:LANES]], axis=1)
+    dn_rows[:, pl.ds(pl.multiple_of(32 * x, 32), 32), :] = right
+    tiles = [ref[8 * 16 :, :].astype(F32) for ref in lefts]
+    dn = jnp.zeros((32, RANK), F32)
+    for q in range(DN_TILES):
+        left = jnp.concatenate([tile[8 * q : 8 * q + 8] for tile in tiles], axis=0)
+        dn = dn + jnp.dot(
+            left.astype(BF16), dn_rows[q].astype(BF16), preferred_element_type=F32
         )
-        right = basis[s : s + 2, 0:LANES, :].reshape(2 * LANES, LANES)
-        gu = gu + jnp.dot(left, right, preferred_element_type=F32)
-    tiles = lbar[GU_ROWS:BLOCK, :].astype(F32)
-    dn = jnp.zeros((8, RANK), F32)
-    for q in range(DN_TILES):
-        right = basis[4 * q : 4 * q + 4, LANES:B_ROWS, :].astype(F32)
-        right = jnp.concatenate([right[:, :, 0:RANK], right[:, :, RANK:LANES]], axis=1)
-        dn = dn + jnp.dot(
-            tiles[8 * q : 8 * q + 8].astype(BF16),
-            right.reshape(LANES, RANK).astype(BF16),
-            preferred_element_type=F32,
+    for k in range(4):
+        part = jnp.concatenate(
+            [
+                gu[16 * k : 16 * k + 8, 0:RANK],
+                gu[16 * k + 8 : 16 * k + 16, RANK:LANES],
+                dn[8 * k : 8 * k + 8],
+            ],
+            axis=0,
         )
-    part = jnp.concatenate([gu[0:8, 0:RANK], gu[8:16, RANK:LANES], dn], axis=0)
-    block = split_hi_lo(part)
-    for rep in range(REPS):
-        out[rep] = block
-
-
-def p_part(lbar, basis):
+        block = split_hi_lo(part)
+        to_x = lax.rem(x - k + 4, 4)
+        for rep in range(REPS):
+            out[4 * rep + to_x] = block
+
+
+def p_part(rows, basis):
     return pl.pallas_call(
         p_part_kernel,
-        out_shape=jax.ShapeDtypeStruct((REPS, 24, LANES), BF16),
-        in_specs=[VMEM, VMEM],
+        out_shape=jax.ShapeDtypeStruct((4 * REPS, 24, LANES), BF16),
+        in_specs=[VMEM] * 5,
         out_specs=VMEM,
+        scratch_shapes=[pltpu.VMEM((DN_TILES, LANES, RANK), F32)],
         compiler_params=params(16),
-    )(lbar, basis)
+    )(*rows, basis)
 
 
 def p_sum_kernel(ps, lbar, out):
     total = jnp.sum(ps[...].astype(F32), axis=0)
-    rows = split_hi_lo(total[:, 0:RANK] + total[:, RANK:LANES]).astype(F32)
+    rows = total[:, 0:RANK] + total[:, RANK:LANES]
+    rows = jnp.concatenate(
+        [jnp.concatenate([rows[0:8], rows[8:16]], axis=1),
+         jnp.concatenate([rows[16:24], jnp.zeros((8, RANK), F32)], axis=1)],
+        axis=0,
+    )
     tiles = lbar[GU_ROWS:BLOCK, :].astype(F32)
     for s in range(SHARDS):
         gu = lbar[16 * s : 16 * s + 16, :].astype(F32)
@@ -239,7 +333,7 @@
 def p_sum(ps, lbar):
     return pl.pallas_call(
         p_sum_kernel,
-        out_shape=jax.ShapeDtypeStruct((SHARDS, 48, LANES), BF16),
+        out_shape=jax.ShapeDtypeStruct((SHARDS, 40, LANES), BF16),
         in_specs=[VMEM, VMEM],
         out_specs=VMEM,
         compiler_params=params(16),
@@ -298,14 +392,15 @@
     )
 
 
-def factor_kernel(pos, recv, a_out, q_out, q_rows):
+def factor_kernel(recv, a_out, q_out, q_rows):
     block = recv[...].astype(F32)
     columns = [
         block[:, 8 * m : 8 * m + 8, :].reshape(256, LANES).astype(BF16) for m in range(3)
     ]
-    left = block[:, 24:48, :]
-    left = left[:, :, 0:RANK] + left[:, :, RANK:LANES]
-    lefts = [left[:, 8 * m : 8 * m + 8, :].reshape(256, RANK) for m in range(3)]
+    lefts = [
+        block[:, 24:32, 0:RANK], block[:, 24:32, RANK:LANES], block[:, 32:40, 0:RANK]
+    ]
+    lefts = [left.reshape(256, RANK) for left in lefts]
     grams = [exact_dot(p, p, ((0,), (0,))) for p in lefts]
     inverses = inverse_factors(grams)
     hs = [exact_dot(p, v, ((1,), (1,))).astype(BF16) for p, v in zip(lefts, inverses)]
@@ -318,24 +413,24 @@
         recons.append(recon.reshape(SHARDS, 8, LANES))
     a_out[...] = jnp.concatenate(recons, axis=1).astype(BF16)
     q_rows[...] = qs[2]
-    dn = q_rows[pl.ds(pl.multiple_of(32 * lax.rem(pos[2], 4), 32), 32), :]
+    dn = q_rows[pl.ds(pl.multiple_of(32 * lax.axis_index("x"), 32), 32), :]
     dn = jnp.concatenate([dn, jnp.zeros_like(dn)], axis=1)
     gu = jnp.concatenate(qs[:2], axis=1)
     q_out[...] = jnp.concatenate([gu, dn], axis=0).astype(BF16)
 
 
-def factor(pos, recv):
+def factor(recv):
     return pl.pallas_call(
         factor_kernel,
         out_shape=(
             jax.ShapeDtypeStruct((SHARDS, 24, LANES), BF16),
             jax.ShapeDtypeStruct((Q_ROWS, LANES), BF16),
         ),
-        in_specs=[SMEM, VMEM],
+        in_specs=[VMEM],
         out_specs=(VMEM, VMEM),
         scratch_shapes=[pltpu.VMEM((LANES, RANK), F32)],
         compiler_params=params(32),
-    )(pos, recv)
+    )(recv)
 
 
 Q_ROWS = LANES + 32
@@ -363,42 +458,15 @@
 
 
 def finish_kernel(
-    pos, b0, b1, b2, b3, b4, b5, b6, b7, gs, gf, ge, gm, ds, df, de, dm,
+    b0, b1, b2, b3, b4, b5, b6, b7, gs, gc, gm, ds, dc, dm,
     gs_o, ge_o, gm_o, ds_o, de_o, dm_o, gb_o, db_o,
-    gs_v, ge_v, gm_v, ds_v, de_v, dm_v, stage, q_full, q_dn,
-    gs_i, gf_i, ge_i, gm_i, ds_i, df_i, de_i, dm_i, sems, sems_in,
+    gs_v, ge_v, gm_v, ds_v, de_v, dm_v, stage, q_full, q_dn, sems,
 ):
-    arrivals = []
-
-    def bring(pairs, at):
-        row = []
-        for i, (src, dst) in enumerate(pairs):
-            row.append(
-                pltpu.make_async_copy(src.at[at], dst.at[at], sems_in.at[len(arrivals), i])
-            )
-            row[-1].start()
-        arrivals.append(row)
-
     bounds = [first_tile(PER * g) * LANES for g in range(GROUPS + 1)]
-    for g in range(GROUPS):
-        bring(
-            ((gs, gs_i), (gf, gf_i), (ge, ge_i), (gm, gm_i)),
-            (slice(None), slice(None), pl.ds(bounds[g], bounds[g + 1] - bounds[g])),
-        )
-    bring(((ds, ds_i), (df, df_i), (de, de_i), (dm, dm_i)), (slice(None), slice(None)))
-    y, core, mine = pos[0], pos[1], pos[2]
+    y, core, mine = places()
     for i, block in enumerate((b0, b1, b2, b3, b4, b5, b6, b7)):
         rep = 2 * lax.rem(y - i % 4 + 4, 4) + (core if i < 4 else 1 - core)
         stage[rep] = block[...]
-
-    def outer(slow, fast, error, moment, recon):
-        combined = slow - fast.astype(F32) + error.astype(F32)
-        moment_next = 0.9 * moment + recon
-        return (
-            slow - 0.7 * (recon + 0.9 * moment_next),
-            (combined - recon).astype(BF16),
-            moment_next,
-        )
 
     copies = []
 
@@ -413,8 +481,6 @@
         return stage[rep, 16 * shard : 16 * shard + 16, :].astype(F32).reshape(2, 8, LANES)
 
     for g in range(GROUPS):
-        for copy in arrivals[g]:
-            copy.wait()
         for shard in range(PER * g, PER * (g + 1)):
             for j in range(first_tile(shard + 1) - first_tile(shard)):
                 recon = gu_recon(j, shard)
@@ -422,15 +488,13 @@
                     other = gu_recon(0 if has_ninth(shard - 1) else 7, shard - 1)
                     recon = jnp.where(lane[None] < offset(shard), other, recon)
                 at = (slice(None), slice(None), pl.ds((first_tile(shard) + j) * LANES, LANES))
-                gs_v[at], ge_v[at], gm_v[at] = outer(
-                    gs_i[at], gf_i[at], ge_i[at], gm_i[at], recon
-                )
+                gs_v[at] = gs[at] - SLOW_GAIN * recon
+                ge_v[at] = (gc[at] - recon).astype(BF16)
+                gm_v[at] = gm[at] + recon
         send(
             ((gs_v, gs_o), (ge_v, ge_o), (gm_v, gm_o)),
             (slice(None), slice(None), pl.ds(bounds[g], bounds[g + 1] - bounds[g])),
         )
-    for copy in arrivals[GROUPS]:
-        copy.wait()
     tiles = [stage[r, GU_ROWS:BLOCK, :].astype(F32) for r in range(REPS)]
     for shard in range(SHARDS):
         q, a = shard // 4, shard % 4
@@ -442,7 +506,9 @@
                     piece = pltpu.roll(piece, 32 * (k - a) % LANES, 1)
                 recon = piece if k == 0 else jnp.where(lane < 32 * k, recon, piece)
             at = (slice(None), pl.ds(DN_COLS * shard + LANES * half, LANES))
-            ds_v[at], de_v[at], dm_v[at] = outer(ds_i[at], df_i[at], de_i[at], dm_i[at], recon)
+            ds_v[at] = ds[at] - SLOW_GAIN * recon
+            de_v[at] = (dc[at] - recon).astype(BF16)
+            dm_v[at] = dm[at] + recon
     send(((ds_v, ds_o), (de_v, de_o), (dm_v, dm_o)), (slice(None), slice(None)))
 
     for r in range(REPS):
@@ -457,43 +523,38 @@
         copy.wait()
 
 
-def finish(pos, blocks, gs, gf, ge, gm, ds, df, de, dm):
-    def like(a):
-        return jax.ShapeDtypeStruct(a.shape, a.dtype)
-
+def finish(blocks, parts, dn_parts):
     gu, dn = (2, 8, FF), (8, D)
+    kinds = (F32, BF16, F32)
     return pl.pallas_call(
         finish_kernel,
         out_shape=(
-            like(gs), like(ge), like(gm), like(ds), like(de), like(dm),
+            *[jax.ShapeDtypeStruct(gu, kind) for kind in kinds],
+            *[jax.ShapeDtypeStruct(dn, kind) for kind in kinds],
             jax.ShapeDtypeStruct((GU_COLS, LANES), BF16),
             jax.ShapeDtypeStruct((RANK, DN_COLS), BF16),
         ),
-        in_specs=[SMEM] + [VMEM] * 8 + [ANY] * 8,
+        in_specs=[VMEM] * 14,
         out_specs=(ANY,) * 6 + (VMEM, VMEM),
         scratch_shapes=[
-            pltpu.VMEM(gu, F32),
-            pltpu.VMEM(gu, BF16),
-            pltpu.VMEM(gu, F32),
-            pltpu.VMEM(dn, F32),
-            pltpu.VMEM(dn, BF16),
-            pltpu.VMEM(dn, F32),
+            *[pltpu.VMEM(gu, kind) for kind in kinds],
+            *[pltpu.VMEM(dn, kind) for kind in kinds],
             pltpu.VMEM((REPS, PAYLOAD, LANES), BF16),
             pltpu.VMEM((9 * LANES, LANES), F32),
             pltpu.VMEM((DN_COLS, RANK), F32),
-            pltpu.VMEM(gu, F32),
-            pltpu.VMEM(gu, BF16),
-            pltpu.VMEM(gu, BF16),
-            pltpu.VMEM(gu, F32),
-            pltpu.VMEM(dn, F32),
-            pltpu.VMEM(dn, BF16),
-            pltpu.VMEM(dn, BF16),
-            pltpu.VMEM(dn, F32),
             pltpu.SemaphoreType.DMA((3 * (GROUPS + 1),)),
-            pltpu.SemaphoreType.DMA((GROUPS + 1, 4)),
         ],
-        compiler_params=params(56),
-    )(pos, *blocks, gs, gf, ge, gm, ds, df, de, dm)
+        compiler_params=params(32),
+    )(*blocks, *parts, *dn_parts)
+
+
+MOMENT_GAIN = 0.7 * 0.9 * 0.9
+SLOW_GAIN = 0.7 * 1.9
+
+
+def settled(slow, fast, error, moment):
+    combined = slow - fast.astype(F32) + error.astype(F32)
+    return slow - MOMENT_GAIN * moment, combined, 0.9 * moment
 
 
 def shift(value, axis, size, by):
@@ -511,20 +572,19 @@
 def on_device(
     gu_slow, gu_fast, gu_error, gu_moment, gu_basis, dn_slow, dn_fast, dn_error, dn_moment, dn_basis
 ):
-    pos = jnp.stack([lax.axis_index("y"), lax.axis_index("core"), lax.axis_index(SHARD)])
-    pos = pos.astype(jnp.int32)
     gu_fast, gu_error = gu_fast[0], gu_error[0]
     dn_fast, dn_error = dn_fast[0], dn_error[0]
-    basis = exchange(basis_tiles(pos, gu_basis, dn_basis.T), SHARD)
-    own, oth = lower(pos, gu_slow, gu_fast, gu_error, dn_slow, dn_fast, dn_error)
+    basis = exchange(basis_tiles(gu_basis, dn_basis.T), "z")
+    own, oth = lower(gu_slow, gu_fast, gu_error, dn_slow, dn_fast, dn_error)
     came = swap(oth)
-    pair = own.astype(F32) + came.astype(F32)
-    sends = {by: pair[by].astype(BF16) for by in (2, 1, 3)}
-    comes = {by: shift(sends[by], "y", 4, by) for by in (2, 1, 3)}
-    lbar = y_sum(own, came, comes)
-    parts = exchange(p_part(lbar, basis), ("y", "core"))
+    zero, *sends = pair_sums(own, came)
+    comes = {by: shift(sends[by - 1], "y", 4, by) for by in (2, 1, 3)}
+    lbar, *rows = y_sum(zero, comes)
+    for by in (2, 1, 3):
+        rows[by] = shift(rows[by], "x", 4, by)
+    parts = exchange(p_part(rows, basis), ("y", "core", "x"))
     recv = exchange(p_sum(parts, lbar), SHARD)
-    a_blocks, q_block = factor(pos, recv)
+    a_blocks, q_block = factor(recv)
     payload = pack(exchange(a_blocks, SHARD), q_block)
     mine = {0: payload}
     for by in (2, 1, 3):
@@ -532,7 +592,9 @@
     blocks = [mine[by] for by in range(4)]
     blocks = blocks + [swap(b) for b in blocks]
     gs, ge, gm, ds, de, dm, gb, db = finish(
-        pos, blocks, gu_slow, gu_fast, gu_error, gu_moment, dn_slow, dn_fast, dn_error, dn_moment
+        blocks,
+        settled(gu_slow, gu_fast, gu_error, gu_moment),
+        settled(dn_slow, dn_fast, dn_error, dn_moment),
     )
     return gs, ge[None], gm, gb, ds, de[None], dm, db.T
 

time: 120 us -> 111 us (0.925)
  waiting for transfers between devices: 19 us -> 9.31 us
  blocking collectives: 45.8 us -> 50.5 us
  Pallas kernels: 19.4 us -> 15.4 us
  local copies, waits for them, and re-layouts: 2.43 us -> 1.09 us
    all_to_all x1, waiting for transfers between devices: 6.75 us -> 0.01 us  [exchange(): return lax.all_to_all(value, axis, 0, 0, tiled=False)]
    ppermute x6 -> x9, starting transfers between devices: 6 us -> 12.2 us  [shift(): lax.ppermute(value, axis, [(i, (i + by) % size) for i in range(size)])]
    all_to_all x1, starting transfers between devices: 11.9 us -> 6.46 us  [exchange(): return lax.all_to_all(value, axis, 0, 0, tiled=False)]
    all_to_all x3, blocking collectives: 45.8 us -> 50.5 us  [exchange(): return lax.all_to_all(value, axis, 0, 0, tiled=False)]
    pallas_call x6 -> x7, Pallas kernels: 14.3 us -> 11.5 us  [the longest x1 3.64 us: lower(): pl.pallas_call(lower_kernel, out_shape=(shape, shape), in_specs=[HBM] * 6...]
    mul x0 -> x2, other arithmetic: none -> 2.27 us  [settled(): return (slow - MOMENT_GAIN * moment, combined, 0.9 * moment)]
    ppermute x5, waiting for transfers between devices: 2.87 us -> 0.94 us  [swap(): return lax.ppermute(value, 'core', [(0, 1), (1, 0)])]
    another operation x2 -> x0, other arithmetic: 1.37 us -> none
  transfers between devices with their start and end apart: 12 -> 15, of which waited for: 6 -> 5; matrix products, arithmetic and copies ran while one was open for 1% -> 2% of each run, Pallas kernels for 4% -> 3%
where the time goes in v3:
time: 111 us
  blocking collectives  50.5 us (45%)
  starting transfers between devices  31.2 us (28%)
  Pallas kernels  15.4 us (14%)
  waiting for transfers between devices  9.31 us (8%)
  other arithmetic  2.27 us (2%)
    all_to_all x3, blocking collectives, exchange(): return lax.all_to_all(value, axis, 0, 0, tiled=False)  50.5 us
    ppermute x5, starting transfers between devices, swap(): return lax.ppermute(value, 'core', [(0, 1), (1, 0)])  12.5 us
    ppermute x9, starting transfers between devices, shift(): lax.ppermute(value, axis, [(i, (i + by) % size) for i in range(size)])  12.2 us
    ppermute x9, waiting for transfers between devices, shift(): lax.ppermute(value, axis, [(i, (i + by) % size) for i in range(size)])  8.36 us
    all_to_all x1, starting transfers between devices, exchange(): return lax.all_to_all(value, axis, 0, 0, tiled=False)  6.46 us
    pallas_call x1, Pallas kernels, factor(): pl.pallas_call(factor_kernel, out_shape=(jax.ShapeDtypeStruct((SHARDS, 24...  3.93 us
    pallas_call x1, Pallas kernels, lower(): pl.pallas_call(lower_kernel, out_shape=(shape, shape), in_specs=[HBM] * 6...  3.64 us
    pallas_call x1, Pallas kernels, finish(): pl.pallas_call(finish_kernel, out_shape=(*[jax.ShapeDtypeStruct(gu, kind)...  3.62 us
  transfers between devices with their start and end apart: 15, of which 5 were waited for; matrix products, arithmetic and copies ran while one was open for 2% of the time, Pallas kernels for 3%

profile of v3, /device:TPU:1, one launch (start us, length us, event | category | flops | bytes accessed | tf_op | source)
XLA Modules:
  0.0 110.7 jit_solution(9098947865558374278)
XLA Ops:
  0.6 3.6 %shard_map.161 = (bf16[4,576,128]{2,1,0:T(8,128)(2,1)}, bf16[4,576,128]{2,1,0:T(8,128)(2,1)}) custom-call(f32[2,8,29568]{2,1,0:T(8,128)} %gs.1, bf16[2,8,29568]{2,1,0:T(8,128)(2,1)} %bitcast.12, bf16[2,8,29568]{2,1,0:T(8,128)(2,1)} %bitcast.13, f32[8,8192]{1,0:T(8,128)} %ds.1, bf16[8,8192]{1,0:T(8,128)(2,1)} %bitcast.14, bf16[8,8192]{1,0:T(8,128)(2,1)} %bitcast.15), custom_call_target="tpu_custom_call" | custom-call | flops 1 | bytes 1 | tf_op jit(solution)/shard_map/pallas_call | solution.py:129
  4.3 3.3 %collective-permute-start = (bf16[4,576,128]{2,1,0:T(8,128)(2,1)}, bf16[4,576,128]{2,1,0:T(8,128)(2,1)S(1)}, u32[]{:S(2)}, u32[]{:S(2)}) collective-permute-start(bf16[4,576,128]{2,1,0:T(8,128)(2,1)} %get-tuple-element.30), channel_id=1, source_target_pairs={{0,32},{32,0},{1,33},{33,1},{2,34},{34,2},{3,35},{35,3},{4,36},{36... | collective-permute-start | bytes 1769480 | tf_op jit(solution)/shard_map/ppermute | solution.py:565
  7.6 1.9 %shard_map.164 = bf16[8,144,128]{2,1,0:T(8,128)(2,1)} custom-call(bf16[924,128]{1,0:T(8,128)(2,1)} %gu_any.1, bf16[64,256]{1,0:T(8,128)(2,1)} %bitcast.16), custom_call_target="tpu_custom_call" | custom-call | tf_op jit(solution)/shard_map/pallas_call | solution.py:178
  9.5 6.5 %all-to-all-start = ((bf16[8,144,128]{2,1,0:T(8,128)(2,1)}), bf16[8,144,128]{2,1,0:T(8,128)(2,1)S(1)}, u32[]{:S(2)}, u32[]{:S(2)}) async-start(bf16[8,144,128]{2,1,0:T(8,128)(2,1)} %shard_map.164), calls=%async_computation | async-start | bytes 589824 | tf_op jit(solution)/shard_map/all_to_all | solution.py:569
  15.9 1.1 copy-done
  17.0 1.7 %shard_map.162 = (f32[576,128]{1,0:T(8,128)S(1)}, bf16[576,128]{1,0:T(8,128)(2,1)S(1)}, bf16[576,128]{1,0:T(8,128)(2,1)S(1)}, bf16[576,128]{1,0:T(8,128)(2,1)S(1)}) custom-call(bf16[4,576,128]{2,1,0:T(8,128)(2,1)S(1)} %copy-done, bf16[4,576,128]{2,1,0:T(8,128)(2,1)S(1)} %collective-permute-done.came), custom_call_target="tpu_custom_call" | custom-call | flops 1 | bytes 1 | tf_op jit(solution)/shard_map/pallas_call | solution.py:215
  18.7 1.4 %collective-permute-start.1 = (bf16[576,128]{1,0:T(8,128)(2,1)S(1)}, bf16[576,128]{1,0:T(8,128)(2,1)S(1)}, u32[]{:S(2)}, u32[]{:S(2)}) collective-permute-start(bf16[576,128]{1,0:T(8,128)(2,1)S(1)} %get-tuple-element.32), channel_id=1, source_target_pairs={{0,64},{64,128},{128,192},{192,0},{1,65},{65,129},{129,193},{193,1... | collective-permute-start | bytes 442376 | tf_op jit(solution)/shard_map/ppermute | solution.py:561
  20.1 2.6 %collective-permute-start.2 = (bf16[576,128]{1,0:T(8,128)(2,1)S(1)}, bf16[576,128]{1,0:T(8,128)(2,1)S(1)}, u32[]{:S(2)}, u32[]{:S(2)}) collective-permute-start(bf16[576,128]{1,0:T(8,128)(2,1)S(1)} %get-tuple-element.33), channel_id=1, source_target_pairs={{0,128},{64,192},{128,0},{192,64},{1,129},{65,193},{129,1},{193,65... | collective-permute-start | bytes 442376 | tf_op jit(solution)/shard_map/ppermute | solution.py:561
  22.7 1.1 collective-permute-start.3
  23.8 1.5 %collective-permute-done.1.one = bf16[576,128]{1,0:T(8,128)(2,1)S(1)} collective-permute-done((bf16[576,128]{1,0:T(8,128)(2,1)S(1)}, bf16[576,128]{1,0:T(8,128)(2,1)S(1)}, u32[]{:S(2)}, u32[]{:S(2)}) %collective-permute-start.1) | collective-permute-done | bytes 147488 | tf_op jit(solution)/shard_map/ppermute | solution.py:561
  25.3 4.3 %collective-permute-done.2.two = bf16[576,128]{1,0:T(8,128)(2,1)S(1)} collective-permute-done((bf16[576,128]{1,0:T(8,128)(2,1)S(1)}, bf16[576,128]{1,0:T(8,128)(2,1)S(1)}, u32[]{:S(2)}, u32[]{:S(2)}) %collective-permute-start.2) | collective-permute-done | bytes 147488 | tf_op jit(solution)/shard_map/ppermute | solution.py:561
  29.6 0.1 shard_map.163
  29.7 1.3 %collective-permute-start.4 = (bf16[192,128]{1,0:T(8,128)(2,1)S(1)}, bf16[192,128]{1,0:T(8,128)(2,1)S(1)}, u32[]{:S(2)}, u32[]{:S(2)}) collective-permute-start(bf16[192,128]{1,0:T(8,128)(2,1)S(1)} %get-tuple-element.36), channel_id=1, source_target_pairs={{0,1},{1,2},{2,3},{3,0},{4,5},{5,6},{6,7},{7,4},{8,9},{9,10},{10,1... | collective-permute-start | bytes 147464 | tf_op jit(solution)/shard_map/ppermute | solution.py:561
  31.0 2.5 %collective-permute-start.5 = (bf16[192,128]{1,0:T(8,128)(2,1)S(1)}, bf16[192,128]{1,0:T(8,128)(2,1)S(1)}, u32[]{:S(2)}, u32[]{:S(2)}) collective-permute-start(bf16[192,128]{1,0:T(8,128)(2,1)S(1)} %get-tuple-element.37), channel_id=1, source_target_pairs={{0,2},{1,3},{2,0},{3,1},{4,6},{5,7},{6,4},{7,5},{8,10},{9,11},{10,... | collective-permute-start | bytes 147464 | tf_op jit(solution)/shard_map/ppermute | solution.py:561
  33.4 1.2 %collective-permute-start.6 = (bf16[192,128]{1,0:T(8,128)(2,1)S(1)}, bf16[192,128]{1,0:T(8,128)(2,1)S(1)}, u32[]{:S(2)}, u32[]{:S(2)}) collective-permute-start(bf16[192,128]{1,0:T(8,128)(2,1)S(1)} %get-tuple-element.38), channel_id=1, source_target_pairs={{0,3},{1,0},{2,1},{3,2},{4,7},{5,4},{6,5},{7,6},{8,11},{9,8},{10,9... | collective-permute-start | bytes 147464 | tf_op jit(solution)/shard_map/ppermute | solution.py:561
  34.6 0.9 collective-permute-done.5.l2
  35.5 1.7 %collective-permute-done.6.l3 = bf16[192,128]{1,0:T(8,128)(2,1)S(1)} collective-permute-done((bf16[192,128]{1,0:T(8,128)(2,1)S(1)}, bf16[192,128]{1,0:T(8,128)(2,1)S(1)}, u32[]{:S(2)}, u32[]{:S(2)}) %collective-permute-start.6) | collective-permute-done | bytes 49184 | tf_op jit(solution)/shard_map/ppermute | solution.py:561
  37.1 0.4 shard_map.165
  37.5 16.2 %all_to_all.20.ps = bf16[32,24,128]{2,1,0:T(8,128)(2,1)S(1)} all-to-all(bf16[32,24,128]{2,1,0:T(8,128)(2,1)S(1)} %shard_map.165), channel_id=1, replica_groups=mesh['y'=4,'core'=2,'z'=8,'x'=4] {'y','core','x'}, dimensions={0} | all-to-all | bytes 393216 | tf_op jit(solution)/shard_map/all_to_all | solution.py:569
  53.7 0.2 shard_map.166
  53.9 19.9 %all_to_all.21.recv = bf16[32,40,128]{2,1,0:T(8,128)(2,1)S(1)} all-to-all(bf16[32,40,128]{2,1,0:T(8,128)(2,1)S(1)} %shard_map.166), channel_id=1, replica_groups=mesh['y'=4,'core'=2,'z'=8,'x'=4] {'z','x'}, dimensions={0} | all-to-all | bytes 655360 | tf_op jit(solution)/shard_map/all_to_all | solution.py:569
  73.8 3.9 %shard_map.167 = (bf16[32,24,128]{2,1,0:T(8,128)(2,1)S(1)}, bf16[160,128]{1,0:T(8,128)(2,1)S(1)}) custom-call(bf16[32,40,128]{2,1,0:T(8,128)(2,1)S(1)} %all_to_all.21.recv), custom_call_target="tpu_custom_call" | custom-call | tf_op jit(solution)/shard_map/pallas_call | solution.py:423
  77.8 14.4 %all_to_all.22.rows = bf16[32,24,128]{2,1,0:T(8,128)(2,1)S(1)} all-to-all(bf16[32,24,128]{2,1,0:T(8,128)(2,1)S(1)} %get-tuple-element.40), channel_id=1, replica_groups=mesh['y'=4,'core'=2,'z'=8,'x'=4] {'z','x'}, dimensions={0} | all-to-all | bytes 393216 | tf_op jit(solution)/shard_map/all_to_all | solution.py:569
  92.3 1.0 collective-permute-start.9
  93.2 1.2 %collective-permute-start.8 = (bf16[736,128]{1,0:T(8,128)(2,1)S(1)}, bf16[736,128]{1,0:T(8,128)(2,1)S(1)}, u32[]{:S(2)}, u32[]{:S(2)}) collective-permute-start(bf16[736,128]{1,0:T(8,128)(2,1)S(1)} %shard_map.168.b0), channel_id=1, source_target_pairs={{0,128},{64,192},{128,0},{192,64},{1,129},{65,193},{129,1},{193,65... | collective-permute-start | bytes 565256 | tf_op jit(solution)/shard_map/ppermute | solution.py:561
  94.5 2.2 %broadcast_multiply_fusion = (f32[2,8,29568]{2,1,0:T(8,128)S(1)}, f32[2,8,29568]{2,1,0:T(8,128)S(1)}, f32[2,8,29568]{2,1,0:T(8,128)S(1)}) fusion(f32[2,8,29568]{2,1,0:T(8,128)} %param.13, f32[2,8,29568]{2,1,0:T(8,128)S(1)} %copy-done.1, bf16[1,2,8,29568]{3,2,1,0:T(8,128)(2,1)} %param.12, bf16[1,2,8,29568]{3,2,1,0:T(8,128)(2,1)S(1)} %copy-done.2), kind=kLoop, calls=%fused_computation.2 | loop fusion | flops 3311616 | bytes 11354112 | tf_op jit(solution)/shard_map/mul | solution.py:557
  96.7 3.8 %collective-permute-start.10 = (bf16[736,128]{1,0:T(8,128)(2,1)S(1)}, bf16[736,128]{1,0:T(8,128)(2,1)S(1)}, u32[]{:S(2)}, u32[]{:S(2)}) collective-permute-start(bf16[736,128]{1,0:T(8,128)(2,1)S(1)} %shard_map.168.b0), channel_id=1, source_target_pairs={{0,32},{32,0},{1,33},{33,1},{2,34},{34,2},{3,35},{35,3},{4,36},{36... | collective-permute-start | bytes 565256 | tf_op jit(solution)/shard_map/ppermute | solution.py:565
  100.5 1.0 collective-permute-start.13
  101.5 2.5 %collective-permute-start.12 = (bf16[736,128]{1,0:T(8,128)(2,1)S(1)}, bf16[736,128]{1,0:T(8,128)(2,1)S(1)}, u32[]{:S(2)}, u32[]{:S(2)}) collective-permute-start(bf16[736,128]{1,0:T(8,128)(2,1)S(1)} %collective-permute-done.8.b2), channel_id=1, source_target_pairs={{0,32},{32,0},{1,33},{33,1},{2,34},{34,2},{3,35},{35,3},{4,36},{36... | collective-permute-start | bytes 565256 | tf_op jit(solution)/shard_map/ppermute | solution.py:565
  104.0 1.9 %collective-permute-start.11 = (bf16[736,128]{1,0:T(8,128)(2,1)S(1)}, bf16[736,128]{1,0:T(8,128)(2,1)S(1)}, u32[]{:S(2)}, u32[]{:S(2)}) collective-permute-start(bf16[736,128]{1,0:T(8,128)(2,1)S(1)} %collective-permute-done.7.b1), channel_id=1, source_target_pairs={{0,32},{32,0},{1,33},{33,1},{2,34},{34,2},{3,35},{35,3},{4,36},{36... | collective-permute-start | bytes 565256 | tf_op jit(solution)/shard_map/ppermute | solution.py:565
  106.0 0.9 collective-permute-done.11.b5
  107.0 3.6 %shard_map.169 = (f32[2,8,29568]{2,1,0:T(8,128)}, bf16[2,8,29568]{2,1,0:T(8,128)(2,1)}, f32[2,8,29568]{2,1,0:T(8,128)}, f32[8,8192]{1,0:T(8,128)}, bf16[8,8192]{...) custom-call(bf16[736,128]{1,0:T(8,128)(2,1)S(1)} %shard_map.168.b0, ...), custom_call_target="tpu_custom_call" | custom-call | tf_op jit(solution)/shard_map/pallas_call | solution.py:529
  (26 shorter events, 0.2 us)
Async XLA Ops:
  4.3 11.7 %collective-permute-start = (bf16[4,576,128]{2,1,0:T(8,128)(2,1)}, bf16[4,576,128]{2,1,0:T(8,128)(2,1)S(1)}, u32[]{:S(2)}, u32[]{:S(2)}) collective-permute-start(bf16[4,576,128]{2,1,0:T(8,128)(2,1)} %get-tuple-element.30), channel_id=1, source_target_pairs={{0,32},{32,0},{1,33},{33,1},{2,34},{34,2},{3,35},{35,3},{4,36},{36... | collective-permute-start | bytes 1769480 | tf_op jit(solution)/shard_map/ppermute | solution.py:565
  9.5 25.1 %all-to-all-start = ((bf16[8,144,128]{2,1,0:T(8,128)(2,1)}), bf16[8,144,128]{2,1,0:T(8,128)(2,1)S(1)}, u32[]{:S(2)}, u32[]{:S(2)}) async-start(bf16[8,144,128]{2,1,0:T(8,128)(2,1)} %shard_map.164), calls=%async_computation | async-start | bytes 589824 | tf_op jit(solution)/shard_map/all_to_all | solution.py:569
  15.9 1.1 copy-start
  18.7 6.6 %collective-permute-start.1 = (bf16[576,128]{1,0:T(8,128)(2,1)S(1)}, bf16[576,128]{1,0:T(8,128)(2,1)S(1)}, u32[]{:S(2)}, u32[]{:S(2)}) collective-permute-start(bf16[576,128]{1,0:T(8,128)(2,1)S(1)} %get-tuple-element.32), channel_id=1, source_target_pairs={{0,64},{64,128},{128,192},{192,0},{1,65},{65,129},{129,193},{193,1... | collective-permute-start | bytes 442376 | tf_op jit(solution)/shard_map/ppermute | solution.py:561
  20.1 9.5 %collective-permute-start.2 = (bf16[576,128]{1,0:T(8,128)(2,1)S(1)}, bf16[576,128]{1,0:T(8,128)(2,1)S(1)}, u32[]{:S(2)}, u32[]{:S(2)}) collective-permute-start(bf16[576,128]{1,0:T(8,128)(2,1)S(1)} %get-tuple-element.33), channel_id=1, source_target_pairs={{0,128},{64,192},{128,0},{192,64},{1,129},{65,193},{129,1},{193,65... | collective-permute-start | bytes 442376 | tf_op jit(solution)/shard_map/ppermute | solution.py:561
  22.7 6.8 %collective-permute-start.3 = (bf16[576,128]{1,0:T(8,128)(2,1)S(1)}, bf16[576,128]{1,0:T(8,128)(2,1)S(1)}, u32[]{:S(2)}, u32[]{:S(2)}) collective-permute-start(bf16[576,128]{1,0:T(8,128)(2,1)S(1)} %get-tuple-element.34), channel_id=1, source_target_pairs={{0,192},{64,0},{128,64},{192,128},{1,193},{65,1},{129,65},{193,129... | collective-permute-start | bytes 442376 | tf_op jit(solution)/shard_map/ppermute | solution.py:561
  29.7 64.8 %copy-start.1 = (f32[2,8,29568]{2,1,0:T(8,128)S(1)}, f32[2,8,29568]{2,1,0:T(8,128)}, u32[]{:S(2)}) copy-start(f32[2,8,29568]{2,1,0:T(8,128)} %gs.1) | copy-start | bytes 5677060
  29.7 4.9 %collective-permute-start.4 = (bf16[192,128]{1,0:T(8,128)(2,1)S(1)}, bf16[192,128]{1,0:T(8,128)(2,1)S(1)}, u32[]{:S(2)}, u32[]{:S(2)}) collective-permute-start(bf16[192,128]{1,0:T(8,128)(2,1)S(1)} %get-tuple-element.36), channel_id=1, source_target_pairs={{0,1},{1,2},{2,3},{3,0},{4,5},{5,6},{6,7},{7,4},{8,9},{9,10},{10,1... | collective-permute-start | bytes 147464 | tf_op jit(solution)/shard_map/ppermute | solution.py:561
  31.0 4.5 %collective-permute-start.5 = (bf16[192,128]{1,0:T(8,128)(2,1)S(1)}, bf16[192,128]{1,0:T(8,128)(2,1)S(1)}, u32[]{:S(2)}, u32[]{:S(2)}) collective-permute-start(bf16[192,128]{1,0:T(8,128)(2,1)S(1)} %get-tuple-element.37), channel_id=1, source_target_pairs={{0,2},{1,3},{2,0},{3,1},{4,6},{5,7},{6,4},{7,5},{8,10},{9,11},{10,... | collective-permute-start | bytes 147464 | tf_op jit(solution)/shard_map/ppermute | solution.py:561
  33.4 3.7 %collective-permute-start.6 = (bf16[192,128]{1,0:T(8,128)(2,1)S(1)}, bf16[192,128]{1,0:T(8,128)(2,1)S(1)}, u32[]{:S(2)}, u32[]{:S(2)}) collective-permute-start(bf16[192,128]{1,0:T(8,128)(2,1)S(1)} %get-tuple-element.38), channel_id=1, source_target_pairs={{0,3},{1,0},{2,1},{3,2},{4,7},{5,4},{6,5},{7,6},{8,11},{9,8},{10,9... | collective-permute-start | bytes 147464 | tf_op jit(solution)/shard_map/ppermute | solution.py:561
  34.6 59.9 %copy-start.2 = (bf16[1,2,8,29568]{3,2,1,0:T(8,128)(2,1)S(1)}, bf16[1,2,8,29568]{3,2,1,0:T(8,128)(2,1)}, u32[]{:S(2)}) copy-start(bf16[1,2,8,29568]{3,2,1,0:T(8,128)(2,1)} %param.11) | copy-start | bytes 2838532
  92.2 13.7 %copy-start.3 = (f32[8,8192]{1,0:T(8,128)S(1)}, f32[8,8192]{1,0:T(8,128)}, u32[]{:S(2)}) copy-start(f32[8,8192]{1,0:T(8,128)} %ds.1) | copy-start | bytes 786436
  92.2 13.7 %copy-start.4 = (bf16[1,8,8192]{2,1,0:T(8,128)(2,1)S(1)}, bf16[1,8,8192]{2,1,0:T(8,128)(2,1)}, u32[]{:S(2)}) copy-start(bf16[1,8,8192]{2,1,0:T(8,128)(2,1)} %param.16) | copy-start | bytes 393220
  92.2 13.7 %copy-start.5 = (bf16[1,8,8192]{2,1,0:T(8,128)(2,1)S(1)}, bf16[1,8,8192]{2,1,0:T(8,128)(2,1)}, u32[]{:S(2)}) copy-start(bf16[1,8,8192]{2,1,0:T(8,128)(2,1)} %param.17) | copy-start | bytes 393220
  92.2 13.7 %copy-start.6 = (f32[8,8192]{1,0:T(8,128)S(1)}, f32[8,8192]{1,0:T(8,128)}, u32[]{:S(2)}) copy-start(f32[8,8192]{1,0:T(8,128)} %param.18) | copy-start | bytes 786436
  92.3 8.2 %collective-permute-start.9 = (bf16[736,128]{1,0:T(8,128)(2,1)S(1)}, bf16[736,128]{1,0:T(8,128)(2,1)S(1)}, u32[]{:S(2)}, u32[]{:S(2)}) collective-permute-start(bf16[736,128]{1,0:T(8,128)(2,1)S(1)} %shard_map.168.b0), channel_id=1, source_target_pairs={{0,192},{64,0},{128,64},{192,128},{1,193},{65,1},{129,65},{193,129... | collective-permute-start | bytes 565256 | tf_op jit(solution)/shard_map/ppermute | solution.py:561
  93.2 8.3 %collective-permute-start.8 = (bf16[736,128]{1,0:T(8,128)(2,1)S(1)}, bf16[736,128]{1,0:T(8,128)(2,1)S(1)}, u32[]{:S(2)}, u32[]{:S(2)}) collective-permute-start(bf16[736,128]{1,0:T(8,128)(2,1)S(1)} %shard_map.168.b0), channel_id=1, source_target_pairs={{0,128},{64,192},{128,0},{192,64},{1,129},{65,193},{129,1},{193,65... | collective-permute-start | bytes 565256 | tf_op jit(solution)/shard_map/ppermute | solution.py:561
  94.5 9.5 %collective-permute-start.7 = (bf16[736,128]{1,0:T(8,128)(2,1)S(1)}, bf16[736,128]{1,0:T(8,128)(2,1)S(1)}, u32[]{:S(2)}, u32[]{:S(2)}) collective-permute-start(bf16[736,128]{1,0:T(8,128)(2,1)S(1)} %shard_map.168.b0), channel_id=1, source_target_pairs={{0,64},{64,128},{128,192},{192,0},{1,65},{65,129},{129,193},{193,1... | collective-permute-start | bytes 565256 | tf_op jit(solution)/shard_map/ppermute | solution.py:561
  96.7 9.3 %collective-permute-start.10 = (bf16[736,128]{1,0:T(8,128)(2,1)S(1)}, bf16[736,128]{1,0:T(8,128)(2,1)S(1)}, u32[]{:S(2)}, u32[]{:S(2)}) collective-permute-start(bf16[736,128]{1,0:T(8,128)(2,1)S(1)} %shard_map.168.b0), channel_id=1, source_target_pairs={{0,32},{32,0},{1,33},{33,1},{2,34},{34,2},{3,35},{35,3},{4,36},{36... | collective-permute-start | bytes 565256 | tf_op jit(solution)/shard_map/ppermute | solution.py:565
  100.5 5.5 %collective-permute-start.13 = (bf16[736,128]{1,0:T(8,128)(2,1)S(1)}, bf16[736,128]{1,0:T(8,128)(2,1)S(1)}, u32[]{:S(2)}, u32[]{:S(2)}) collective-permute-start(bf16[736,128]{1,0:T(8,128)(2,1)S(1)} %collective-permute-done.9.b3), channel_id=1, source_target_pairs={{0,32},{32,0},{1,33},{33,1},{2,34},{34,2},{3,35},{35,3},{4,36},{36... | collective-permute-start | bytes 565256 | tf_op jit(solution)/shard_map/ppermute | solution.py:565
  101.5 4.5 %collective-permute-start.12 = (bf16[736,128]{1,0:T(8,128)(2,1)S(1)}, bf16[736,128]{1,0:T(8,128)(2,1)S(1)}, u32[]{:S(2)}, u32[]{:S(2)}) collective-permute-start(bf16[736,128]{1,0:T(8,128)(2,1)S(1)} %collective-permute-done.8.b2), channel_id=1, source_target_pairs={{0,32},{32,0},{1,33},{33,1},{2,34},{34,2},{3,35},{35,3},{4,36},{36... | collective-permute-start | bytes 565256 | tf_op jit(solution)/shard_map/ppermute | solution.py:565
  104.0 3.0 %collective-permute-start.11 = (bf16[736,128]{1,0:T(8,128)(2,1)S(1)}, bf16[736,128]{1,0:T(8,128)(2,1)S(1)}, u32[]{:S(2)}, u32[]{:S(2)}) collective-permute-start(bf16[736,128]{1,0:T(8,128)(2,1)S(1)} %collective-permute-done.7.b1), channel_id=1, source_target_pairs={{0,32},{32,0},{1,33},{33,1},{2,34},{34,2},{3,35},{35,3},{4,36},{36... | collective-permute-start | bytes 565256 | tf_op jit(solution)/shard_map/ppermute | solution.py:565

commit v4 on v3

--- a/solution.py
+++ b/solution.py
@@ -64,10 +64,11 @@
 GU_ROWS = SHARDS * 16
 DN_TILES = D // REPS // LANES
 BLOCK = GU_ROWS + DN_TILES * 8
+X_ROWS = 8 * 16 + 16
 
 
 def lower_kernel(gs, gf, ge, ds, df, de, own, oth, gsv, gfv, gev, dsv, dfv, dev, sems):
-    y, core, _ = places()
+    core = lax.axis_index("core")
     bounds = group_bounds()
     copies = []
     for g in range(GROUPS):
@@ -85,11 +86,14 @@
         copies.append(row)
     first = core == 0
     lane = lane_ids()
-    slots = [lax.rem(yy - y + 4, 4) for yy in range(4)]
 
     def gu_tile(tile):
         at = (slice(None), slice(None), pl.ds(tile * LANES, LANES))
         return gsv[at] - gfv[at].astype(F32) + gev[at].astype(F32)
+
+    def put(yy, x, at, one, two):
+        own[4 * yy + x, at : at + 16] = jnp.where(first, one, two).astype(BF16)
+        oth[4 * yy + x, at : at + 16] = jnp.where(first, two, one).astype(BF16)
 
     for shard in range(SHARDS):
         if shard % PER == 0:
@@ -100,32 +104,30 @@
             tiles[0] = jnp.where(lane[None] < 24, gu_tile(first_tile(shard) + 8), tiles[0])
         for yy in range(4):
             one, two = (tiles[2 * yy + c].reshape(16, LANES) for c in range(2))
-            at = slice(16 * shard, 16 * shard + 16)
-            own[slots[yy], at] = jnp.where(first, one, two).astype(BF16)
-            oth[slots[yy], at] = jnp.where(first, two, one).astype(BF16)
-    for half in range(DN_TILES // 2):
+            put(yy, shard % 4, 16 * (shard // 4), one, two)
+    for x in range(4):
         parts = [[None, None] for _ in range(REPS)]
-        for k in range(2):
-            wide = pl.ds(4 * DN_COLS * (2 * half + k), 4 * DN_COLS)
-            dn = dsv[:, wide] - dfv[:, wide].astype(F32) + dev[:, wide].astype(F32)
+        for p in range(2):
+            sources = []
+            for j in range(4):
+                at = (slice(None), pl.ds(DN_COLS * (4 * (4 * p + j) + x), DN_COLS))
+                sources.append(dsv[at] - dfv[at].astype(F32) + dev[at].astype(F32))
             for r in range(REPS):
                 tile = None
-                for a in range(4):
-                    at = DN_COLS * a + LANES * (r // 4)
-                    piece = dn[:, at : at + LANES]
-                    if a != r % 4:
-                        piece = pltpu.roll(piece, 32 * (a - r % 4) % LANES, 1)
-                    tile = piece if a == 0 else jnp.where(lane < 32 * a, tile, piece)
-                parts[r][k] = tile
+                for j in range(4):
+                    at = LANES * (r // 4)
+                    piece = sources[j][:, at : at + LANES]
+                    if j != r % 4:
+                        piece = pltpu.roll(piece, 32 * (j - r % 4) % LANES, 1)
+                    tile = piece if j == 0 else jnp.where(lane < 32 * j, tile, piece)
+                parts[r][p] = tile
         for yy in range(4):
             one, two = (jnp.concatenate(parts[2 * yy + c], axis=0) for c in range(2))
-            at = slice(GU_ROWS + 16 * half, GU_ROWS + 16 * half + 16)
-            own[slots[yy], at] = jnp.where(first, one, two).astype(BF16)
-            oth[slots[yy], at] = jnp.where(first, two, one).astype(BF16)
+            put(yy, x, 8 * 16, one, two)
 
 
 def lower(gs, gf, ge, ds, df, de):
-    shape = jax.ShapeDtypeStruct((4, BLOCK, LANES), BF16)
+    shape = jax.ShapeDtypeStruct((16, X_ROWS, LANES), BF16)
     return pl.pallas_call(
         lower_kernel,
         out_shape=(shape, shape),
@@ -140,7 +142,7 @@
             pltpu.VMEM((8, D), BF16),
             pltpu.SemaphoreType.DMA((GROUPS, 6)),
         ],
-        compiler_params=params(59),
+        compiler_params=params(54),
         cost_estimate=LIGHT,
     )(gs, gf, ge, ds, df, de)
 
@@ -187,157 +189,133 @@
             pltpu.VMEM((RANK, DN_COLS), BF16),
             pltpu.SemaphoreType.DMA((2,)),
         ],
-        compiler_params=params(59),
+        compiler_params=params(16),
     )(gu, dn_t)
 
 
-def pair_kernel(own, came, zero, one, two, three, own_v, came_v, sems):
-    order = (2, 1, 3, 0)
-    copies = []
-    for k in order:
-        row = []
-        for i, (src, dst) in enumerate(((own, own_v), (came, came_v))):
-            row.append(pltpu.make_async_copy(src.at[k], dst.at[k], sems.at[k, i]))
-            row[-1].start()
-        copies.append(row)
-    outs = (zero, one, two, three)
-    for k, row in zip(order, copies):
-        for copy in row:
-            copy.wait()
-        for at in range(0, BLOCK, 64):
-            rows = slice(at, at + 64)
-            total = own_v[k, rows].astype(F32) + came_v[k, rows].astype(F32)
-            outs[k][rows] = total.astype(outs[k].dtype)
+def pair_kernel(own, came, zero, one, two, three):
+    y = lax.axis_index("y")
+    for k, out in ((2, two), (1, one), (3, three), (0, zero)):
+        to = 4 * lax.rem(y + k, 4)
+        for x in range(4):
+            total = own[to + x].astype(F32) + came[to + x].astype(F32)
+            out[x] = total.astype(out.dtype)
 
 
 def pair_sums(own, came):
-    block = (BLOCK, LANES)
+    block = (4, X_ROWS, LANES)
     return pl.pallas_call(
         pair_kernel,
         out_shape=(
             jax.ShapeDtypeStruct(block, F32),
             *[jax.ShapeDtypeStruct(block, BF16)] * 3,
         ),
-        in_specs=[ANY] * 2,
+        in_specs=[VMEM] * 2,
         out_specs=(VMEM,) * 4,
-        scratch_shapes=[
-            pltpu.VMEM((4, BLOCK, LANES), BF16),
-            pltpu.VMEM((4, BLOCK, LANES), BF16),
-            pltpu.SemaphoreType.DMA((4, 2)),
-        ],
         compiler_params=params(16),
         cost_estimate=LIGHT,
     )(own, came)
 
 
-X_ROWS = 8 * 16 + DN_TILES * 8
-
-
-def y_sum_kernel(zero, one, two, three, out, x0, x1, x2, x3):
-    for at in range(0, BLOCK, 64):
-        rows = slice(at, at + 64)
-        total = zero[rows]
+def y_sum_kernel(zero, one, two, three, x0, x1, x2, x3, sums):
+    for x in range(4):
+        total = zero[x]
         for ref in (one, two, three):
-            total = total + ref[rows].astype(F32)
-        out[rows] = total.astype(BF16)
+            total = total + ref[x].astype(F32)
+        sums[x] = total.astype(BF16)
     x = lax.axis_index("x")
     for k, ref in enumerate((x0, x1, x2, x3)):
-        to_x = lax.rem(x + k, 4)
-        for z in range(8):
-            at = pl.multiple_of(16 * (4 * z + to_x), 16)
-            ref[16 * z : 16 * z + 16, :] = out[pl.ds(at, 16), :]
-        ref[8 * 16 :, :] = out[GU_ROWS:BLOCK, :]
+        ref[...] = sums[lax.rem(x + k, 4)]
 
 
 def y_sum(zero, comes):
     return pl.pallas_call(
         y_sum_kernel,
-        out_shape=(
-            jax.ShapeDtypeStruct((BLOCK, LANES), BF16),
-            *[jax.ShapeDtypeStruct((X_ROWS, LANES), BF16)] * 4,
-        ),
+        out_shape=(jax.ShapeDtypeStruct((X_ROWS, LANES), BF16),) * 4,
         in_specs=[VMEM] * 4,
-        out_specs=(VMEM,) * 5,
+        out_specs=(VMEM,) * 4,
+        scratch_shapes=[pltpu.VMEM((4, X_ROWS, LANES), BF16)],
         compiler_params=params(16),
     )(zero, comes[1], comes[2], comes[3])
 
 
-def split_hi_lo(value):
-    hi = value.astype(BF16).astype(F32)
-    return jnp.concatenate([hi, value - hi], axis=-1).astype(BF16)
-
-
-def p_part_kernel(l0, l1, l2, l3, basis, out, dn_rows):
+P_ROWS = 48
+Z_ROWS = 4 * 24 + P_ROWS
+
+
+def p_part_kernel(l0, l1, l2, l3, basis, rows, out, stage):
     x = lax.axis_index("x")
-    lefts = (l0, l1, l2, l3)
+    for k, ref in enumerate((l0, l1, l2, l3)):
+        stage[lax.rem(x - k + 4, 4)] = ref[...]
+    lows = [stage[x] for x in range(4)]
+    sums = [stage[x, 8 * 16 : X_ROWS, :].astype(F32) for x in range(4)]
     gu = jnp.zeros((64, LANES), F32)
     for z in range(0, 8, 2):
         left = [
-            jnp.concatenate([ref[16 * i : 16 * i + 16, :] for ref in lefts], axis=0)
+            jnp.concatenate([low[16 * i : 16 * i + 16] for low in lows], axis=0)
             for i in (z, z + 1)
         ]
+        rows[z, 0:64, :] = left[0]
+        rows[z + 1, 0:64, :] = left[1]
         right = basis[z : z + 2, 0:LANES, :].reshape(2 * LANES, LANES)
         gu = gu + jnp.dot(jnp.concatenate(left, axis=1), right, preferred_element_type=F32)
-    dn_rows[...] = jnp.zeros_like(dn_rows)
-    right = basis[:, LANES:B_ROWS, :].astype(F32)
-    right = jnp.concatenate([right[:, :, 0:RANK], right[:, :, RANK:LANES]], axis=1)
-    dn_rows[:, pl.ds(pl.multiple_of(32 * x, 32), 32), :] = right
-    tiles = [ref[8 * 16 :, :].astype(F32) for ref in lefts]
     dn = jnp.zeros((32, RANK), F32)
-    for q in range(DN_TILES):
-        left = jnp.concatenate([tile[8 * q : 8 * q + 8] for tile in tiles], axis=0)
-        dn = dn + jnp.dot(
-            left.astype(BF16), dn_rows[q].astype(BF16), preferred_element_type=F32
-        )
-    for k in range(4):
-        part = jnp.concatenate(
+    for p in range(2):
+        left = [total[8 * p : 8 * p + 8] for total in sums]
+        left = jnp.concatenate(left, axis=0).astype(BF16)
+        for z in range(4 * p, 4 * p + 4):
+            rows[z, 64:96, :] = left
+        right = basis[4 * p : 4 * p + 4, LANES:B_ROWS, :].astype(F32)
+        right = jnp.concatenate([right[:, :, 0:RANK], right[:, :, RANK:LANES]], axis=1)
+        right = right.reshape(LANES, RANK).astype(BF16)
+        dn = dn + jnp.dot(left, right, preferred_element_type=F32)
+    parts = [
+        jnp.concatenate(
             [
-                gu[16 * k : 16 * k + 8, 0:RANK],
-                gu[16 * k + 8 : 16 * k + 16, RANK:LANES],
-                dn[8 * k : 8 * k + 8],
+                gu[16 * x : 16 * x + 8, 0:RANK],
+                gu[16 * x + 8 : 16 * x + 16, RANK:LANES],
+                dn[8 * x : 8 * x + 8],
             ],
             axis=0,
         )
-        block = split_hi_lo(part)
-        to_x = lax.rem(x - k + 4, 4)
-        for rep in range(REPS):
-            out[4 * rep + to_x] = block
+        for x in range(4)
+    ]
+    block = jnp.concatenate(
+        [jnp.concatenate(parts[k : k + 2], axis=1) for k in (0, 2)], axis=0
+    ).astype(BF16)
+    for member in range(32):
+        out[member] = block
 
 
 def p_part(rows, basis):
     return pl.pallas_call(
         p_part_kernel,
-        out_shape=jax.ShapeDtypeStruct((4 * REPS, 24, LANES), BF16),
+        out_shape=(
+            jax.ShapeDtypeStruct((8, 96, LANES), BF16),
+            jax.ShapeDtypeStruct((32, P_ROWS, LANES), BF16),
+        ),
         in_specs=[VMEM] * 5,
-        out_specs=VMEM,
-        scratch_shapes=[pltpu.VMEM((DN_TILES, LANES, RANK), F32)],
+        out_specs=(VMEM,) * 2,
+        scratch_shapes=[pltpu.VMEM((4, X_ROWS, LANES), BF16)],
         compiler_params=params(16),
     )(*rows, basis)
 
 
-def p_sum_kernel(ps, lbar, out):
-    total = jnp.sum(ps[...].astype(F32), axis=0)
-    rows = total[:, 0:RANK] + total[:, RANK:LANES]
-    rows = jnp.concatenate(
-        [jnp.concatenate([rows[0:8], rows[8:16]], axis=1),
-         jnp.concatenate([rows[16:24], jnp.zeros((8, RANK), F32)], axis=1)],
-        axis=0,
-    )
-    tiles = lbar[GU_ROWS:BLOCK, :].astype(F32)
-    for s in range(SHARDS):
-        gu = lbar[16 * s : 16 * s + 16, :].astype(F32)
-        dn = tiles[8 * (s // 4) : 8 * (s // 4) + 8]
-        out[s] = jnp.concatenate([gu, dn, rows], axis=0).astype(BF16)
-
-
-def p_sum(ps, lbar):
+def p_sum_kernel(ps, rows, out):
+    total = jnp.sum(ps[...].astype(F32), axis=0).astype(BF16)
+    for z in range(8):
+        out[z, 0:96, :] = rows[z]
+        out[z, 96:Z_ROWS, :] = total
+
+
+def p_sum(ps, rows):
     return pl.pallas_call(
         p_sum_kernel,
-        out_shape=jax.ShapeDtypeStruct((SHARDS, 40, LANES), BF16),
+        out_shape=jax.ShapeDtypeStruct((8, Z_ROWS, LANES), BF16),
         in_specs=[VMEM, VMEM],
         out_specs=VMEM,
         compiler_params=params(16),
-    )(ps, lbar)
+    )(ps, rows)
 
 
 def inverse_factors(grams):
@@ -394,13 +372,17 @@
 
 def factor_kernel(recv, a_out, q_out, q_rows):
     block = recv[...].astype(F32)
-    columns = [
-        block[:, 8 * m : 8 * m + 8, :].reshape(256, LANES).astype(BF16) for m in range(3)
-    ]
-    lefts = [
-        block[:, 24:32, 0:RANK], block[:, 24:32, RANK:LANES], block[:, 32:40, 0:RANK]
-    ]
-    lefts = [left.reshape(256, RANK) for left in lefts]
+    gu = block[:, 0:64, :].reshape(8, 4, 16, LANES)
+    columns = [gu[:, :, 0:8], gu[:, :, 8:16], block[:, 64:96, :]]
+    columns = [column.reshape(256, LANES).astype(BF16) for column in columns]
+    lefts = []
+    for m in range(3):
+        left = [
+            block[:, at : at + 8, RANK * b : RANK * b + RANK]
+            for at in (96 + 8 * m, 120 + 8 * m)
+            for b in range(2)
+        ]
+        lefts.append(jnp.stack(left, axis=1).reshape(256, RANK))
     grams = [exact_dot(p, p, ((0,), (0,))) for p in lefts]
     inverses = inverse_factors(grams)
     hs = [exact_dot(p, v, ((1,), (1,))).astype(BF16) for p, v in zip(lefts, inverses)]
@@ -413,7 +395,7 @@
         recons.append(recon.reshape(SHARDS, 8, LANES))
     a_out[...] = jnp.concatenate(recons, axis=1).astype(BF16)
     q_rows[...] = qs[2]
-    dn = q_rows[pl.ds(pl.multiple_of(32 * lax.axis_index("x"), 32), 32), :]
+    dn = q_rows[pl.ds(pl.multiple_of(32 * lax.rem(lax.axis_index("z"), 4), 32), 32), :]
     dn = jnp.concatenate([dn, jnp.zeros_like(dn)], axis=1)
     gu = jnp.concatenate(qs[:2], axis=1)
     q_out[...] = jnp.concatenate([gu, dn], axis=0).astype(BF16)
@@ -440,9 +422,9 @@
 def pack_kernel(rows, q, out):
     for s in range(SHARDS):
         out[16 * s : 16 * s + 16, :] = rows[s].astype(F32)[0:16].astype(BF16)
-    for half in range(DN_TILES // 2):
-        two = [rows[8 * half + 4 * k].astype(F32)[16:24] for k in range(2)]
-        at = GU_ROWS + 16 * half
+    for x in range(4):
+        two = [rows[16 * p + x].astype(F32)[16:24] for p in range(2)]
+        at = GU_ROWS + 16 * x
         out[at : at + 16, :] = jnp.concatenate(two, axis=0).astype(BF16)
     out[BLOCK:PAYLOAD, :] = q[...]
 
@@ -497,7 +479,8 @@
         )
     tiles = [stage[r, GU_ROWS:BLOCK, :].astype(F32) for r in range(REPS)]
     for shard in range(SHARDS):
-        q, a = shard // 4, shard % 4
+        z, x = shard // 4, shard % 4
+        q, a = 2 * x + z // 4, z % 4
         for half in range(2):
             recon = None
             for k in range(4):
@@ -579,11 +562,12 @@
     came = swap(oth)
     zero, *sends = pair_sums(own, came)
     comes = {by: shift(sends[by - 1], "y", 4, by) for by in (2, 1, 3)}
-    lbar, *rows = y_sum(zero, comes)
+    rows = list(y_sum(zero, comes))
     for by in (2, 1, 3):
         rows[by] = shift(rows[by], "x", 4, by)
-    parts = exchange(p_part(rows, basis), ("y", "core", "x"))
-    recv = exchange(p_sum(parts, lbar), SHARD)
+    rows, parts = p_part(rows, basis)
+    parts = exchange(parts, ("y", "core", "x"))
+    recv = exchange(p_sum(parts, rows), "z")
     a_blocks, q_block = factor(recv)
     payload = pack(exchange(a_blocks, SHARD), q_block)
     mine = {0: payload}

time: 111 us -> 108 us (0.973)
  Pallas kernels: 15.4 us -> 13.1 us
  other arithmetic: 2.27 us -> 0.61 us
  starting transfers between devices: 31.2 us -> 32.7 us
    mul x2, other arithmetic: 2.27 us -> 0.61 us  [settled(): return (slow - MOMENT_GAIN * moment, combined, 0.9 * moment)]
    pallas_call x1, Pallas kernels: 1.71 us -> 0.13 us  [pair_sums(): pl.pallas_call(pair_kernel, out_shape=(jax.ShapeDtypeStruct(block, F32),...]
    ppermute x5, starting transfers between devices: 12.5 us -> 14 us  [swap(): return lax.ppermute(value, 'core', [(0, 1), (1, 0)])]
  transfers between devices with their start and end apart: 15 -> 15, of which waited for: 5 -> 5; matrix products, arithmetic and copies ran while one was open for 2% -> 1% of each run, Pallas kernels for 3% -> 1%
where the time goes in v4:
time: 108 us; the launch traced here: 107 us
  blocking collectives  49.9 us (46%)
  starting transfers between devices  32.7 us (30%)
  Pallas kernels  13.1 us (12%)
  waiting for transfers between devices  9 us (8%)
  local copies, waits for them, and re-layouts  1.11 us (1%)
    all_to_all x3, blocking collectives, exchange(): return lax.all_to_all(value, axis, 0, 0, tiled=False)  49.9 us
    ppermute x5, starting transfers between devices, swap(): return lax.ppermute(value, 'core', [(0, 1), (1, 0)])  14 us
    ppermute x9, starting transfers between devices, shift(): lax.ppermute(value, axis, [(i, (i + by) % size) for i in range(size)])  12.3 us
    ppermute x9, waiting for transfers between devices, shift(): lax.ppermute(value, axis, [(i, (i + by) % size) for i in range(size)])  8.05 us
    all_to_all x1, starting transfers between devices, exchange(): return lax.all_to_all(value, axis, 0, 0, tiled=False)  6.46 us
    pallas_call x1, Pallas kernels, factor(): pl.pallas_call(factor_kernel, out_shape=(jax.ShapeDtypeStruct((SHARDS, 24...  3.94 us
    pallas_call x1, Pallas kernels, lower(): pl.pallas_call(lower_kernel, out_shape=(shape, shape), in_specs=[HBM] * 6...  3.67 us
    pallas_call x1, Pallas kernels, finish(): pl.pallas_call(finish_kernel, out_shape=(*[jax.ShapeDtypeStruct(gu, kind)...  3.62 us
  transfers between devices with their start and end apart: 15, of which 5 were waited for; matrix products, arithmetic and copies ran while one was open for 1% of the time, Pallas kernels for 1%

profile of v4, /device:TPU:1, one launch (start us, length us, event | category | flops | bytes accessed | tf_op | source)
XLA Modules:
  0.0 107.4 jit_solution(16863308868049488348)
XLA Ops:
  0.7 3.7 %shard_map.161 = (bf16[16,144,128]{2,1,0:T(8,128)(2,1)}, bf16[16,144,128]{2,1,0:T(8,128)(2,1)}) custom-call(f32[2,8,29568]{2,1,0:T(8,128)} %gs.1, bf16[2,8,29568]{2,1,0:T(8,128)(2,1)} %bitcast.13, bf16[2,8,29568]{2,1,0:T(8,128)(2,1)} %bitcast.14, f32[8,8192]{1,0:T(8,128)} %ds.1, bf16[8,8192]{1,0:T(8,128)(2,1)} %bitcast.15, bf16[8,8192]{1,0:T(8,128)(2,1)} %bitcast.16), custom_call_target="tpu_custom_call" | custom-call | flops 1 | bytes 1 | tf_op jit(solution)/shard_map/pallas_call | solution.py:131
  4.3 3.3 %collective-permute-start = (bf16[16,144,128]{2,1,0:T(8,128)(2,1)}, bf16[16,144,128]{2,1,0:T(8,128)(2,1)S(1)}, u32[]{:S(2)}, u32[]{:S(2)}) collective-permute-start(bf16[16,144,128]{2,1,0:T(8,128)(2,1)} %get-tuple-element.31), channel_id=1, source_target_pairs={{0,32},{32,0},{1,33},{33,1},{2,34},{34,2},{3,35},{35,3},{4,36},{36... | collective-permute-start | bytes 1769480 | tf_op jit(solution)/shard_map/ppermute | solution.py:548
  7.7 1.3 %shard_map.164 = bf16[8,144,128]{2,1,0:T(8,128)(2,1)} custom-call(bf16[924,128]{1,0:T(8,128)(2,1)S(1)} %copy-done.1, bf16[64,256]{1,0:T(8,128)(2,1)S(1)} %bitcast.12), custom_call_target="tpu_custom_call" | custom-call | tf_op jit(solution)/shard_map/pallas_call | solution.py:180
  8.9 6.5 %all-to-all-start = ((bf16[8,144,128]{2,1,0:T(8,128)(2,1)}), bf16[8,144,128]{2,1,0:T(8,128)(2,1)S(1)}, u32[]{:S(2)}, u32[]{:S(2)}) async-start(bf16[8,144,128]{2,1,0:T(8,128)(2,1)} %shard_map.164), calls=%async_computation | async-start | bytes 589824 | tf_op jit(solution)/shard_map/all_to_all | solution.py:552
  15.4 1.1 copy-done
  16.5 0.1 shard_map.162
  16.6 1.4 %collective-permute-start.1 = (bf16[4,144,128]{2,1,0:T(8,128)(2,1)S(1)}, bf16[4,144,128]{2,1,0:T(8,128)(2,1)S(1)}, u32[]{:S(2)}, u32[]{:S(2)}) collective-permute-start(bf16[4,144,128]{2,1,0:T(8,128)(2,1)S(1)} %get-tuple-element.33), channel_id=1, source_target_pairs={{0,64},{64,128},{128,192},{192,0},{1,65},{65,129},{129,193},{193,1... | collective-permute-start | bytes 442376 | tf_op jit(solution)/shard_map/ppermute | solution.py:544
  18.0 2.6 %collective-permute-start.2 = (bf16[4,144,128]{2,1,0:T(8,128)(2,1)S(1)}, bf16[4,144,128]{2,1,0:T(8,128)(2,1)S(1)}, u32[]{:S(2)}, u32[]{:S(2)}) collective-permute-start(bf16[4,144,128]{2,1,0:T(8,128)(2,1)S(1)} %get-tuple-element.34), channel_id=1, source_target_pairs={{0,128},{64,192},{128,0},{192,64},{1,129},{65,193},{129,1},{193,65... | collective-permute-start | bytes 442376 | tf_op jit(solution)/shard_map/ppermute | solution.py:544
  20.6 1.1 collective-permute-start.3
  21.7 1.5 %collective-permute-done.1.one = bf16[4,144,128]{2,1,0:T(8,128)(2,1)S(1)} collective-permute-done((bf16[4,144,128]{2,1,0:T(8,128)(2,1)S(1)}, bf16[4,144,128]{2,1,0:T(8,128)(2,1)S(1)}, u32[]{:S(2)}, u32[]{:S(2)}) %collective-permute-start.1) | collective-permute-done | bytes 147488 | tf_op jit(solution)/shard_map/ppermute | solution.py:544
  23.1 4.3 %collective-permute-done.2.two = bf16[4,144,128]{2,1,0:T(8,128)(2,1)S(1)} collective-permute-done((bf16[4,144,128]{2,1,0:T(8,128)(2,1)S(1)}, bf16[4,144,128]{2,1,0:T(8,128)(2,1)S(1)}, u32[]{:S(2)}, u32[]{:S(2)}) %collective-permute-start.2) | collective-permute-done | bytes 147488 | tf_op jit(solution)/shard_map/ppermute | solution.py:544
  27.4 0.1 shard_map.163
  27.5 1.3 %collective-permute-start.4 = (bf16[144,128]{1,0:T(8,128)(2,1)S(1)}, bf16[144,128]{1,0:T(8,128)(2,1)S(1)}, u32[]{:S(2)}, u32[]{:S(2)}) collective-permute-start(bf16[144,128]{1,0:T(8,128)(2,1)S(1)} %get-tuple-element.37), channel_id=1, source_target_pairs={{0,1},{1,2},{2,3},{3,0},{4,5},{5,6},{6,7},{7,4},{8,9},{9,10},{10,1... | collective-permute-start | bytes 110600 | tf_op jit(solution)/shard_map/ppermute | solution.py:544
  28.8 2.5 %collective-permute-start.5 = (bf16[144,128]{1,0:T(8,128)(2,1)S(1)}, bf16[144,128]{1,0:T(8,128)(2,1)S(1)}, u32[]{:S(2)}, u32[]{:S(2)}) collective-permute-start(bf16[144,128]{1,0:T(8,128)(2,1)S(1)} %get-tuple-element.38), channel_id=1, source_target_pairs={{0,2},{1,3},{2,0},{3,1},{4,6},{5,7},{6,4},{7,5},{8,10},{9,11},{10,... | collective-permute-start | bytes 110600 | tf_op jit(solution)/shard_map/ppermute | solution.py:544
  31.2 1.2 %collective-permute-start.6 = (bf16[144,128]{1,0:T(8,128)(2,1)S(1)}, bf16[144,128]{1,0:T(8,128)(2,1)S(1)}, u32[]{:S(2)}, u32[]{:S(2)}) collective-permute-start(bf16[144,128]{1,0:T(8,128)(2,1)S(1)} %get-tuple-element.39), channel_id=1, source_target_pairs={{0,3},{1,0},{2,1},{3,2},{4,7},{5,4},{6,5},{7,6},{8,11},{9,8},{10,9... | collective-permute-start | bytes 110600 | tf_op jit(solution)/shard_map/ppermute | solution.py:544
  32.4 0.7 collective-permute-done.5.l2
  33.1 1.6 %collective-permute-done.6.l3 = bf16[144,128]{1,0:T(8,128)(2,1)S(1)} collective-permute-done((bf16[144,128]{1,0:T(8,128)(2,1)S(1)}, bf16[144,128]{1,0:T(8,128)(2,1)S(1)}, u32[]{:S(2)}, u32[]{:S(2)}) %collective-permute-start.6) | collective-permute-done | bytes 36896 | tf_op jit(solution)/shard_map/ppermute | solution.py:544
  34.7 0.3 shard_map.165
  35.1 18.4 %all_to_all.20.ps = bf16[32,48,128]{2,1,0:T(8,128)(2,1)S(1)} all-to-all(bf16[32,48,128]{2,1,0:T(8,128)(2,1)S(1)} %get-tuple-element.40), channel_id=1, replica_groups=mesh['y'=4,'core'=2,'z'=8,'x'=4] {'y','core','x'}, dimensions={0} | all-to-all | bytes 786432 | tf_op jit(solution)/shard_map/all_to_all | solution.py:552
  53.5 18.5 %all_to_all.21.recv = bf16[8,144,128]{2,1,0:T(8,128)(2,1)S(1)} all-to-all(bf16[8,144,128]{2,1,0:T(8,128)(2,1)S(1)} %shard_map.166), channel_id=1, replica_groups=mesh['y'=4,'core'=2,'z'=8,'x'=4] {'z'}, dimensions={0} | all-to-all | bytes 589824 | tf_op jit(solution)/shard_map/all_to_all | solution.py:552
  72.0 3.9 %shard_map.167 = (bf16[32,24,128]{2,1,0:T(8,128)(2,1)S(1)}, bf16[160,128]{1,0:T(8,128)(2,1)S(1)}) custom-call(bf16[8,144,128]{2,1,0:T(8,128)(2,1)S(1)} %all_to_all.21.recv), custom_call_target="tpu_custom_call" | custom-call | tf_op jit(solution)/shard_map/pallas_call | solution.py:405
  76.0 13.0 %all_to_all.22.rows = bf16[32,24,128]{2,1,0:T(8,128)(2,1)S(1)} all-to-all(bf16[32,24,128]{2,1,0:T(8,128)(2,1)S(1)} %get-tuple-element.42), channel_id=1, replica_groups=mesh['y'=4,'core'=2,'z'=8,'x'=4] {'z','x'}, dimensions={0} | all-to-all | bytes 393216 | tf_op jit(solution)/shard_map/all_to_all | solution.py:552
  89.0 0.9 collective-permute-start.9
  89.9 1.3 %collective-permute-start.8 = (bf16[736,128]{1,0:T(8,128)(2,1)S(1)}, bf16[736,128]{1,0:T(8,128)(2,1)S(1)}, u32[]{:S(2)}, u32[]{:S(2)}) collective-permute-start(bf16[736,128]{1,0:T(8,128)(2,1)S(1)} %shard_map.168.b0), channel_id=1, source_target_pairs={{0,128},{64,192},{128,0},{192,64},{1,129},{65,193},{129,1},{193,65... | collective-permute-start | bytes 565256 | tf_op jit(solution)/shard_map/ppermute | solution.py:544
  91.2 0.2 collective-permute-start.7
  91.4 0.5 broadcast_multiply_fusion
  91.9 3.7 %collective-permute-start.10 = (bf16[736,128]{1,0:T(8,128)(2,1)S(1)}, bf16[736,128]{1,0:T(8,128)(2,1)S(1)}, u32[]{:S(2)}, u32[]{:S(2)}) collective-permute-start(bf16[736,128]{1,0:T(8,128)(2,1)S(1)} %shard_map.168.b0), channel_id=1, source_target_pairs={{0,32},{32,0},{1,33},{33,1},{2,34},{34,2},{3,35},{35,3},{4,36},{36... | collective-permute-start | bytes 565256 | tf_op jit(solution)/shard_map/ppermute | solution.py:548
  95.7 2.6 %collective-permute-start.13 = (bf16[736,128]{1,0:T(8,128)(2,1)S(1)}, bf16[736,128]{1,0:T(8,128)(2,1)S(1)}, u32[]{:S(2)}, u32[]{:S(2)}) collective-permute-start(bf16[736,128]{1,0:T(8,128)(2,1)S(1)} %collective-permute-done.9.b3), channel_id=1, source_target_pairs={{0,32},{32,0},{1,33},{33,1},{2,34},{34,2},{3,35},{35,3},{4,36},{36... | collective-permute-start | bytes 565256 | tf_op jit(solution)/shard_map/ppermute | solution.py:548
  98.3 2.4 %collective-permute-start.12 = (bf16[736,128]{1,0:T(8,128)(2,1)S(1)}, bf16[736,128]{1,0:T(8,128)(2,1)S(1)}, u32[]{:S(2)}, u32[]{:S(2)}) collective-permute-start(bf16[736,128]{1,0:T(8,128)(2,1)S(1)} %collective-permute-done.8.b2), channel_id=1, source_target_pairs={{0,32},{32,0},{1,33},{33,1},{2,34},{34,2},{3,35},{35,3},{4,36},{36... | collective-permute-start | bytes 565256 | tf_op jit(solution)/shard_map/ppermute | solution.py:548
  100.7 1.9 %collective-permute-start.11 = (bf16[736,128]{1,0:T(8,128)(2,1)S(1)}, bf16[736,128]{1,0:T(8,128)(2,1)S(1)}, u32[]{:S(2)}, u32[]{:S(2)}) collective-permute-start(bf16[736,128]{1,0:T(8,128)(2,1)S(1)} %collective-permute-done.7.b1), channel_id=1, source_target_pairs={{0,32},{32,0},{1,33},{33,1},{2,34},{34,2},{3,35},{35,3},{4,36},{36... | collective-permute-start | bytes 565256 | tf_op jit(solution)/shard_map/ppermute | solution.py:548
  102.7 0.9 collective-permute-done.11.b5
  103.6 3.6 %shard_map.169 = (f32[2,8,29568]{2,1,0:T(8,128)}, bf16[2,8,29568]{2,1,0:T(8,128)(2,1)}, f32[2,8,29568]{2,1,0:T(8,128)}, f32[8,8192]{1,0:T(8,128)}, bf16[8,8192]{...) custom-call(bf16[736,128]{1,0:T(8,128)(2,1)S(1)} %shard_map.168.b0, ...), custom_call_target="tpu_custom_call" | custom-call | tf_op jit(solution)/shard_map/pallas_call | solution.py:512
  (34 shorter events, 0.3 us)
Async XLA Ops:
  0.6 7.0 %copy-start.1 = (bf16[924,128]{1,0:T(8,128)(2,1)S(1)}, bf16[924,128]{1,0:T(8,128)(2,1)}, u32[]{:S(2)}) copy-start(bf16[924,128]{1,0:T(8,128)(2,1)} %gu_any.1) | copy-start | bytes 709636
  0.6 7.0 %copy-start.2 = (bf16[256,64]{0,1:T(8,128)(2,1)S(1)}, bf16[256,64]{0,1:T(8,128)(2,1)}, u32[]{:S(2)}) copy-start(bf16[256,64]{0,1:T(8,128)(2,1)} %param.19) | copy-start | bytes 98308
  4.3 11.1 %collective-permute-start = (bf16[16,144,128]{2,1,0:T(8,128)(2,1)}, bf16[16,144,128]{2,1,0:T(8,128)(2,1)S(1)}, u32[]{:S(2)}, u32[]{:S(2)}) collective-permute-start(bf16[16,144,128]{2,1,0:T(8,128)(2,1)} %get-tuple-element.31), channel_id=1, source_target_pairs={{0,32},{32,0},{1,33},{33,1},{2,34},{34,2},{3,35},{35,3},{4,36},{36... | collective-permute-start | bytes 1769480 | tf_op jit(solution)/shard_map/ppermute | solution.py:548
  8.9 23.4 %all-to-all-start = ((bf16[8,144,128]{2,1,0:T(8,128)(2,1)}), bf16[8,144,128]{2,1,0:T(8,128)(2,1)S(1)}, u32[]{:S(2)}, u32[]{:S(2)}) async-start(bf16[8,144,128]{2,1,0:T(8,128)(2,1)} %shard_map.164), calls=%async_computation | async-start | bytes 589824 | tf_op jit(solution)/shard_map/all_to_all | solution.py:552
  15.4 1.1 copy-start
  16.5 74.9 %copy-start.6 = (f32[2,8,29568]{2,1,0:T(8,128)S(1)}, f32[2,8,29568]{2,1,0:T(8,128)}, u32[]{:S(2)}) copy-start(f32[2,8,29568]{2,1,0:T(8,128)} %param.13) | copy-start | bytes 5677060
  16.6 6.5 %collective-permute-start.1 = (bf16[4,144,128]{2,1,0:T(8,128)(2,1)S(1)}, bf16[4,144,128]{2,1,0:T(8,128)(2,1)S(1)}, u32[]{:S(2)}, u32[]{:S(2)}) collective-permute-start(bf16[4,144,128]{2,1,0:T(8,128)(2,1)S(1)} %get-tuple-element.33), channel_id=1, source_target_pairs={{0,64},{64,128},{128,192},{192,0},{1,65},{65,129},{129,193},{193,1... | collective-permute-start | bytes 442376 | tf_op jit(solution)/shard_map/ppermute | solution.py:544
  18.0 9.4 %collective-permute-start.2 = (bf16[4,144,128]{2,1,0:T(8,128)(2,1)S(1)}, bf16[4,144,128]{2,1,0:T(8,128)(2,1)S(1)}, u32[]{:S(2)}, u32[]{:S(2)}) collective-permute-start(bf16[4,144,128]{2,1,0:T(8,128)(2,1)S(1)} %get-tuple-element.34), channel_id=1, source_target_pairs={{0,128},{64,192},{128,0},{192,64},{1,129},{65,193},{129,1},{193,65... | collective-permute-start | bytes 442376 | tf_op jit(solution)/shard_map/ppermute | solution.py:544
  20.6 6.8 %collective-permute-start.3 = (bf16[4,144,128]{2,1,0:T(8,128)(2,1)S(1)}, bf16[4,144,128]{2,1,0:T(8,128)(2,1)S(1)}, u32[]{:S(2)}, u32[]{:S(2)}) collective-permute-start(bf16[4,144,128]{2,1,0:T(8,128)(2,1)S(1)} %get-tuple-element.35), channel_id=1, source_target_pairs={{0,192},{64,0},{128,64},{192,128},{1,193},{65,1},{129,65},{193,129... | collective-permute-start | bytes 442376 | tf_op jit(solution)/shard_map/ppermute | solution.py:544
  27.5 4.9 %collective-permute-start.4 = (bf16[144,128]{1,0:T(8,128)(2,1)S(1)}, bf16[144,128]{1,0:T(8,128)(2,1)S(1)}, u32[]{:S(2)}, u32[]{:S(2)}) collective-permute-start(bf16[144,128]{1,0:T(8,128)(2,1)S(1)} %get-tuple-element.37), channel_id=1, source_target_pairs={{0,1},{1,2},{2,3},{3,0},{4,5},{5,6},{6,7},{7,4},{8,9},{9,10},{10,1... | collective-permute-start | bytes 110600 | tf_op jit(solution)/shard_map/ppermute | solution.py:544
  28.8 4.3 %collective-permute-start.5 = (bf16[144,128]{1,0:T(8,128)(2,1)S(1)}, bf16[144,128]{1,0:T(8,128)(2,1)S(1)}, u32[]{:S(2)}, u32[]{:S(2)}) collective-permute-start(bf16[144,128]{1,0:T(8,128)(2,1)S(1)} %get-tuple-element.38), channel_id=1, source_target_pairs={{0,2},{1,3},{2,0},{3,1},{4,6},{5,7},{6,4},{7,5},{8,10},{9,11},{10,... | collective-permute-start | bytes 110600 | tf_op jit(solution)/shard_map/ppermute | solution.py:544
  31.2 3.5 %collective-permute-start.6 = (bf16[144,128]{1,0:T(8,128)(2,1)S(1)}, bf16[144,128]{1,0:T(8,128)(2,1)S(1)}, u32[]{:S(2)}, u32[]{:S(2)}) collective-permute-start(bf16[144,128]{1,0:T(8,128)(2,1)S(1)} %get-tuple-element.39), channel_id=1, source_target_pairs={{0,3},{1,0},{2,1},{3,2},{4,7},{5,4},{6,5},{7,6},{8,11},{9,8},{10,9... | collective-permute-start | bytes 110600 | tf_op jit(solution)/shard_map/ppermute | solution.py:544
  34.7 56.7 %copy-start.3 = (f32[2,8,29568]{2,1,0:T(8,128)S(1)}, f32[2,8,29568]{2,1,0:T(8,128)}, u32[]{:S(2)}) copy-start(f32[2,8,29568]{2,1,0:T(8,128)} %gs.1) | copy-start | bytes 5677060
  34.7 56.7 %copy-start.4 = (bf16[1,2,8,29568]{3,2,1,0:T(8,128)(2,1)S(1)}, bf16[1,2,8,29568]{3,2,1,0:T(8,128)(2,1)}, u32[]{:S(2)}) copy-start(bf16[1,2,8,29568]{3,2,1,0:T(8,128)(2,1)} %param.11) | copy-start | bytes 2838532
  34.7 56.7 %copy-start.5 = (bf16[1,2,8,29568]{3,2,1,0:T(8,128)(2,1)S(1)}, bf16[1,2,8,29568]{3,2,1,0:T(8,128)(2,1)}, u32[]{:S(2)}) copy-start(bf16[1,2,8,29568]{3,2,1,0:T(8,128)(2,1)} %param.12) | copy-start | bytes 2838532
  89.0 13.6 %copy-start.7 = (f32[8,8192]{1,0:T(8,128)S(1)}, f32[8,8192]{1,0:T(8,128)}, u32[]{:S(2)}) copy-start(f32[8,8192]{1,0:T(8,128)} %ds.1) | copy-start | bytes 786436
  89.0 13.6 %copy-start.8 = (bf16[1,8,8192]{2,1,0:T(8,128)(2,1)S(1)}, bf16[1,8,8192]{2,1,0:T(8,128)(2,1)}, u32[]{:S(2)}) copy-start(bf16[1,8,8192]{2,1,0:T(8,128)(2,1)} %param.16) | copy-start | bytes 393220
  89.0 13.6 %copy-start.9 = (bf16[1,8,8192]{2,1,0:T(8,128)(2,1)S(1)}, bf16[1,8,8192]{2,1,0:T(8,128)(2,1)}, u32[]{:S(2)}) copy-start(bf16[1,8,8192]{2,1,0:T(8,128)(2,1)} %param.17) | copy-start | bytes 393220
  89.0 13.6 %copy-start.10 = (f32[8,8192]{1,0:T(8,128)S(1)}, f32[8,8192]{1,0:T(8,128)}, u32[]{:S(2)}) copy-start(f32[8,8192]{1,0:T(8,128)} %param.18) | copy-start | bytes 786436
  89.0 6.7 %collective-permute-start.9 = (bf16[736,128]{1,0:T(8,128)(2,1)S(1)}, bf16[736,128]{1,0:T(8,128)(2,1)S(1)}, u32[]{:S(2)}, u32[]{:S(2)}) collective-permute-start(bf16[736,128]{1,0:T(8,128)(2,1)S(1)} %shard_map.168.b0), channel_id=1, source_target_pairs={{0,192},{64,0},{128,64},{192,128},{1,193},{65,1},{129,65},{193,129... | collective-permute-start | bytes 565256 | tf_op jit(solution)/shard_map/ppermute | solution.py:544
  89.9 8.4 %collective-permute-start.8 = (bf16[736,128]{1,0:T(8,128)(2,1)S(1)}, bf16[736,128]{1,0:T(8,128)(2,1)S(1)}, u32[]{:S(2)}, u32[]{:S(2)}) collective-permute-start(bf16[736,128]{1,0:T(8,128)(2,1)S(1)} %shard_map.168.b0), channel_id=1, source_target_pairs={{0,128},{64,192},{128,0},{192,64},{1,129},{65,193},{129,1},{193,65... | collective-permute-start | bytes 565256 | tf_op jit(solution)/shard_map/ppermute | solution.py:544
  91.2 9.4 %collective-permute-start.7 = (bf16[736,128]{1,0:T(8,128)(2,1)S(1)}, bf16[736,128]{1,0:T(8,128)(2,1)S(1)}, u32[]{:S(2)}, u32[]{:S(2)}) collective-permute-start(bf16[736,128]{1,0:T(8,128)(2,1)S(1)} %shard_map.168.b0), channel_id=1, source_target_pairs={{0,64},{64,128},{128,192},{192,0},{1,65},{65,129},{129,193},{193,1... | collective-permute-start | bytes 565256 | tf_op jit(solution)/shard_map/ppermute | solution.py:544
  91.9 10.7 %collective-permute-start.10 = (bf16[736,128]{1,0:T(8,128)(2,1)S(1)}, bf16[736,128]{1,0:T(8,128)(2,1)S(1)}, u32[]{:S(2)}, u32[]{:S(2)}) collective-permute-start(bf16[736,128]{1,0:T(8,128)(2,1)S(1)} %shard_map.168.b0), channel_id=1, source_target_pairs={{0,32},{32,0},{1,33},{33,1},{2,34},{34,2},{3,35},{35,3},{4,36},{36... | collective-permute-start | bytes 565256 | tf_op jit(solution)/shard_map/ppermute | solution.py:548
  95.7 7.0 %collective-permute-start.13 = (bf16[736,128]{1,0:T(8,128)(2,1)S(1)}, bf16[736,128]{1,0:T(8,128)(2,1)S(1)}, u32[]{:S(2)}, u32[]{:S(2)}) collective-permute-start(bf16[736,128]{1,0:T(8,128)(2,1)S(1)} %collective-permute-done.9.b3), channel_id=1, source_target_pairs={{0,32},{32,0},{1,33},{33,1},{2,34},{34,2},{3,35},{35,3},{4,36},{36... | collective-permute-start | bytes 565256 | tf_op jit(solution)/shard_map/ppermute | solution.py:548
  98.3 4.4 %collective-permute-start.12 = (bf16[736,128]{1,0:T(8,128)(2,1)S(1)}, bf16[736,128]{1,0:T(8,128)(2,1)S(1)}, u32[]{:S(2)}, u32[]{:S(2)}) collective-permute-start(bf16[736,128]{1,0:T(8,128)(2,1)S(1)} %collective-permute-done.8.b2), channel_id=1, source_target_pairs={{0,32},{32,0},{1,33},{33,1},{2,34},{34,2},{3,35},{35,3},{4,36},{36... | collective-permute-start | bytes 565256 | tf_op jit(solution)/shard_map/ppermute | solution.py:548
  100.7 3.0 %collective-permute-start.11 = (bf16[736,128]{1,0:T(8,128)(2,1)S(1)}, bf16[736,128]{1,0:T(8,128)(2,1)S(1)}, u32[]{:S(2)}, u32[]{:S(2)}) collective-permute-start(bf16[736,128]{1,0:T(8,128)(2,1)S(1)} %collective-permute-done.7.b1), channel_id=1, source_target_pairs={{0,32},{32,0},{1,33},{33,1},{2,34},{34,2},{3,35},{35,3},{4,36},{36... | collective-permute-start | bytes 565256 | tf_op jit(solution)/shard_map/ppermute | solution.py:548

commit v5 on v4

--- a/solution.py
+++ b/solution.py
@@ -28,6 +28,7 @@
 
 
 LIGHT = pl.CostEstimate(flops=1, bytes_accessed=1, transcendentals=0)
+HEAVY = pl.CostEstimate(flops=10**13, bytes_accessed=10**11, transcendentals=0)
 
 
 def params(mib):
@@ -193,7 +194,7 @@
     )(gu, dn_t)
 
 
-def pair_kernel(own, came, zero, one, two, three):
+def pair_kernel(own, came, after, zero, one, two, three):
     y = lax.axis_index("y")
     for k, out in ((2, two), (1, one), (3, three), (0, zero)):
         to = 4 * lax.rem(y + k, 4)
@@ -202,7 +203,7 @@
             out[x] = total.astype(out.dtype)
 
 
-def pair_sums(own, came):
+def pair_sums(own, came, after):
     block = (4, X_ROWS, LANES)
     return pl.pallas_call(
         pair_kernel,
@@ -210,11 +211,11 @@
             jax.ShapeDtypeStruct(block, F32),
             *[jax.ShapeDtypeStruct(block, BF16)] * 3,
         ),
-        in_specs=[VMEM] * 2,
+        in_specs=[VMEM] * 2 + [ANY],
         out_specs=(VMEM,) * 4,
         compiler_params=params(16),
         cost_estimate=LIGHT,
-    )(own, came)
+    )(own, came, after)
 
 
 def y_sum_kernel(zero, one, two, three, x0, x1, x2, x3, sums):
@@ -236,6 +237,7 @@
         out_specs=(VMEM,) * 4,
         scratch_shapes=[pltpu.VMEM((4, X_ROWS, LANES), BF16)],
         compiler_params=params(16),
+        cost_estimate=HEAVY,
     )(zero, comes[1], comes[2], comes[3])
 
 
@@ -557,10 +559,11 @@
 ):
     gu_fast, gu_error = gu_fast[0], gu_error[0]
     dn_fast, dn_error = dn_fast[0], dn_error[0]
-    basis = exchange(basis_tiles(gu_basis, dn_basis.T), "z")
+    tiles = basis_tiles(gu_basis, dn_basis.T)
+    basis = exchange(tiles, "z")
     own, oth = lower(gu_slow, gu_fast, gu_error, dn_slow, dn_fast, dn_error)
     came = swap(oth)
-    zero, *sends = pair_sums(own, came)
+    zero, *sends = pair_sums(own, came, tiles)
     comes = {by: shift(sends[by - 1], "y", 4, by) for by in (2, 1, 3)}
     rows = list(y_sum(zero, comes))
     for by in (2, 1, 3):

time: 108 us -> 103 us (0.954)
  blocking collectives: 49.9 us -> 45.3 us
  waiting for transfers between devices: 9 us -> 7.27 us
  other arithmetic: 0.61 us -> 2.13 us
  starting transfers between devices: 32.7 us -> 31.2 us
  Pallas kernels: 13.1 us -> 14.3 us
    ppermute x9, waiting for transfers between devices: 8.05 us -> 0.02 us  [shift(): lax.ppermute(value, axis, [(i, (i + by) % size) for i in range(size)])]
    all_to_all x1, waiting for transfers between devices: 0.01 us -> 5.72 us  [exchange(): return lax.all_to_all(value, axis, 0, 0, tiled=False)]
    all_to_all x3, blocking collectives: 49.9 us -> 45.3 us  [exchange(): return lax.all_to_all(value, axis, 0, 0, tiled=False)]
    ppermute x9, starting transfers between devices: 12.3 us -> 10.6 us  [shift(): lax.ppermute(value, axis, [(i, (i + by) % size) for i in range(size)])]
    all_to_all x1, starting transfers between devices: 6.46 us -> 8.19 us  [exchange(): return lax.all_to_all(value, axis, 0, 0, tiled=False)]
    mul x2, other arithmetic: 0.61 us -> 2.13 us  [settled(): return (slow - MOMENT_GAIN * moment, combined, 0.9 * moment)]
    ppermute x5, starting transfers between devices: 14 us -> 12.5 us  [swap(): return lax.ppermute(value, 'core', [(0, 1), (1, 0)])]
    pallas_call x1, Pallas kernels: 0.35 us -> 1.47 us  [p_part(): pl.pallas_call(p_part_kernel, out_shape=(jax.ShapeDtypeStruct((8, 96, LAN...]
  transfers between devices with their start and end apart: 15 -> 15, of which waited for: 5 -> 3; matrix products, arithmetic and copies ran while one was open for 1% -> 2% of each run, Pallas kernels for 1% -> 1%
where the time goes in v5:
time: 103 us; the launch traced here: 102 us
  blocking collectives  45.3 us (44%)
  starting transfers between devices  31.2 us (30%)
  Pallas kernels  14.3 us (14%)
  waiting for transfers between devices  7.27 us (7%)
  other arithmetic  2.13 us (2%)
  local copies, waits for them, and re-layouts  1.12 us (1%)
    all_to_all x3, blocking collectives, exchange(): return lax.all_to_all(value, axis, 0, 0, tiled=False)  45.3 us
    ppermute x5, starting transfers between devices, swap(): return lax.ppermute(value, 'core', [(0, 1), (1, 0)])  12.5 us
    ppermute x9, starting transfers between devices, shift(): lax.ppermute(value, axis, [(i, (i + by) % size) for i in range(size)])  10.6 us
    all_to_all x1, starting transfers between devices, exchange(): return lax.all_to_all(value, axis, 0, 0, tiled=False)  8.19 us
    all_to_all x1, waiting for transfers between devices, exchange(): return lax.all_to_all(value, axis, 0, 0, tiled=False)  5.72 us
    pallas_call x1, Pallas kernels, factor(): pl.pallas_call(factor_kernel, out_shape=(jax.ShapeDtypeStruct((SHARDS, 24...  3.94 us
    pallas_call x1, Pallas kernels, lower(): pl.pallas_call(lower_kernel, out_shape=(shape, shape), in_specs=[HBM] * 6...  3.67 us
    pallas_call x1, Pallas kernels, finish(): pl.pallas_call(finish_kernel, out_shape=(*[jax.ShapeDtypeStruct(gu, kind)...  3.62 us
  transfers between devices with their start and end apart: 15, of which 3 were waited for; matrix products, arithmetic and copies ran while one was open for 2% of the time, Pallas kernels for 1%

profile of v5, /device:TPU:1, one launch (start us, length us, event | category | flops | bytes accessed | tf_op | source)
XLA Modules:
  0.0 102.3 jit_solution(14051974515130074768)
XLA Ops:
  0.7 3.7 %shard_map.161 = (bf16[16,144,128]{2,1,0:T(8,128)(2,1)}, bf16[16,144,128]{2,1,0:T(8,128)(2,1)}) custom-call(f32[2,8,29568]{2,1,0:T(8,128)} %gs.1, bf16[2,8,29568]{2,1,0:T(8,128)(2,1)} %bitcast.13, bf16[2,8,29568]{2,1,0:T(8,128)(2,1)} %bitcast.14, f32[8,8192]{1,0:T(8,128)} %ds.1, bf16[8,8192]{1,0:T(8,128)(2,1)} %bitcast.15, bf16[8,8192]{1,0:T(8,128)(2,1)} %bitcast.16), custom_call_target="tpu_custom_call" | custom-call | flops 1 | bytes 1 | tf_op jit(solution)/shard_map/pallas_call | solution.py:132
  4.3 3.3 %collective-permute-start = (bf16[16,144,128]{2,1,0:T(8,128)(2,1)}, bf16[16,144,128]{2,1,0:T(8,128)(2,1)S(1)}, u32[]{:S(2)}, u32[]{:S(2)}) collective-permute-start(bf16[16,144,128]{2,1,0:T(8,128)(2,1)} %get-tuple-element.31), channel_id=1, source_target_pairs={{0,32},{32,0},{1,33},{33,1},{2,34},{34,2},{3,35},{35,3},{4,36},{36... | collective-permute-start | bytes 1769480 | tf_op jit(solution)/shard_map/ppermute | solution.py:550
  7.7 1.3 %shard_map.162.after = bf16[8,144,128]{2,1,0:T(8,128)(2,1)} custom-call(bf16[924,128]{1,0:T(8,128)(2,1)S(1)} %copy-done.1, bf16[64,256]{1,0:T(8,128)(2,1)S(1)} %bitcast.12), custom_call_target="tpu_custom_call" | custom-call | tf_op jit(solution)/shard_map/pallas_call | solution.py:181
  8.9 0.6 collective-permute-done.came
  9.5 1.1 %copy-done = bf16[16,144,128]{2,1,0:T(8,128)(2,1)S(1)} copy-done((bf16[16,144,128]{2,1,0:T(8,128)(2,1)S(1)}, bf16[16,144,128]{2,1,0:T(8,128)(2,1)}, u32[]{:S(2)}) %copy-start) | copy-done | bytes 589848
  10.6 0.1 shard_map.163
  10.7 0.1 collective-permute-start.1
  10.8 2.2 %collective-permute-start.2 = (bf16[4,144,128]{2,1,0:T(8,128)(2,1)S(1)}, bf16[4,144,128]{2,1,0:T(8,128)(2,1)S(1)}, u32[]{:S(2)}, u32[]{:S(2)}) collective-permute-start(bf16[4,144,128]{2,1,0:T(8,128)(2,1)S(1)} %get-tuple-element.34), channel_id=1, source_target_pairs={{0,128},{64,192},{128,0},{192,64},{1,129},{65,193},{129,1},{193,65... | collective-permute-start | bytes 442376 | tf_op jit(solution)/shard_map/ppermute | solution.py:546
  13.0 1.1 %collective-permute-start.3 = (bf16[4,144,128]{2,1,0:T(8,128)(2,1)S(1)}, bf16[4,144,128]{2,1,0:T(8,128)(2,1)S(1)}, u32[]{:S(2)}, u32[]{:S(2)}) collective-permute-start(bf16[4,144,128]{2,1,0:T(8,128)(2,1)S(1)} %get-tuple-element.35), channel_id=1, source_target_pairs={{0,192},{64,0},{128,64},{192,128},{1,193},{65,1},{129,65},{193,129... | collective-permute-start | bytes 442376 | tf_op jit(solution)/shard_map/ppermute | solution.py:546
  14.0 8.2 %all-to-all-start = ((bf16[8,144,128]{2,1,0:T(8,128)(2,1)}), bf16[8,144,128]{2,1,0:T(8,128)(2,1)}, u32[]{:S(2)}, u32[]{:S(2)}) async-start(bf16[8,144,128]{2,1,0:T(8,128)(2,1)} %shard_map.162.after), calls=%async_computation | async-start | bytes 589824 | tf_op jit(solution)/shard_map/all_to_all | solution.py:554
  22.2 0.1 shard_map.164
  22.3 1.3 %collective-permute-start.4 = (bf16[144,128]{1,0:T(8,128)(2,1)S(1)}, bf16[144,128]{1,0:T(8,128)(2,1)S(1)}, u32[]{:S(2)}, u32[]{:S(2)}) collective-permute-start(bf16[144,128]{1,0:T(8,128)(2,1)S(1)} %get-tuple-element.37), channel_id=1, source_target_pairs={{0,1},{1,2},{2,3},{3,0},{4,5},{5,6},{6,7},{7,4},{8,9},{9,10},{10,1... | collective-permute-start | bytes 110600 | tf_op jit(solution)/shard_map/ppermute | solution.py:546
  23.6 2.5 %collective-permute-start.5 = (bf16[144,128]{1,0:T(8,128)(2,1)S(1)}, bf16[144,128]{1,0:T(8,128)(2,1)S(1)}, u32[]{:S(2)}, u32[]{:S(2)}) collective-permute-start(bf16[144,128]{1,0:T(8,128)(2,1)S(1)} %get-tuple-element.38), channel_id=1, source_target_pairs={{0,2},{1,3},{2,0},{3,1},{4,6},{5,7},{6,4},{7,5},{8,10},{9,11},{10,... | collective-permute-start | bytes 110600 | tf_op jit(solution)/shard_map/ppermute | solution.py:546
  26.1 1.2 %collective-permute-start.6 = (bf16[144,128]{1,0:T(8,128)(2,1)S(1)}, bf16[144,128]{1,0:T(8,128)(2,1)S(1)}, u32[]{:S(2)}, u32[]{:S(2)}) collective-permute-start(bf16[144,128]{1,0:T(8,128)(2,1)S(1)} %get-tuple-element.39), channel_id=1, source_target_pairs={{0,3},{1,0},{2,1},{3,2},{4,7},{5,4},{6,5},{7,6},{8,11},{9,8},{10,9... | collective-permute-start | bytes 110600 | tf_op jit(solution)/shard_map/ppermute | solution.py:546
  27.2 5.7 %all-to-all-done.basis = bf16[8,144,128]{2,1,0:T(8,128)(2,1)} async-done(((bf16[8,144,128]{2,1,0:T(8,128)(2,1)}), bf16[8,144,128]{2,1,0:T(8,128)(2,1)}, u32[]{:S(2)}, u32[]{:S(2)}) %all-to-all-start) | async-done | bytes 294944 | tf_op jit(solution)/shard_map/all_to_all | solution.py:554
  33.0 1.5 %shard_map.165 = (bf16[8,96,128]{2,1,0:T(8,128)(2,1)S(1)}, bf16[32,48,128]{2,1,0:T(8,128)(2,1)S(1)}) custom-call(bf16[144,128]{1,0:T(8,128)(2,1)S(1)} %get-tuple-element.36.l0, bf16[144,128]{1,0:T(8,128)(2,1)S(1)} %collective-permute-done.4.l1, bf16[144,128]{1,0:T(8,128)(2,1)S(1)} %collective-permute-done.5.l2, ...), custom_call_target="tpu_custom_call" | custom-call | tf_op jit(solution)/shard_map/pallas_call | solution.py:293
  34.5 17.4 %all_to_all.20.ps = bf16[32,48,128]{2,1,0:T(8,128)(2,1)S(1)} all-to-all(bf16[32,48,128]{2,1,0:T(8,128)(2,1)S(1)} %get-tuple-element.40), channel_id=1, replica_groups=mesh['y'=4,'core'=2,'z'=8,'x'=4] {'y','core','x'}, dimensions={0} | all-to-all | bytes 786432 | tf_op jit(solution)/shard_map/all_to_all | solution.py:554
  51.9 0.1 shard_map.166
  52.0 14.9 %all_to_all.21.recv = bf16[8,144,128]{2,1,0:T(8,128)(2,1)S(1)} all-to-all(bf16[8,144,128]{2,1,0:T(8,128)(2,1)S(1)} %shard_map.166), channel_id=1, replica_groups=mesh['y'=4,'core'=2,'z'=8,'x'=4] {'z'}, dimensions={0} | all-to-all | bytes 589824 | tf_op jit(solution)/shard_map/all_to_all | solution.py:554
  66.9 3.9 %shard_map.167 = (bf16[32,24,128]{2,1,0:T(8,128)(2,1)S(1)}, bf16[160,128]{1,0:T(8,128)(2,1)S(1)}) custom-call(bf16[8,144,128]{2,1,0:T(8,128)(2,1)S(1)} %all_to_all.21.recv), custom_call_target="tpu_custom_call" | custom-call | tf_op jit(solution)/shard_map/pallas_call | solution.py:407
  70.9 13.0 %all_to_all.22.rows = bf16[32,24,128]{2,1,0:T(8,128)(2,1)S(1)} all-to-all(bf16[32,24,128]{2,1,0:T(8,128)(2,1)S(1)} %get-tuple-element.42), channel_id=1, replica_groups=mesh['y'=4,'core'=2,'z'=8,'x'=4] {'z','x'}, dimensions={0} | all-to-all | bytes 393216 | tf_op jit(solution)/shard_map/all_to_all | solution.py:554
  83.9 0.9 collective-permute-start.9
  84.8 1.3 %collective-permute-start.8 = (bf16[736,128]{1,0:T(8,128)(2,1)S(1)}, bf16[736,128]{1,0:T(8,128)(2,1)S(1)}, u32[]{:S(2)}, u32[]{:S(2)}) collective-permute-start(bf16[736,128]{1,0:T(8,128)(2,1)S(1)} %shard_map.168.b0), channel_id=1, source_target_pairs={{0,128},{64,192},{128,0},{192,64},{1,129},{65,193},{129,1},{193,65... | collective-permute-start | bytes 565256 | tf_op jit(solution)/shard_map/ppermute | solution.py:546
  86.1 0.2 collective-permute-start.7
  86.3 2.0 %broadcast_multiply_fusion = (f32[2,8,29568]{2,1,0:T(8,128)S(1)}, f32[2,8,29568]{2,1,0:T(8,128)S(1)}, f32[2,8,29568]{2,1,0:T(8,128)S(1)}) fusion(f32[2,8,29568]{2,1,0:T(8,128)} %param.13, f32[2,8,29568]{2,1,0:T(8,128)S(1)} %copy-done.3, bf16[1,2,8,29568]{3,2,1,0:T(8,128)(2,1)S(1)} %copy-done.5, bf16[1,2,8,29568]{3,2,1,0:T(8,128)(2,1)S(1)} %copy-done.4), kind=kLoop, calls=%fused_computation.2 | loop fusion | flops 3311616 | bytes 11354112 | tf_op jit(solution)/shard_map/mul | solution.py:542
  88.3 3.7 %collective-permute-start.10 = (bf16[736,128]{1,0:T(8,128)(2,1)S(1)}, bf16[736,128]{1,0:T(8,128)(2,1)S(1)}, u32[]{:S(2)}, u32[]{:S(2)}) collective-permute-start(bf16[736,128]{1,0:T(8,128)(2,1)S(1)} %shard_map.168.b0), channel_id=1, source_target_pairs={{0,32},{32,0},{1,33},{33,1},{2,34},{34,2},{3,35},{35,3},{4,36},{36... | collective-permute-start | bytes 565256 | tf_op jit(solution)/shard_map/ppermute | solution.py:550
  92.1 1.1 %collective-permute-start.13 = (bf16[736,128]{1,0:T(8,128)(2,1)S(1)}, bf16[736,128]{1,0:T(8,128)(2,1)S(1)}, u32[]{:S(2)}, u32[]{:S(2)}) collective-permute-start(bf16[736,128]{1,0:T(8,128)(2,1)S(1)} %collective-permute-done.9.b3), channel_id=1, source_target_pairs={{0,32},{32,0},{1,33},{33,1},{2,34},{34,2},{3,35},{35,3},{4,36},{36... | collective-permute-start | bytes 565256 | tf_op jit(solution)/shard_map/ppermute | solution.py:550
  93.2 2.4 %collective-permute-start.12 = (bf16[736,128]{1,0:T(8,128)(2,1)S(1)}, bf16[736,128]{1,0:T(8,128)(2,1)S(1)}, u32[]{:S(2)}, u32[]{:S(2)}) collective-permute-start(bf16[736,128]{1,0:T(8,128)(2,1)S(1)} %collective-permute-done.8.b2), channel_id=1, source_target_pairs={{0,32},{32,0},{1,33},{33,1},{2,34},{34,2},{3,35},{35,3},{4,36},{36... | collective-permute-start | bytes 565256 | tf_op jit(solution)/shard_map/ppermute | solution.py:550
  95.6 1.9 %collective-permute-start.11 = (bf16[736,128]{1,0:T(8,128)(2,1)S(1)}, bf16[736,128]{1,0:T(8,128)(2,1)S(1)}, u32[]{:S(2)}, u32[]{:S(2)}) collective-permute-start(bf16[736,128]{1,0:T(8,128)(2,1)S(1)} %collective-permute-done.7.b1), channel_id=1, source_target_pairs={{0,32},{32,0},{1,33},{33,1},{2,34},{34,2},{3,35},{35,3},{4,36},{36... | collective-permute-start | bytes 565256 | tf_op jit(solution)/shard_map/ppermute | solution.py:550
  97.5 0.1 broadcast_multiply_fusion.1
  97.6 0.9 collective-permute-done.11.b5
  98.5 3.6 %shard_map.169 = (f32[2,8,29568]{2,1,0:T(8,128)}, bf16[2,8,29568]{2,1,0:T(8,128)(2,1)}, f32[2,8,29568]{2,1,0:T(8,128)}, f32[8,8192]{1,0:T(8,128)}, bf16[8,8192]{...) custom-call(bf16[736,128]{1,0:T(8,128)(2,1)S(1)} %shard_map.168.b0, ...), custom_call_target="tpu_custom_call" | custom-call | tf_op jit(solution)/shard_map/pallas_call | solution.py:514
  (32 shorter events, 0.1 us)
Async XLA Ops:
  0.6 7.0 %copy-start.1 = (bf16[924,128]{1,0:T(8,128)(2,1)S(1)}, bf16[924,128]{1,0:T(8,128)(2,1)}, u32[]{:S(2)}) copy-start(bf16[924,128]{1,0:T(8,128)(2,1)} %gu_any.1) | copy-start | bytes 709636
  0.6 7.0 %copy-start.2 = (bf16[256,64]{0,1:T(8,128)(2,1)S(1)}, bf16[256,64]{0,1:T(8,128)(2,1)}, u32[]{:S(2)}) copy-start(bf16[256,64]{0,1:T(8,128)(2,1)} %param.19) | copy-start | bytes 98308
  4.3 5.2 %collective-permute-start = (bf16[16,144,128]{2,1,0:T(8,128)(2,1)}, bf16[16,144,128]{2,1,0:T(8,128)(2,1)S(1)}, u32[]{:S(2)}, u32[]{:S(2)}) collective-permute-start(bf16[16,144,128]{2,1,0:T(8,128)(2,1)} %get-tuple-element.31), channel_id=1, source_target_pairs={{0,32},{32,0},{1,33},{33,1},{2,34},{34,2},{3,35},{35,3},{4,36},{36... | collective-permute-start | bytes 1769480 | tf_op jit(solution)/shard_map/ppermute | solution.py:550
  9.5 1.1 %copy-start = (bf16[16,144,128]{2,1,0:T(8,128)(2,1)S(1)}, bf16[16,144,128]{2,1,0:T(8,128)(2,1)}, u32[]{:S(2)}) copy-start(bf16[16,144,128]{2,1,0:T(8,128)(2,1)} %get-tuple-element.30.own) | copy-start | bytes 1769476
  10.7 11.5 %collective-permute-start.1 = (bf16[4,144,128]{2,1,0:T(8,128)(2,1)S(1)}, bf16[4,144,128]{2,1,0:T(8,128)(2,1)S(1)}, u32[]{:S(2)}, u32[]{:S(2)}) collective-permute-start(bf16[4,144,128]{2,1,0:T(8,128)(2,1)S(1)} %get-tuple-element.33), channel_id=1, source_target_pairs={{0,64},{64,128},{128,192},{192,0},{1,65},{65,129},{129,193},{193,1... | collective-permute-start | bytes 442376 | tf_op jit(solution)/shard_map/ppermute | solution.py:546
  10.8 11.4 %collective-permute-start.2 = (bf16[4,144,128]{2,1,0:T(8,128)(2,1)S(1)}, bf16[4,144,128]{2,1,0:T(8,128)(2,1)S(1)}, u32[]{:S(2)}, u32[]{:S(2)}) collective-permute-start(bf16[4,144,128]{2,1,0:T(8,128)(2,1)S(1)} %get-tuple-element.34), channel_id=1, source_target_pairs={{0,128},{64,192},{128,0},{192,64},{1,129},{65,193},{129,1},{193,65... | collective-permute-start | bytes 442376 | tf_op jit(solution)/shard_map/ppermute | solution.py:546
  13.0 9.3 %collective-permute-start.3 = (bf16[4,144,128]{2,1,0:T(8,128)(2,1)S(1)}, bf16[4,144,128]{2,1,0:T(8,128)(2,1)S(1)}, u32[]{:S(2)}, u32[]{:S(2)}) collective-permute-start(bf16[4,144,128]{2,1,0:T(8,128)(2,1)S(1)} %get-tuple-element.35), channel_id=1, source_target_pairs={{0,192},{64,0},{128,64},{192,128},{1,193},{65,1},{129,65},{193,129... | collective-permute-start | bytes 442376 | tf_op jit(solution)/shard_map/ppermute | solution.py:546
  14.0 18.9 %all-to-all-start = ((bf16[8,144,128]{2,1,0:T(8,128)(2,1)}), bf16[8,144,128]{2,1,0:T(8,128)(2,1)}, u32[]{:S(2)}, u32[]{:S(2)}) async-start(bf16[8,144,128]{2,1,0:T(8,128)(2,1)} %shard_map.162.after), calls=%async_computation | async-start | bytes 589824 | tf_op jit(solution)/shard_map/all_to_all | solution.py:554
  22.3 10.6 %collective-permute-start.4 = (bf16[144,128]{1,0:T(8,128)(2,1)S(1)}, bf16[144,128]{1,0:T(8,128)(2,1)S(1)}, u32[]{:S(2)}, u32[]{:S(2)}) collective-permute-start(bf16[144,128]{1,0:T(8,128)(2,1)S(1)} %get-tuple-element.37), channel_id=1, source_target_pairs={{0,1},{1,2},{2,3},{3,0},{4,5},{5,6},{6,7},{7,4},{8,9},{9,10},{10,1... | collective-permute-start | bytes 110600 | tf_op jit(solution)/shard_map/ppermute | solution.py:546
  23.6 9.3 %collective-permute-start.5 = (bf16[144,128]{1,0:T(8,128)(2,1)S(1)}, bf16[144,128]{1,0:T(8,128)(2,1)S(1)}, u32[]{:S(2)}, u32[]{:S(2)}) collective-permute-start(bf16[144,128]{1,0:T(8,128)(2,1)S(1)} %get-tuple-element.38), channel_id=1, source_target_pairs={{0,2},{1,3},{2,0},{3,1},{4,6},{5,7},{6,4},{7,5},{8,10},{9,11},{10,... | collective-permute-start | bytes 110600 | tf_op jit(solution)/shard_map/ppermute | solution.py:546
  26.1 6.9 %collective-permute-start.6 = (bf16[144,128]{1,0:T(8,128)(2,1)S(1)}, bf16[144,128]{1,0:T(8,128)(2,1)S(1)}, u32[]{:S(2)}, u32[]{:S(2)}) collective-permute-start(bf16[144,128]{1,0:T(8,128)(2,1)S(1)} %get-tuple-element.39), channel_id=1, source_target_pairs={{0,3},{1,0},{2,1},{3,2},{4,7},{5,4},{6,5},{7,6},{8,11},{9,8},{10,9... | collective-permute-start | bytes 110600 | tf_op jit(solution)/shard_map/ppermute | solution.py:546
  33.0 53.3 %copy-start.3 = (f32[2,8,29568]{2,1,0:T(8,128)S(1)}, f32[2,8,29568]{2,1,0:T(8,128)}, u32[]{:S(2)}) copy-start(f32[2,8,29568]{2,1,0:T(8,128)} %gs.1) | copy-start | bytes 5677060
  33.0 53.3 %copy-start.4 = (bf16[1,2,8,29568]{3,2,1,0:T(8,128)(2,1)S(1)}, bf16[1,2,8,29568]{3,2,1,0:T(8,128)(2,1)}, u32[]{:S(2)}) copy-start(bf16[1,2,8,29568]{3,2,1,0:T(8,128)(2,1)} %param.11) | copy-start | bytes 2838532
  33.0 53.3 %copy-start.5 = (bf16[1,2,8,29568]{3,2,1,0:T(8,128)(2,1)S(1)}, bf16[1,2,8,29568]{3,2,1,0:T(8,128)(2,1)}, u32[]{:S(2)}) copy-start(bf16[1,2,8,29568]{3,2,1,0:T(8,128)(2,1)} %param.12) | copy-start | bytes 2838532
  83.9 13.6 %copy-start.6 = (f32[8,8192]{1,0:T(8,128)S(1)}, f32[8,8192]{1,0:T(8,128)}, u32[]{:S(2)}) copy-start(f32[8,8192]{1,0:T(8,128)} %ds.1) | copy-start | bytes 786436
  83.9 13.6 %copy-start.7 = (bf16[1,8,8192]{2,1,0:T(8,128)(2,1)S(1)}, bf16[1,8,8192]{2,1,0:T(8,128)(2,1)}, u32[]{:S(2)}) copy-start(bf16[1,8,8192]{2,1,0:T(8,128)(2,1)} %param.16) | copy-start | bytes 393220
  83.9 13.6 %copy-start.8 = (bf16[1,8,8192]{2,1,0:T(8,128)(2,1)S(1)}, bf16[1,8,8192]{2,1,0:T(8,128)(2,1)}, u32[]{:S(2)}) copy-start(bf16[1,8,8192]{2,1,0:T(8,128)(2,1)} %param.17) | copy-start | bytes 393220
  83.9 13.6 %copy-start.9 = (f32[8,8192]{1,0:T(8,128)S(1)}, f32[8,8192]{1,0:T(8,128)}, u32[]{:S(2)}) copy-start(f32[8,8192]{1,0:T(8,128)} %param.18) | copy-start | bytes 786436
  83.9 8.2 %collective-permute-start.9 = (bf16[736,128]{1,0:T(8,128)(2,1)S(1)}, bf16[736,128]{1,0:T(8,128)(2,1)S(1)}, u32[]{:S(2)}, u32[]{:S(2)}) collective-permute-start(bf16[736,128]{1,0:T(8,128)(2,1)S(1)} %shard_map.168.b0), channel_id=1, source_target_pairs={{0,192},{64,0},{128,64},{192,128},{1,193},{65,1},{129,65},{193,129... | collective-permute-start | bytes 565256 | tf_op jit(solution)/shard_map/ppermute | solution.py:546
  84.8 8.4 %collective-permute-start.8 = (bf16[736,128]{1,0:T(8,128)(2,1)S(1)}, bf16[736,128]{1,0:T(8,128)(2,1)S(1)}, u32[]{:S(2)}, u32[]{:S(2)}) collective-permute-start(bf16[736,128]{1,0:T(8,128)(2,1)S(1)} %shard_map.168.b0), channel_id=1, source_target_pairs={{0,128},{64,192},{128,0},{192,64},{1,129},{65,193},{129,1},{193,65... | collective-permute-start | bytes 565256 | tf_op jit(solution)/shard_map/ppermute | solution.py:546
  86.1 9.4 %collective-permute-start.7 = (bf16[736,128]{1,0:T(8,128)(2,1)S(1)}, bf16[736,128]{1,0:T(8,128)(2,1)S(1)}, u32[]{:S(2)}, u32[]{:S(2)}) collective-permute-start(bf16[736,128]{1,0:T(8,128)(2,1)S(1)} %shard_map.168.b0), channel_id=1, source_target_pairs={{0,64},{64,128},{128,192},{192,0},{1,65},{65,129},{129,193},{193,1... | collective-permute-start | bytes 565256 | tf_op jit(solution)/shard_map/ppermute | solution.py:546
  88.3 9.2 %collective-permute-start.10 = (bf16[736,128]{1,0:T(8,128)(2,1)S(1)}, bf16[736,128]{1,0:T(8,128)(2,1)S(1)}, u32[]{:S(2)}, u32[]{:S(2)}) collective-permute-start(bf16[736,128]{1,0:T(8,128)(2,1)S(1)} %shard_map.168.b0), channel_id=1, source_target_pairs={{0,32},{32,0},{1,33},{33,1},{2,34},{34,2},{3,35},{35,3},{4,36},{36... | collective-permute-start | bytes 565256 | tf_op jit(solution)/shard_map/ppermute | solution.py:550
  92.1 5.5 %collective-permute-start.13 = (bf16[736,128]{1,0:T(8,128)(2,1)S(1)}, bf16[736,128]{1,0:T(8,128)(2,1)S(1)}, u32[]{:S(2)}, u32[]{:S(2)}) collective-permute-start(bf16[736,128]{1,0:T(8,128)(2,1)S(1)} %collective-permute-done.9.b3), channel_id=1, source_target_pairs={{0,32},{32,0},{1,33},{33,1},{2,34},{34,2},{3,35},{35,3},{4,36},{36... | collective-permute-start | bytes 565256 | tf_op jit(solution)/shard_map/ppermute | solution.py:550
  93.2 4.4 %collective-permute-start.12 = (bf16[736,128]{1,0:T(8,128)(2,1)S(1)}, bf16[736,128]{1,0:T(8,128)(2,1)S(1)}, u32[]{:S(2)}, u32[]{:S(2)}) collective-permute-start(bf16[736,128]{1,0:T(8,128)(2,1)S(1)} %collective-permute-done.8.b2), channel_id=1, source_target_pairs={{0,32},{32,0},{1,33},{33,1},{2,34},{34,2},{3,35},{35,3},{4,36},{36... | collective-permute-start | bytes 565256 | tf_op jit(solution)/shard_map/ppermute | solution.py:550
  95.6 3.0 %collective-permute-start.11 = (bf16[736,128]{1,0:T(8,128)(2,1)S(1)}, bf16[736,128]{1,0:T(8,128)(2,1)S(1)}, u32[]{:S(2)}, u32[]{:S(2)}) collective-permute-start(bf16[736,128]{1,0:T(8,128)(2,1)S(1)} %collective-permute-done.7.b1), channel_id=1, source_target_pairs={{0,32},{32,0},{1,33},{33,1},{2,34},{34,2},{3,35},{35,3},{4,36},{36... | collective-permute-start | bytes 565256 | tf_op jit(solution)/shard_map/ppermute | solution.py:550

commit v6 on v5

--- a/solution.py
+++ b/solution.py
@@ -28,7 +28,7 @@
 
 
 LIGHT = pl.CostEstimate(flops=1, bytes_accessed=1, transcendentals=0)
-HEAVY = pl.CostEstimate(flops=10**13, bytes_accessed=10**11, transcendentals=0)
+HEAVY = pl.CostEstimate(flops=3 * 10**10, bytes_accessed=10**8, transcendentals=0)
 
 
 def params(mib):

time: 103 us -> 102 us (level)
  other arithmetic: 2.13 us -> 0.6 us
  starting transfers between devices: 31.2 us -> 32.7 us
  Pallas kernels: 14.3 us -> 13.1 us
    mul x2, other arithmetic: 2.13 us -> 0.6 us  [settled(): return (slow - MOMENT_GAIN * moment, combined, 0.9 * moment)]
    ppermute x5, starting transfers between devices: 12.5 us -> 14 us  [swap(): return lax.ppermute(value, 'core', [(0, 1), (1, 0)])]
    pallas_call x1, Pallas kernels: 1.47 us -> 0.35 us  [p_part(): pl.pallas_call(p_part_kernel, out_shape=(jax.ShapeDtypeStruct((8, 96, LAN...]
  transfers between devices with their start and end apart: 15 -> 15, of which waited for: 3 -> 3; matrix products, arithmetic and copies ran while one was open for 2% -> 1% of each run, Pallas kernels for 1% -> 1%
where the time goes in v6:
time: 102 us; the launch traced here: 101 us
  blocking collectives  45.6 us (45%)
  starting transfers between devices  32.7 us (32%)
  Pallas kernels  13.1 us (13%)
  waiting for transfers between devices  7.15 us (7%)
  local copies, waits for them, and re-layouts  1.12 us (1%)
    all_to_all x3, blocking collectives, exchange(): return lax.all_to_all(value, axis, 0, 0, tiled=False)  45.6 us
    ppermute x5, starting transfers between devices, swap(): return lax.ppermute(value, 'core', [(0, 1), (1, 0)])  14 us
    ppermute x9, starting transfers between devices, shift(): lax.ppermute(value, axis, [(i, (i + by) % size) for i in range(size)])  10.6 us
    all_to_all x1, starting transfers between devices, exchange(): return lax.all_to_all(value, axis, 0, 0, tiled=False)  8.19 us
    all_to_all x1, waiting for transfers between devices, exchange(): return lax.all_to_all(value, axis, 0, 0, tiled=False)  5.61 us
    pallas_call x1, Pallas kernels, factor(): pl.pallas_call(factor_kernel, out_shape=(jax.ShapeDtypeStruct((SHARDS, 24...  3.94 us
    pallas_call x1, Pallas kernels, lower(): pl.pallas_call(lower_kernel, out_shape=(shape, shape), in_specs=[HBM] * 6...  3.67 us
    pallas_call x1, Pallas kernels, finish(): pl.pallas_call(finish_kernel, out_shape=(*[jax.ShapeDtypeStruct(gu, kind)...  3.62 us
  transfers between devices with their start and end apart: 15, of which 3 were waited for; matrix products, arithmetic and copies ran while one was open for 1% of the time, Pallas kernels for 1%

profile of v6, /device:TPU:1, one launch (start us, length us, event | category | flops | bytes accessed | tf_op | source)
XLA Modules:
  0.0 101.3 jit_solution(9902967159552729360)
XLA Ops:
  0.7 3.7 %shard_map.161 = (bf16[16,144,128]{2,1,0:T(8,128)(2,1)}, bf16[16,144,128]{2,1,0:T(8,128)(2,1)}) custom-call(f32[2,8,29568]{2,1,0:T(8,128)} %gs.1, bf16[2,8,29568]{2,1,0:T(8,128)(2,1)} %bitcast.13, bf16[2,8,29568]{2,1,0:T(8,128)(2,1)} %bitcast.14, f32[8,8192]{1,0:T(8,128)} %ds.1, bf16[8,8192]{1,0:T(8,128)(2,1)} %bitcast.15, bf16[8,8192]{1,0:T(8,128)(2,1)} %bitcast.16), custom_call_target="tpu_custom_call" | custom-call | flops 1 | bytes 1 | tf_op jit(solution)/shard_map/pallas_call | solution.py:132
  4.3 3.3 %collective-permute-start = (bf16[16,144,128]{2,1,0:T(8,128)(2,1)}, bf16[16,144,128]{2,1,0:T(8,128)(2,1)S(1)}, u32[]{:S(2)}, u32[]{:S(2)}) collective-permute-start(bf16[16,144,128]{2,1,0:T(8,128)(2,1)} %get-tuple-element.31), channel_id=1, source_target_pairs={{0,32},{32,0},{1,33},{33,1},{2,34},{34,2},{3,35},{35,3},{4,36},{36... | collective-permute-start | bytes 1769480 | tf_op jit(solution)/shard_map/ppermute | solution.py:550
  7.7 1.3 %shard_map.162.after = bf16[8,144,128]{2,1,0:T(8,128)(2,1)} custom-call(bf16[924,128]{1,0:T(8,128)(2,1)S(1)} %copy-done.1, bf16[64,256]{1,0:T(8,128)(2,1)S(1)} %bitcast.12), custom_call_target="tpu_custom_call" | custom-call | tf_op jit(solution)/shard_map/pallas_call | solution.py:181
  8.9 0.6 collective-permute-done.came
  9.5 1.1 %copy-done = bf16[16,144,128]{2,1,0:T(8,128)(2,1)S(1)} copy-done((bf16[16,144,128]{2,1,0:T(8,128)(2,1)S(1)}, bf16[16,144,128]{2,1,0:T(8,128)(2,1)}, u32[]{:S(2)}) %copy-start) | copy-done | bytes 589848
  10.6 0.1 shard_map.163
  10.7 0.1 collective-permute-start.1
  10.8 2.2 %collective-permute-start.2 = (bf16[4,144,128]{2,1,0:T(8,128)(2,1)S(1)}, bf16[4,144,128]{2,1,0:T(8,128)(2,1)S(1)}, u32[]{:S(2)}, u32[]{:S(2)}) collective-permute-start(bf16[4,144,128]{2,1,0:T(8,128)(2,1)S(1)} %get-tuple-element.34), channel_id=1, source_target_pairs={{0,128},{64,192},{128,0},{192,64},{1,129},{65,193},{129,1},{193,65... | collective-permute-start | bytes 442376 | tf_op jit(solution)/shard_map/ppermute | solution.py:546
  13.0 1.1 %collective-permute-start.3 = (bf16[4,144,128]{2,1,0:T(8,128)(2,1)S(1)}, bf16[4,144,128]{2,1,0:T(8,128)(2,1)S(1)}, u32[]{:S(2)}, u32[]{:S(2)}) collective-permute-start(bf16[4,144,128]{2,1,0:T(8,128)(2,1)S(1)} %get-tuple-element.35), channel_id=1, source_target_pairs={{0,192},{64,0},{128,64},{192,128},{1,193},{65,1},{129,65},{193,129... | collective-permute-start | bytes 442376 | tf_op jit(solution)/shard_map/ppermute | solution.py:546
  14.0 8.2 %all-to-all-start = ((bf16[8,144,128]{2,1,0:T(8,128)(2,1)}), bf16[8,144,128]{2,1,0:T(8,128)(2,1)S(1)}, u32[]{:S(2)}, u32[]{:S(2)}) async-start(bf16[8,144,128]{2,1,0:T(8,128)(2,1)} %shard_map.162.after), calls=%async_computation | async-start | bytes 589824 | tf_op jit(solution)/shard_map/all_to_all | solution.py:554
  22.3 0.1 shard_map.164
  22.3 1.3 %collective-permute-start.4 = (bf16[144,128]{1,0:T(8,128)(2,1)S(1)}, bf16[144,128]{1,0:T(8,128)(2,1)S(1)}, u32[]{:S(2)}, u32[]{:S(2)}) collective-permute-start(bf16[144,128]{1,0:T(8,128)(2,1)S(1)} %get-tuple-element.37), channel_id=1, source_target_pairs={{0,1},{1,2},{2,3},{3,0},{4,5},{5,6},{6,7},{7,4},{8,9},{9,10},{10,1... | collective-permute-start | bytes 110600 | tf_op jit(solution)/shard_map/ppermute | solution.py:546
  23.6 2.5 %collective-permute-start.5 = (bf16[144,128]{1,0:T(8,128)(2,1)S(1)}, bf16[144,128]{1,0:T(8,128)(2,1)S(1)}, u32[]{:S(2)}, u32[]{:S(2)}) collective-permute-start(bf16[144,128]{1,0:T(8,128)(2,1)S(1)} %get-tuple-element.38), channel_id=1, source_target_pairs={{0,2},{1,3},{2,0},{3,1},{4,6},{5,7},{6,4},{7,5},{8,10},{9,11},{10,... | collective-permute-start | bytes 110600 | tf_op jit(solution)/shard_map/ppermute | solution.py:546
  26.1 1.2 %collective-permute-start.6 = (bf16[144,128]{1,0:T(8,128)(2,1)S(1)}, bf16[144,128]{1,0:T(8,128)(2,1)S(1)}, u32[]{:S(2)}, u32[]{:S(2)}) collective-permute-start(bf16[144,128]{1,0:T(8,128)(2,1)S(1)} %get-tuple-element.39), channel_id=1, source_target_pairs={{0,3},{1,0},{2,1},{3,2},{4,7},{5,4},{6,5},{7,6},{8,11},{9,8},{10,9... | collective-permute-start | bytes 110600 | tf_op jit(solution)/shard_map/ppermute | solution.py:546
  27.2 5.6 %all-to-all-done.basis = bf16[8,144,128]{2,1,0:T(8,128)(2,1)S(1)} async-done(((bf16[8,144,128]{2,1,0:T(8,128)(2,1)}), bf16[8,144,128]{2,1,0:T(8,128)(2,1)S(1)}, u32[]{:S(2)}, u32[]{:S(2)}) %all-to-all-start) | async-done | bytes 294944 | tf_op jit(solution)/shard_map/all_to_all | solution.py:554
  32.9 0.4 shard_map.165
  33.3 17.6 %all_to_all.20.ps = bf16[32,48,128]{2,1,0:T(8,128)(2,1)S(1)} all-to-all(bf16[32,48,128]{2,1,0:T(8,128)(2,1)S(1)} %get-tuple-element.40), channel_id=1, replica_groups=mesh['y'=4,'core'=2,'z'=8,'x'=4] {'y','core','x'}, dimensions={0} | all-to-all | bytes 786432 | tf_op jit(solution)/shard_map/all_to_all | solution.py:554
  50.8 0.1 shard_map.166
  50.9 15.0 %all_to_all.21.recv = bf16[8,144,128]{2,1,0:T(8,128)(2,1)S(1)} all-to-all(bf16[8,144,128]{2,1,0:T(8,128)(2,1)S(1)} %shard_map.166), channel_id=1, replica_groups=mesh['y'=4,'core'=2,'z'=8,'x'=4] {'z'}, dimensions={0} | all-to-all | bytes 589824 | tf_op jit(solution)/shard_map/all_to_all | solution.py:554
  65.9 3.9 %shard_map.167 = (bf16[32,24,128]{2,1,0:T(8,128)(2,1)S(1)}, bf16[160,128]{1,0:T(8,128)(2,1)S(1)}) custom-call(bf16[8,144,128]{2,1,0:T(8,128)(2,1)S(1)} %all_to_all.21.recv), custom_call_target="tpu_custom_call" | custom-call | tf_op jit(solution)/shard_map/pallas_call | solution.py:407
  69.9 13.0 %all_to_all.22.rows = bf16[32,24,128]{2,1,0:T(8,128)(2,1)S(1)} all-to-all(bf16[32,24,128]{2,1,0:T(8,128)(2,1)S(1)} %get-tuple-element.42), channel_id=1, replica_groups=mesh['y'=4,'core'=2,'z'=8,'x'=4] {'z','x'}, dimensions={0} | all-to-all | bytes 393216 | tf_op jit(solution)/shard_map/all_to_all | solution.py:554
  82.9 0.9 collective-permute-start.9
  83.8 1.3 %collective-permute-start.8 = (bf16[736,128]{1,0:T(8,128)(2,1)S(1)}, bf16[736,128]{1,0:T(8,128)(2,1)S(1)}, u32[]{:S(2)}, u32[]{:S(2)}) collective-permute-start(bf16[736,128]{1,0:T(8,128)(2,1)S(1)} %shard_map.168.b0), channel_id=1, source_target_pairs={{0,128},{64,192},{128,0},{192,64},{1,129},{65,193},{129,1},{193,65... | collective-permute-start | bytes 565256 | tf_op jit(solution)/shard_map/ppermute | solution.py:546
  85.1 0.2 collective-permute-start.7
  85.3 0.5 broadcast_multiply_fusion
  85.8 3.7 %collective-permute-start.10 = (bf16[736,128]{1,0:T(8,128)(2,1)S(1)}, bf16[736,128]{1,0:T(8,128)(2,1)S(1)}, u32[]{:S(2)}, u32[]{:S(2)}) collective-permute-start(bf16[736,128]{1,0:T(8,128)(2,1)S(1)} %shard_map.168.b0), channel_id=1, source_target_pairs={{0,32},{32,0},{1,33},{33,1},{2,34},{34,2},{3,35},{35,3},{4,36},{36... | collective-permute-start | bytes 565256 | tf_op jit(solution)/shard_map/ppermute | solution.py:550
  89.6 2.6 %collective-permute-start.13 = (bf16[736,128]{1,0:T(8,128)(2,1)S(1)}, bf16[736,128]{1,0:T(8,128)(2,1)S(1)}, u32[]{:S(2)}, u32[]{:S(2)}) collective-permute-start(bf16[736,128]{1,0:T(8,128)(2,1)S(1)} %collective-permute-done.9.b3), channel_id=1, source_target_pairs={{0,32},{32,0},{1,33},{33,1},{2,34},{34,2},{3,35},{35,3},{4,36},{36... | collective-permute-start | bytes 565256 | tf_op jit(solution)/shard_map/ppermute | solution.py:550
  92.2 2.4 %collective-permute-start.12 = (bf16[736,128]{1,0:T(8,128)(2,1)S(1)}, bf16[736,128]{1,0:T(8,128)(2,1)S(1)}, u32[]{:S(2)}, u32[]{:S(2)}) collective-permute-start(bf16[736,128]{1,0:T(8,128)(2,1)S(1)} %collective-permute-done.8.b2), channel_id=1, source_target_pairs={{0,32},{32,0},{1,33},{33,1},{2,34},{34,2},{3,35},{35,3},{4,36},{36... | collective-permute-start | bytes 565256 | tf_op jit(solution)/shard_map/ppermute | solution.py:550
  94.6 1.9 %collective-permute-start.11 = (bf16[736,128]{1,0:T(8,128)(2,1)S(1)}, bf16[736,128]{1,0:T(8,128)(2,1)S(1)}, u32[]{:S(2)}, u32[]{:S(2)}) collective-permute-start(bf16[736,128]{1,0:T(8,128)(2,1)S(1)} %collective-permute-done.7.b1), channel_id=1, source_target_pairs={{0,32},{32,0},{1,33},{33,1},{2,34},{34,2},{3,35},{35,3},{4,36},{36... | collective-permute-start | bytes 565256 | tf_op jit(solution)/shard_map/ppermute | solution.py:550
  96.5 0.1 broadcast_multiply_fusion.1
  96.6 0.9 collective-permute-done.11.b5
  97.5 3.6 %shard_map.169 = (f32[2,8,29568]{2,1,0:T(8,128)}, bf16[2,8,29568]{2,1,0:T(8,128)(2,1)}, f32[2,8,29568]{2,1,0:T(8,128)}, f32[8,8192]{1,0:T(8,128)}, bf16[8,8192]{...) custom-call(bf16[736,128]{1,0:T(8,128)(2,1)S(1)} %shard_map.168.b0, ...), custom_call_target="tpu_custom_call" | custom-call | tf_op jit(solution)/shard_map/pallas_call | solution.py:514
  (34 shorter events, 0.1 us)
Async XLA Ops:
  0.6 7.0 %copy-start.1 = (bf16[924,128]{1,0:T(8,128)(2,1)S(1)}, bf16[924,128]{1,0:T(8,128)(2,1)}, u32[]{:S(2)}) copy-start(bf16[924,128]{1,0:T(8,128)(2,1)} %gu_any.1) | copy-start | bytes 709636
  0.6 7.0 %copy-start.2 = (bf16[256,64]{0,1:T(8,128)(2,1)S(1)}, bf16[256,64]{0,1:T(8,128)(2,1)}, u32[]{:S(2)}) copy-start(bf16[256,64]{0,1:T(8,128)(2,1)} %param.19) | copy-start | bytes 98308
  4.3 5.2 %collective-permute-start = (bf16[16,144,128]{2,1,0:T(8,128)(2,1)}, bf16[16,144,128]{2,1,0:T(8,128)(2,1)S(1)}, u32[]{:S(2)}, u32[]{:S(2)}) collective-permute-start(bf16[16,144,128]{2,1,0:T(8,128)(2,1)} %get-tuple-element.31), channel_id=1, source_target_pairs={{0,32},{32,0},{1,33},{33,1},{2,34},{34,2},{3,35},{35,3},{4,36},{36... | collective-permute-start | bytes 1769480 | tf_op jit(solution)/shard_map/ppermute | solution.py:550
  9.5 1.1 %copy-start = (bf16[16,144,128]{2,1,0:T(8,128)(2,1)S(1)}, bf16[16,144,128]{2,1,0:T(8,128)(2,1)}, u32[]{:S(2)}) copy-start(bf16[16,144,128]{2,1,0:T(8,128)(2,1)} %get-tuple-element.30.own) | copy-start | bytes 1769476
  10.7 11.5 %collective-permute-start.1 = (bf16[4,144,128]{2,1,0:T(8,128)(2,1)S(1)}, bf16[4,144,128]{2,1,0:T(8,128)(2,1)S(1)}, u32[]{:S(2)}, u32[]{:S(2)}) collective-permute-start(bf16[4,144,128]{2,1,0:T(8,128)(2,1)S(1)} %get-tuple-element.33), channel_id=1, source_target_pairs={{0,64},{64,128},{128,192},{192,0},{1,65},{65,129},{129,193},{193,1... | collective-permute-start | bytes 442376 | tf_op jit(solution)/shard_map/ppermute | solution.py:546
  10.8 11.4 %collective-permute-start.2 = (bf16[4,144,128]{2,1,0:T(8,128)(2,1)S(1)}, bf16[4,144,128]{2,1,0:T(8,128)(2,1)S(1)}, u32[]{:S(2)}, u32[]{:S(2)}) collective-permute-start(bf16[4,144,128]{2,1,0:T(8,128)(2,1)S(1)} %get-tuple-element.34), channel_id=1, source_target_pairs={{0,128},{64,192},{128,0},{192,64},{1,129},{65,193},{129,1},{193,65... | collective-permute-start | bytes 442376 | tf_op jit(solution)/shard_map/ppermute | solution.py:546
  13.0 9.3 %collective-permute-start.3 = (bf16[4,144,128]{2,1,0:T(8,128)(2,1)S(1)}, bf16[4,144,128]{2,1,0:T(8,128)(2,1)S(1)}, u32[]{:S(2)}, u32[]{:S(2)}) collective-permute-start(bf16[4,144,128]{2,1,0:T(8,128)(2,1)S(1)} %get-tuple-element.35), channel_id=1, source_target_pairs={{0,192},{64,0},{128,64},{192,128},{1,193},{65,1},{129,65},{193,129... | collective-permute-start | bytes 442376 | tf_op jit(solution)/shard_map/ppermute | solution.py:546
  14.0 18.8 %all-to-all-start = ((bf16[8,144,128]{2,1,0:T(8,128)(2,1)}), bf16[8,144,128]{2,1,0:T(8,128)(2,1)S(1)}, u32[]{:S(2)}, u32[]{:S(2)}) async-start(bf16[8,144,128]{2,1,0:T(8,128)(2,1)} %shard_map.162.after), calls=%async_computation | async-start | bytes 589824 | tf_op jit(solution)/shard_map/all_to_all | solution.py:554
  22.2 63.0 %copy-start.6 = (f32[2,8,29568]{2,1,0:T(8,128)S(1)}, f32[2,8,29568]{2,1,0:T(8,128)}, u32[]{:S(2)}) copy-start(f32[2,8,29568]{2,1,0:T(8,128)} %param.13) | copy-start | bytes 5677060
  22.3 10.5 %collective-permute-start.4 = (bf16[144,128]{1,0:T(8,128)(2,1)S(1)}, bf16[144,128]{1,0:T(8,128)(2,1)S(1)}, u32[]{:S(2)}, u32[]{:S(2)}) collective-permute-start(bf16[144,128]{1,0:T(8,128)(2,1)S(1)} %get-tuple-element.37), channel_id=1, source_target_pairs={{0,1},{1,2},{2,3},{3,0},{4,5},{5,6},{6,7},{7,4},{8,9},{9,10},{10,1... | collective-permute-start | bytes 110600 | tf_op jit(solution)/shard_map/ppermute | solution.py:546
  23.6 9.2 %collective-permute-start.5 = (bf16[144,128]{1,0:T(8,128)(2,1)S(1)}, bf16[144,128]{1,0:T(8,128)(2,1)S(1)}, u32[]{:S(2)}, u32[]{:S(2)}) collective-permute-start(bf16[144,128]{1,0:T(8,128)(2,1)S(1)} %get-tuple-element.38), channel_id=1, source_target_pairs={{0,2},{1,3},{2,0},{3,1},{4,6},{5,7},{6,4},{7,5},{8,10},{9,11},{10,... | collective-permute-start | bytes 110600 | tf_op jit(solution)/shard_map/ppermute | solution.py:546
  26.1 6.8 %collective-permute-start.6 = (bf16[144,128]{1,0:T(8,128)(2,1)S(1)}, bf16[144,128]{1,0:T(8,128)(2,1)S(1)}, u32[]{:S(2)}, u32[]{:S(2)}) collective-permute-start(bf16[144,128]{1,0:T(8,128)(2,1)S(1)} %get-tuple-element.39), channel_id=1, source_target_pairs={{0,3},{1,0},{2,1},{3,2},{4,7},{5,4},{6,5},{7,6},{8,11},{9,8},{10,9... | collective-permute-start | bytes 110600 | tf_op jit(solution)/shard_map/ppermute | solution.py:546
  32.9 52.4 %copy-start.3 = (f32[2,8,29568]{2,1,0:T(8,128)S(1)}, f32[2,8,29568]{2,1,0:T(8,128)}, u32[]{:S(2)}) copy-start(f32[2,8,29568]{2,1,0:T(8,128)} %gs.1) | copy-start | bytes 5677060
  32.9 52.4 %copy-start.4 = (bf16[1,2,8,29568]{3,2,1,0:T(8,128)(2,1)S(1)}, bf16[1,2,8,29568]{3,2,1,0:T(8,128)(2,1)}, u32[]{:S(2)}) copy-start(bf16[1,2,8,29568]{3,2,1,0:T(8,128)(2,1)} %param.11) | copy-start | bytes 2838532
  32.9 52.4 %copy-start.5 = (bf16[1,2,8,29568]{3,2,1,0:T(8,128)(2,1)S(1)}, bf16[1,2,8,29568]{3,2,1,0:T(8,128)(2,1)}, u32[]{:S(2)}) copy-start(bf16[1,2,8,29568]{3,2,1,0:T(8,128)(2,1)} %param.12) | copy-start | bytes 2838532
  82.9 13.6 %copy-start.7 = (f32[8,8192]{1,0:T(8,128)S(1)}, f32[8,8192]{1,0:T(8,128)}, u32[]{:S(2)}) copy-start(f32[8,8192]{1,0:T(8,128)} %ds.1) | copy-start | bytes 786436
  82.9 13.6 %copy-start.8 = (bf16[1,8,8192]{2,1,0:T(8,128)(2,1)S(1)}, bf16[1,8,8192]{2,1,0:T(8,128)(2,1)}, u32[]{:S(2)}) copy-start(bf16[1,8,8192]{2,1,0:T(8,128)(2,1)} %param.16) | copy-start | bytes 393220
  82.9 13.6 %copy-start.9 = (bf16[1,8,8192]{2,1,0:T(8,128)(2,1)S(1)}, bf16[1,8,8192]{2,1,0:T(8,128)(2,1)}, u32[]{:S(2)}) copy-start(bf16[1,8,8192]{2,1,0:T(8,128)(2,1)} %param.17) | copy-start | bytes 393220
  82.9 13.6 %copy-start.10 = (f32[8,8192]{1,0:T(8,128)S(1)}, f32[8,8192]{1,0:T(8,128)}, u32[]{:S(2)}) copy-start(f32[8,8192]{1,0:T(8,128)} %param.18) | copy-start | bytes 786436
  82.9 6.7 %collective-permute-start.9 = (bf16[736,128]{1,0:T(8,128)(2,1)S(1)}, bf16[736,128]{1,0:T(8,128)(2,1)S(1)}, u32[]{:S(2)}, u32[]{:S(2)}) collective-permute-start(bf16[736,128]{1,0:T(8,128)(2,1)S(1)} %shard_map.168.b0), channel_id=1, source_target_pairs={{0,192},{64,0},{128,64},{192,128},{1,193},{65,1},{129,65},{193,129... | collective-permute-start | bytes 565256 | tf_op jit(solution)/shard_map/ppermute | solution.py:546
  83.8 8.4 %collective-permute-start.8 = (bf16[736,128]{1,0:T(8,128)(2,1)S(1)}, bf16[736,128]{1,0:T(8,128)(2,1)S(1)}, u32[]{:S(2)}, u32[]{:S(2)}) collective-permute-start(bf16[736,128]{1,0:T(8,128)(2,1)S(1)} %shard_map.168.b0), channel_id=1, source_target_pairs={{0,128},{64,192},{128,0},{192,64},{1,129},{65,193},{129,1},{193,65... | collective-permute-start | bytes 565256 | tf_op jit(solution)/shard_map/ppermute | solution.py:546
  85.1 9.4 %collective-permute-start.7 = (bf16[736,128]{1,0:T(8,128)(2,1)S(1)}, bf16[736,128]{1,0:T(8,128)(2,1)S(1)}, u32[]{:S(2)}, u32[]{:S(2)}) collective-permute-start(bf16[736,128]{1,0:T(8,128)(2,1)S(1)} %shard_map.168.b0), channel_id=1, source_target_pairs={{0,64},{64,128},{128,192},{192,0},{1,65},{65,129},{129,193},{193,1... | collective-permute-start | bytes 565256 | tf_op jit(solution)/shard_map/ppermute | solution.py:546
  85.8 10.7 %collective-permute-start.10 = (bf16[736,128]{1,0:T(8,128)(2,1)S(1)}, bf16[736,128]{1,0:T(8,128)(2,1)S(1)}, u32[]{:S(2)}, u32[]{:S(2)}) collective-permute-start(bf16[736,128]{1,0:T(8,128)(2,1)S(1)} %shard_map.168.b0), channel_id=1, source_target_pairs={{0,32},{32,0},{1,33},{33,1},{2,34},{34,2},{3,35},{35,3},{4,36},{36... | collective-permute-start | bytes 565256 | tf_op jit(solution)/shard_map/ppermute | solution.py:550
  89.6 7.0 %collective-permute-start.13 = (bf16[736,128]{1,0:T(8,128)(2,1)S(1)}, bf16[736,128]{1,0:T(8,128)(2,1)S(1)}, u32[]{:S(2)}, u32[]{:S(2)}) collective-permute-start(bf16[736,128]{1,0:T(8,128)(2,1)S(1)} %collective-permute-done.9.b3), channel_id=1, source_target_pairs={{0,32},{32,0},{1,33},{33,1},{2,34},{34,2},{3,35},{35,3},{4,36},{36... | collective-permute-start | bytes 565256 | tf_op jit(solution)/shard_map/ppermute | solution.py:550
  92.2 4.4 %collective-permute-start.12 = (bf16[736,128]{1,0:T(8,128)(2,1)S(1)}, bf16[736,128]{1,0:T(8,128)(2,1)S(1)}, u32[]{:S(2)}, u32[]{:S(2)}) collective-permute-start(bf16[736,128]{1,0:T(8,128)(2,1)S(1)} %collective-permute-done.8.b2), channel_id=1, source_target_pairs={{0,32},{32,0},{1,33},{33,1},{2,34},{34,2},{3,35},{35,3},{4,36},{36... | collective-permute-start | bytes 565256 | tf_op jit(solution)/shard_map/ppermute | solution.py:550
  94.6 3.0 %collective-permute-start.11 = (bf16[736,128]{1,0:T(8,128)(2,1)S(1)}, bf16[736,128]{1,0:T(8,128)(2,1)S(1)}, u32[]{:S(2)}, u32[]{:S(2)}) collective-permute-start(bf16[736,128]{1,0:T(8,128)(2,1)S(1)} %collective-permute-done.7.b1), channel_id=1, source_target_pairs={{0,32},{32,0},{1,33},{33,1},{2,34},{34,2},{3,35},{35,3},{4,36},{36... | collective-permute-start | bytes 565256 | tf_op jit(solution)/shard_map/ppermute | solution.py:550
